TPU v7x, 32 devices: a whole 2x2x4 slice. The times are simulated.
32 devices in a mesh: groups: 2 (over x), width: 16 (over z, y, core).
Axes of the slice: x: 2, y: 2, z: 4, core: 2. Of those that a mesh axis runs over, the one named last changes fastest.
Arguments:
- stream_in: bfloat16 [2, 128, 8192], P(None, 'groups', 'width'), parts along dimension 1, may hold values from -16 to 16
- norm_gain: float32 [2, 8192], replicated, may hold values from 0.1 to 1.9
- w_gate: bfloat16 [2, 8192, 14336], P(None, None, 'width'), may hold values from -0.0625 to 0.0625
- w_up: bfloat16 [2, 8192, 14336], P(None, None, 'width'), may hold values from -0.0625 to 0.0625
- w_down: bfloat16 [2, 14336, 8192], P(None, 'width'), may hold values from -0.0625 to 0.0625
Outputs:
- stream_out: bfloat16 [2, 128, 8192], P(None, 'groups', 'width'), parts along dimension 1
There are 2 independent parts, one for each index of `groups`. A program takes and returns all parts, laid end to end along the dimension named above; an argument that names none is the same for every part. Nothing has to cross between parts.
All inputs are finite; a program needn't handle non-finite values.
Results may differ from a plain program's by a relative error of at most 0.012.
Values may be sent and summed in bfloat16 or wider, within the bound.
No kernel may reach another device: no remote copies, remote signals or barrier semaphores. Data moves between devices by JAX's collectives and lax.ppermute only.
A program may use at most 192 MiB of HBM per device.

v0:
```python
import jax
import jax.numpy as jnp
from jax import lax
from jax.sharding import PartitionSpec as P

LAYERS = 2
MICRO = 2


def body(stream_in, norm_gain, w_gate, w_up, w_down):
    width_local = stream_in.shape[2]
    offset = lax.axis_index("width") * width_local
    starts = [
        lax.all_gather(stream_in[micro_index], "width", axis=1, tiled=True)
        for micro_index in range(MICRO)
    ]
    results = []
    for micro_index in range(MICRO):
        stream = starts[micro_index]
        for depth in range(LAYERS):
            stream_f = stream.astype(jnp.float32)
            meansq = jnp.mean(stream_f * stream_f, axis=1, keepdims=True)
            normed = (stream_f * lax.rsqrt(meansq + 1e-05) * norm_gain[depth]).astype(jnp.bfloat16)
            gate_out = jnp.dot(normed, w_gate[depth], preferred_element_type=jnp.float32)
            up_out = jnp.dot(normed, w_up[depth], preferred_element_type=jnp.float32)
            hidden = (jax.nn.silu(gate_out) * up_out).astype(jnp.bfloat16)
            partials = jnp.dot(hidden, w_down[depth], preferred_element_type=jnp.float32)
            branch = lax.psum(partials, "width")
            stream = (stream_f + branch).astype(jnp.bfloat16)
        results.append(stream)
    results = [lax.dynamic_slice_in_dim(stream, offset, width_local, 1) for stream in results]
    return jnp.stack(results)


def solution(mesh):
    return jax.shard_map(
        body,
        mesh=mesh,
        in_specs=(
            P(None, "groups", "width"),
            P(),
            P(None, None, "width"),
            P(None, None, "width"),
            P(None, "width", None),
        ),
        out_specs=P(None, "groups", "width"),
        check_vma=False,
    )
```

profile of v0, /device:TPU:0, one launch (start us, length us, event | category | flops | bytes accessed | tf_op | source)
XLA Modules:
  0.0 416.5 jit_solution(16510495588360910265)
XLA Ops:
  6.5 1.5 fusion.118
  8.1 0.0 all-gather.7.cloned.1.call-start
  8.1 0.7 all-gather.7.cloned.1.call-update
  8.9 1.0 fusion.119
  9.9 39.2 %all-gather.5.cloned.1.call-done = bf16[1,64,8192]{2,1,0:T(8,128)(2,1)} async-done(((bf16[1,64,512]{2,1,0:T(8,128)(2,1)}), bf16[1,64,8192]{2,1,0:T(8,128)(2,1)}) %all-gather.5.cloned.1.call-update) | async-done | bytes 1048592 | tf_op jit(solution)/shard_map/all_gather | solution.py:14
  49.1 1.6 fusion.36
  50.7 36.9 %all-gather.7.cloned.1.call-done = bf16[1,64,8192]{2,1,0:T(8,128)(2,1)} async-done(((bf16[1,64,512]{2,1,0:T(8,128)(2,1)}), bf16[1,64,8192]{2,1,0:T(8,128)(2,1)}) %all-gather.7.cloned.1.call-update) | async-done | bytes 1048592 | tf_op jit(solution)/shard_map/all_gather | solution.py:14
  87.5 1.5 fusion.40
  89.1 6.7 %fusion.22 = f32[64,896]{1,0:T(8,128)S(1)} fusion(bf16[2,8192,896]{2,1,0:T(8,128)(2,1)} %param.7, bf16[1,64,8192]{2,1,0:T(8,128)(2,1)S(1)} %copy-done, f32[8192]{0:T(1024)S(1)} %bitcast.82, f32[64]{0:T(128)S(1)} %add_rsqrt_fusion.3), kind=kOutput, calls=%fused_computation.22 | convolution fusion | flops 941621248 | bytes 15991040 | tf_op jit(solution)/shard_map/dot_general | solution.py:24
  95.8 6.6 %fusion.20 = f32[64,896]{1,0:T(8,128)S(1)} fusion(bf16[2,8192,896]{2,1,0:T(8,128)(2,1)} %param.7, bf16[1,64,8192]{2,1,0:T(8,128)(2,1)S(1)} %copy-done.1, f32[64]{0:T(128)S(1)} %add_rsqrt_fusion.1, f32[8192]{0:T(1024)S(1)} %bitcast.83), kind=kOutput, calls=%fused_computation.20 | convolution fusion | flops 941621248 | bytes 15991040 | tf_op jit(solution)/shard_map/dot_general | solution.py:24
  102.4 16.4 %fusion.14 = f32[64,8192]{1,0:T(8,128)} fusion(bf16[2,896,8192]{2,1,0:T(8,128)(2,1)} %param.9, bf16[2,8192,896]{2,1,0:T(8,128)(2,1)} %param.8, bf16[1,64,8192]{2,1,0:T(8,128)(2,1)S(1)} %copy-done, f32[8192]{0:T(1024)S(1)} %bitcast.84, f32[64]{0:T(128)S(1)} %add_rsqrt_fusion.3, f32[64,896]{1,0:T(8,128)S(1)} %fusion.22), kind=kOutput, calls=%fused_computation.14 | convolution fusion | flops 1881489408 | bytes 32768256 | tf_op jit(solution)/shard_map/dot_general | solution.py:27
  118.8 16.3 %fusion.12 = f32[64,8192]{1,0:T(8,128)} fusion(bf16[2,896,8192]{2,1,0:T(8,128)(2,1)} %param.9, bf16[2,8192,896]{2,1,0:T(8,128)(2,1)} %param.8, bf16[1,64,8192]{2,1,0:T(8,128)(2,1)S(1)} %copy-done.1, f32[64]{0:T(128)S(1)} %add_rsqrt_fusion.1, f32[8192]{0:T(1024)S(1)} %bitcast.85, f32[64,896]{1,0:T(8,128)S(1)} %fusion.20), kind=kOutput, calls=%fused_computation.12 | convolution fusion | flops 1881489408 | bytes 32768256 | tf_op jit(solution)/shard_map/dot_general | solution.py:27
  135.1 0.2 all-reduce.5.cloned.1.call-start
  135.4 111.2 %all-reduce.7.cloned.1.call-done = (f32[64,8192]{1,0:T(8,128)}, f32[64,8192]{1,0:T(8,128)}) async-done(((f32[64,8192]{1,0:T(8,128)}, f32[64,8192]{1,0:T(8,128)}), (f32[64,8192]{1,0:T(8,128)}, f32[64,8192]{1,0:T(8,128)})) %all-reduce.7.cloned.1.call-update) | async-done | bytes 4194320 | tf_op jit(solution)/shard_map/psum | solution.py:28
  246.6 4.2 %multiply_reduce_fusion = (f32[64]{0:T(128)S(1)}, f32[64,8192]{1,0:T(8,128)}, f32[64]{0:T(128)S(1)}, f32[64,8192]{1,0:T(8,128)S(1)}) fusion(f32[64,8192]{1,0:T(8,128)} %get-tuple-element.7, bf16[1,64,8192]{2,1,0:T(8,128)(2,1)S(1)} %copy-done.1, f32[64,8192]{1,0:T(8,128)} %get-tuple-element.8, bf16[1,64,8192]{2,1,0:T(8,128)(2,1)S(1)} %copy-done), kind=kLoop, calls=%fused_computation.51 | loop fusion | flops 6291328 | bytes 10486272 | tf_op jit(solution)/shard_map/reduce_sum | solution.py:22
  250.8 1.3 copy-done.3
  252.1 6.6 %fusion.10 = f32[64,896]{1,0:T(8,128)S(1)} fusion(bf16[2,8192,896]{2,1,0:T(8,128)(2,1)} %param.7, f32[64,8192]{1,0:T(8,128)S(1)} %get-tuple-element.18, f32[8192]{0:T(1024)S(1)} %bitcast.78, f32[64]{0:T(128)S(1)} %add_rsqrt_fusion.2), kind=kOutput, calls=%fused_computation.10 | convolution fusion | flops 941096960 | bytes 17039616 | tf_op jit(solution)/shard_map/dot_general | solution.py:24
  258.7 14.6 %fusion.2 = f32[64,8192]{1,0:T(8,128)} fusion(bf16[2,896,8192]{2,1,0:T(8,128)(2,1)} %param.9, bf16[2,8192,896]{2,1,0:T(8,128)(2,1)} %param.8, f32[64,896]{1,0:T(8,128)S(1)} %fusion.10, f32[64,8192]{1,0:T(8,128)} %copy-done.3, f32[8192]{0:T(1024)S(1)} %bitcast.79, f32[64]{0:T(128)S(1)} %add_rsqrt_fusion.2), kind=kOutput, calls=%fused_computation.2 | convolution fusion | flops 1880965120 | bytes 33816832 | tf_op jit(solution)/shard_map/dot_general | solution.py:27
  273.4 6.6 %fusion.8 = f32[64,896]{1,0:T(8,128)S(1)} fusion(bf16[2,8192,896]{2,1,0:T(8,128)(2,1)} %param.7, f32[64,8192]{1,0:T(8,128)S(1)} %copy-done.2, f32[64]{0:T(128)S(1)} %add_rsqrt_fusion, f32[8192]{0:T(1024)S(1)} %bitcast.80), kind=kOutput, calls=%fused_computation.8 | convolution fusion | flops 941096960 | bytes 17039616 | tf_op jit(solution)/shard_map/dot_general | solution.py:24
  280.0 16.4 %fusion = f32[64,8192]{1,0:T(8,128)} fusion(bf16[2,896,8192]{2,1,0:T(8,128)(2,1)} %param.9, bf16[2,8192,896]{2,1,0:T(8,128)(2,1)} %param.8, f32[64,896]{1,0:T(8,128)S(1)} %fusion.8, f32[64,8192]{1,0:T(8,128)S(1)} %copy-done.2, f32[64]{0:T(128)S(1)} %add_rsqrt_fusion, f32[8192]{0:T(1024)S(1)} %bitcast.81), kind=kOutput, calls=%fused_computation | convolution fusion | flops 1880965120 | bytes 33816832 | tf_op jit(solution)/shard_map/dot_general | solution.py:27
  296.4 111.0 %all-reduce.5.cloned.1.call-done = (f32[64,8192]{1,0:T(8,128)}, f32[64,8192]{1,0:T(8,128)}) async-done(((f32[64,8192]{1,0:T(8,128)}, f32[64,8192]{1,0:T(8,128)}), (f32[64,8192]{1,0:T(8,128)}, f32[64,8192]{1,0:T(8,128)})) %all-reduce.5.cloned.1.call-update) | async-done | bytes 4194320 | tf_op jit(solution)/shard_map/psum | solution.py:28
  407.4 1.0 fusion.110
  408.4 0.9 fusion.111
  409.3 0.7 pad_maximum_fusion
  (16 shorter events, 0.1 us)
Async XLA Ops:
  6.5 42.5 %all-gather.5.cloned.1.call-start = ((), (), s32[]{:S(2)}) async-start(), calls=%async_computation | async-start | bytes 1114112 | tf_op jit(solution)/shard_map/all_gather | solution.py:14
  8.1 79.5 %all-gather.7.cloned.1.call-start = ((), (), s32[]{:S(2)}) async-start(), calls=%async_computation.1 | async-start | bytes 1114112 | tf_op jit(solution)/shard_map/all_gather | solution.py:14
  8.8 237.7 %all-reduce.7.cloned.1.call-start = ((), (), s32[]{:S(2)}) async-start(), calls=%async_computation.3 | async-start | bytes 8388608 | tf_op jit(solution)/shard_map/psum | solution.py:28
  49.1 40.0 %copy-start = (bf16[1,64,8192]{2,1,0:T(8,128)(2,1)S(1)}, bf16[1,64,8192]{2,1,0:T(8,128)(2,1)}, u32[]{:S(2)}) copy-start(bf16[1,64,8192]{2,1,0:T(8,128)(2,1)} %all-gather.5.cloned.1.call-done) | copy-start | bytes 3145732
  89.1 6.7 %copy-start.1 = (bf16[1,64,8192]{2,1,0:T(8,128)(2,1)S(1)}, bf16[1,64,8192]{2,1,0:T(8,128)(2,1)}, u32[]{:S(2)}) copy-start(bf16[1,64,8192]{2,1,0:T(8,128)(2,1)} %all-gather.7.cloned.1.call-done) | copy-start | bytes 3145732
  135.1 272.3 %all-reduce.5.cloned.1.call-start = ((), (), s32[]{:S(2)}) async-start(), calls=%async_computation.2 | async-start | bytes 8388608 | tf_op jit(solution)/shard_map/psum | solution.py:28
  250.7 1.4 copy-start.3
  258.7 14.6 %copy-start.2 = (f32[64,8192]{1,0:T(8,128)S(1)}, f32[64,8192]{1,0:T(8,128)}, u32[]{:S(2)}) copy-start(f32[64,8192]{1,0:T(8,128)} %get-tuple-element.12) | copy-start | bytes 6291460
Sparse Core Ops, SparseCore 0:
  9.5 39.4 all-gather.4
  51.2 36.2 all-gather.6
  135.3 111.2 all-reduce.6
  296.5 110.8 all-reduce.4
where the time goes:
time: 417 us
  waiting for transfers between devices  299 us (72%)
  matrix products  90.2 us (22%)
  between operations  13.2 us (3%)
  other arithmetic  9.94 us (2%)
    psum x2, waiting for transfers between devices, body(): branch = lax.psum(partials, 'width')  222 us
    all_gather x2, waiting for transfers between devices, body(): lax.all_gather(stream_in[micro_index], 'width', axis=1, tiled=True)  76.1 us
    dot_general x4, matrix products, body(): jnp.dot(hidden, w_down[depth], preferred_element_type=jnp.float32)  63.7 us
    dot_general x4, matrix products, body(): jnp.dot(normed, w_gate[depth], preferred_element_type=jnp.float32)  26.5 us
  transfers between devices with their start and end apart: 4, of which 4 were waited for; matrix products, arithmetic and copies ran while one was open for 1% of the time, Pallas kernels for 0%

commit v1 on v0

v1 whole, which is shorter than its diff:
```python
import functools

import jax
import jax.numpy as jnp
from jax import lax
from jax.experimental import pallas as pl
from jax.experimental.pallas import tpu as pltpu
from jax.sharding import PartitionSpec as P

AXIS = "width"
EPS = 1e-05
VMEM = pl.BlockSpec(memory_space=pltpu.VMEM)
HBM = pl.BlockSpec(memory_space=pl.ANY)
LIMIT = 40 * 1024 * 1024


def place_of(chip, chips):
    half = chip // 2
    odd = chip - 2 * half
    return half + odd * (chips - 1 - 2 * half)


def chip_at(place, chips):
    far = (place >= chips // 2) * 1
    return 2 * place + far * (2 * chips - 1 - 4 * place)


def shard_at(offset, sibling, chips):
    me = lax.axis_index(AXIS)
    chip = me // 2
    core = me - 2 * chip
    place = lax.rem(place_of(chip, chips) + (offset + chips), chips)
    far = jnp.where(place >= chips // 2, 1, 0)
    there = 2 * place + far * (2 * chips - 1 - 4 * place)
    return 2 * there + (1 - core if sibling else core)


def gate_up_kernel(layer, chips, plan, first, last, *refs):
    refs = list(refs)
    gain_ref, wg_hbm, wu_hbm = refs[:3]
    at = 3
    xs = []
    for _, _, pieces in plan:
        xs.append(refs[at : at + pieces])
        at += pieces
    if not first:
        g_in, u_in, q_in = refs[at : at + 3]
        at += 3
    if last:
        hid_ref = refs[at]
        at += 1
        g_ref, u_ref, q_ref, wg, wu, sems = refs[at:]
    else:
        g_ref, u_ref, q_ref, wg, wu, sems = refs[at:]
    depth = wg.shape[1]
    ids = [shard_at(offset, sibling, chips) for offset, sibling, _ in plan]
    copies = []
    for e, shard in enumerate(ids):
        rows = pl.ds(pl.multiple_of(shard * depth, depth), depth)
        pair = (
            pltpu.make_async_copy(wg_hbm.at[layer, rows, :], wg.at[e], sems.at[e, 0]),
            pltpu.make_async_copy(wu_hbm.at[layer, rows, :], wu.at[e], sems.at[e, 1]),
        )
        for copy in pair:
            copy.start()
        copies.append(pair)
    for e, shard in enumerate(ids):
        parts = [ref[...] for ref in xs[e]]
        x = (parts[0] if len(parts) == 1 else jnp.concatenate(parts, 0)).astype(jnp.float32)
        square = x * x
        q = square[:, :128]
        for lane in range(128, depth, 128):
            q = q + square[:, lane : lane + 128]
        y = (x * gain_ref[layer, shard]).astype(jnp.bfloat16)
        copies[e][0].wait()
        g = jnp.dot(y, wg[e], preferred_element_type=jnp.float32)
        copies[e][1].wait()
        u = jnp.dot(y, wu[e], preferred_element_type=jnp.float32)
        if e == 0 and first:
            g_ref[...], u_ref[...], q_ref[...] = g, u, q
        elif e == 0:
            g_ref[...], u_ref[...], q_ref[...] = g_in[...] + g, u_in[...] + u, q_in[...] + q
        else:
            g_ref[...] += g
            u_ref[...] += u
            q_ref[...] += q
    if last:
        features = depth * 2 * chips
        meansq = jnp.sum(q_ref[...], axis=1, keepdims=True) / features
        scale = lax.rsqrt(meansq + EPS)
        g = g_ref[...] * scale
        hid_ref[...] = (g / (1.0 + jnp.exp(-g)) * (u_ref[...] * scale)).astype(jnp.bfloat16)


def gate_up(layer, chips, plan, xs, gain, wg, wu, acc, last):
    depth = xs[0].shape[-1]
    hid = wg.shape[2]
    rows = 128 if not isinstance(xs[0], tuple) else 0
    rows = max(x.shape[0] for x in xs)
    if all(p[2] == 2 for p in plan):
        rows = 2 * xs[0].shape[0]
    k = len(plan)
    f32 = jnp.float32
    sums = [
        jax.ShapeDtypeStruct((rows, hid), f32),
        jax.ShapeDtypeStruct((rows, hid), f32),
        jax.ShapeDtypeStruct((rows, 128), f32),
    ]
    scratch = [
        pltpu.VMEM((k, depth, hid), jnp.bfloat16),
        pltpu.VMEM((k, depth, hid), jnp.bfloat16),
        pltpu.SemaphoreType.DMA((k, 2)),
    ]
    n_in = 3 + len(xs) + (3 if acc else 0)
    if last:
        out_shape = jax.ShapeDtypeStruct((rows, hid), jnp.bfloat16)
        out_specs = VMEM
        scratch = [pltpu.VMEM(s.shape, s.dtype) for s in sums] + scratch
        aliases = {}
    else:
        out_shape = sums
        out_specs = [VMEM] * 3
        aliases = {3 + len(xs) + i: i for i in range(3)} if acc else {}
    return pl.pallas_call(
        functools.partial(gate_up_kernel, layer, chips, plan, not acc, last),
        out_shape=out_shape,
        in_specs=[VMEM, HBM, HBM] + [VMEM] * (n_in - 3),
        out_specs=out_specs,
        scratch_shapes=scratch,
        input_output_aliases=aliases,
        compiler_params=pltpu.CompilerParams(vmem_limit_bytes=LIMIT),
        cost_estimate=pl.CostEstimate(
            flops=4 * k * rows * depth * hid, bytes_accessed=4 * k * depth * hid, transcendentals=0
        ),
        name="gate_up",
    )(gain, wg, wu, *xs, *(acc or ()))


def down_kernel(layer, chips, offsets, hid_ref, w_hbm, *refs):
    k = len(offsets)
    own, sib = refs[:k], refs[k : 2 * k]
    w, sems = refs[2 * k :]
    cols = w.shape[3]
    copies = []
    for e, offset in enumerate(offsets):
        pair = []
        for side in (1, 0):
            start = pl.multiple_of(shard_at(offset, side == 1, chips) * cols, cols)
            pair.append(
                pltpu.make_async_copy(w_hbm.at[layer, :, pl.ds(start, cols)], w.at[e, side], sems.at[e, side])
            )
            pair[-1].start()
        copies.append(pair)
    for e in range(k):
        copies[e][0].wait()
        sib[e][...] = jnp.dot(hid_ref[...], w[e, 1], preferred_element_type=jnp.float32).astype(jnp.bfloat16)
        copies[e][1].wait()
        own[e][...] = jnp.dot(hid_ref[...], w[e, 0], preferred_element_type=jnp.float32)


def down(layer, chips, offsets, hidden, wd, cols):
    k = len(offsets)
    rows, hid = hidden.shape
    outs = pl.pallas_call(
        functools.partial(down_kernel, layer, chips, offsets),
        out_shape=[jax.ShapeDtypeStruct((rows, cols), jnp.float32)] * k
        + [jax.ShapeDtypeStruct((rows, cols), jnp.bfloat16)] * k,
        in_specs=[VMEM, HBM],
        out_specs=[VMEM] * (2 * k),
        scratch_shapes=[pltpu.VMEM((k, 2, hid, cols), jnp.bfloat16), pltpu.SemaphoreType.DMA((k, 2))],
        compiler_params=pltpu.CompilerParams(vmem_limit_bytes=LIMIT),
        cost_estimate=pl.CostEstimate(
            flops=4 * k * rows * cols * hid, bytes_accessed=4 * k * cols * hid, transcendentals=0
        ),
        name="down",
    )(hidden, wd)
    return outs[:k], outs[k:]


def ring_body(chips, stream_in, norm_gain, w_gate, w_up, w_down):
    micro, seqs, cols = stream_in.shape
    rows = micro * seqs
    part = rows // 2
    layers = w_gate.shape[0]
    far = chips // 2
    ring = [chip_at(place, chips) for place in range(chips)]
    right = [(2 * ring[i] + c, 2 * ring[(i + 1) % chips] + c) for i in range(chips) for c in range(2)]
    left = [(b, a) for a, b in right]
    core = [(i, i ^ 1) for i in range(2 * chips)]

    def send(x, perm):
        return lax.ppermute(x, AXIS, perm)

    f32, bf16 = jnp.float32, jnp.bfloat16
    gain = norm_gain.reshape(layers, 2 * chips, 1, cols)
    stream = stream_in.reshape(rows, cols)
    for layer in range(layers):
        args = (gain, w_gate, w_up)
        r = l = stream
        acc = None
        ready = [(0, False, 1, (stream,))]
        crossing = [(0, send(stream, core))]
        for step in range(1, far):
            r, l = send(r, right), send(l, left)
            acc = gate_up(layer, chips, [e[:3] for e in ready], [x for e in ready for x in e[3]], *args, acc, False)
            ready = [(o, True, 1, (x,)) for o, x in crossing] + [(-step, False, 1, (r,)), (step, False, 1, (l,))]
            crossing = [(-step, send(r, core)), (step, send(l, core))]
        r, l = send(r[:part], right), send(l[part:], left)
        acc = gate_up(layer, chips, [e[:3] for e in ready], [x for e in ready for x in e[3]], *args, acc, False)
        ready = [(o, True, 1, (x,)) for o, x in crossing] + [(far, False, 2, (r, l))]
        rc, lc = send(r, core), send(l, core)
        acc = gate_up(layer, chips, [e[:3] for e in ready], [x for e in ready for x in e[3]], *args, acc, False)
        hidden = gate_up(layer, chips, [(far, True, 2)], [rc, lc], *args, acc, True)
        (own,), (sib,) = down(layer, chips, [far], hidden, w_down, cols)
        total = own + send(sib, core).astype(f32)
        total = total.astype(bf16)
        r, l = send(total[:part], right), send(total[part:], left)
        for step in range(far - 1, 0, -1):
            own, sib = down(layer, chips, [step, -step], hidden, w_down, cols)
            cross = [send(s, core).astype(f32) for s in sib]
            sums = [own[0] + cross[0], own[1] + cross[1]]
            if step == far - 1:
                hole = jnp.zeros((part, cols), bf16)
                r = jnp.concatenate([r, hole], 0)
                l = jnp.concatenate([hole, l], 0)
            r = send((sums[0] + r.astype(f32)).astype(bf16), right)
            l = send((sums[1] + l.astype(f32)).astype(bf16), left)
        (own,), (sib,) = down(layer, chips, [0], hidden, w_down, cols)
        branch = own + send(sib, core).astype(f32)
        stream = (stream.astype(f32) + branch + r.astype(f32) + l.astype(f32)).astype(bf16)
    return stream.reshape(micro, seqs, cols)


def plain_body(stream_in, norm_gain, w_gate, w_up, w_down):
    micro, seqs, cols = stream_in.shape
    layers = w_gate.shape[0]
    f32, bf16 = jnp.float32, jnp.bfloat16
    stream = stream_in.reshape(micro * seqs, cols)
    for layer in range(layers):
        whole = lax.all_gather(stream, AXIS, axis=1, tiled=True).astype(f32)
        meansq = jnp.mean(whole * whole, axis=1, keepdims=True)
        normed = (whole * lax.rsqrt(meansq + EPS) * norm_gain[layer]).astype(bf16)
        gate_out = jnp.dot(normed, w_gate[layer], preferred_element_type=f32)
        up_out = jnp.dot(normed, w_up[layer], preferred_element_type=f32)
        hidden = (jax.nn.silu(gate_out) * up_out).astype(bf16)
        partials = jnp.dot(hidden, w_down[layer], preferred_element_type=f32)
        branch = lax.psum_scatter(partials, AXIS, scatter_dimension=1, tiled=True)
        stream = (stream.astype(f32) + branch).astype(bf16)
    return stream.reshape(micro, seqs, cols)


def solution(mesh):
    devices = mesh.shape[AXIS]

    def body(stream_in, *rest):
        cols = stream_in.shape[2]
        if devices % 8 == 0 and cols % 128 == 0:
            return ring_body(devices // 2, stream_in, *rest)
        return plain_body(stream_in, *rest)

    return jax.shard_map(
        body,
        mesh=mesh,
        in_specs=(
            P(None, "groups", AXIS),
            P(),
            P(None, None, AXIS),
            P(None, None, AXIS),
            P(None, AXIS, None),
        ),
        out_specs=P(None, "groups", AXIS),
        check_vma=False,
    )
```

time: 417 us -> 155 us (0.37)
  waiting for transfers between devices: 299 us -> 49.6 us
  matrix products: 90.2 us -> 0 us
  Pallas kernels: 0 us -> 58.3 us
  starting transfers between devices: 0.3 us -> 42.7 us
  between operations: 13.2 us -> 0.51 us
  other arithmetic: 9.94 us -> 1.38 us
    psum x2 -> x0, waiting for transfers between devices: 222 us -> none  [body(): branch = lax.psum(partials, 'width')]
    dot_general x8 -> x0, matrix products: 90.2 us -> none  [the longest x4 63.7 us: body(): jnp.dot(hidden, w_down[depth], preferred_element_type=jnp.float32)]
    all_gather x2 -> x0, waiting for transfers between devices: 76.1 us -> none  [body(): lax.all_gather(stream_in[micro_index], 'width', axis=1, tiled=True)]
    pallas_call x0 -> x22, Pallas kernels: none -> 58.3 us  [the longest x12 36.2 us: gate_up(): pl.pallas_call(functools.partial(gate_up_kernel, layer, chips, plan, not...]
    ppermute x0 -> x66, waiting for transfers between devices: none -> 49.6 us  [send(): return lax.ppermute(x, AXIS, perm)]
    ppermute x0 -> x66, starting transfers between devices: none -> 42.7 us  [send(): return lax.ppermute(x, AXIS, perm)]
    reduce_sum x3 -> x0, other arithmetic: 7.33 us -> none  [body(): meansq = jnp.mean(stream_f * stream_f, axis=1, keepdims=True)]
  transfers between devices with their start and end apart: 4 -> 66, of which waited for: 4 -> 17; matrix products, arithmetic and copies ran while one was open for 1% -> 1% of each run, Pallas kernels for 0% -> 33%
where the time goes in v1:
time: 155 us; the launch traced here: 154 us
  Pallas kernels  58.3 us (38%)
  waiting for transfers between devices  49.6 us (32%)
  starting transfers between devices  42.7 us (28%)
  local copies, waits for them, and re-layouts  1.89 us (1%)
    ppermute x66, waiting for transfers between devices, send(): return lax.ppermute(x, AXIS, perm)  49.6 us
    ppermute x66, starting transfers between devices, send(): return lax.ppermute(x, AXIS, perm)  42.7 us
    pallas_call x12, Pallas kernels, gate_up(): pl.pallas_call(functools.partial(gate_up_kernel, layer, chips, plan, not...  36.2 us
    pallas_call x10, Pallas kernels, down(): pl.pallas_call(functools.partial(down_kernel, layer, chips, offsets), out...  22.1 us
  transfers between devices with their start and end apart: 66, of which 17 were waited for; matrix products, arithmetic and copies ran while one was open for 1% of the time, Pallas kernels for 33%

profile of v1, /device:TPU:0, one launch (start us, length us, event | category | flops | bytes accessed | tf_op | source)
XLA Modules:
  0.0 154.3 jit_solution(17925232299300964579)
XLA Ops:
  0.0 3.0 %collective-permute-start = (bf16[128,512]{1,0:T(8,128)(2,1)}, bf16[128,512]{1,0:T(8,128)(2,1)S(1)}, u32[]{:S(2)}, u32[]{:S(2)}) collective-permute-start(bf16[128,512]{1,0:T(8,128)(2,1)} %bitcast.3), channel_id=1, source_target_pairs={{0,4},{1,5},{4,8},{5,9},{8,12},{9,13},{12,14},{13,15},{14,10},{15,... | collective-permute-start | bytes 393224 | tf_op jit(solution)/shard_map/ppermute | solution.py:192
  3.0 3.6 %collective-permute-done.refs_4_ = bf16[128,512]{1,0:T(8,128)(2,1)S(1)} collective-permute-done((bf16[128,512]{1,0:T(8,128)(2,1)}, bf16[128,512]{1,0:T(8,128)(2,1)S(1)}, u32[]{:S(2)}, u32[]{:S(2)}) %collective-permute-start) | collective-permute-done | bytes 131104 | tf_op jit(solution)/shard_map/ppermute | solution.py:192
  18.1 3.3 %gate_up.13 = (f32[128,896]{1,0:T(8,128)S(1)}, f32[128,896]{1,0:T(8,128)S(1)}, f32[128,128]{1,0:T(8,128)S(1)}) custom-call(f32[2,16,1,512]{3,2,1,0:T(1,128)S(1)} %reshape.10.refs_0_, bf16[2,8192,896]{2,1,0:T(8,128)(2,1)} %refs_1_.23, bf16[2,8192,896]{2,1,0:T(8,128)(2,1)} %refs_2_.23, ...), custom_call_target="tpu_custom_call", output_to_operand_aliasing={{0}: (6, {}), {1}: (7, {}), {2}: (8, {})} | custom-call | flops 704643072 | bytes 5505024 | tf_op jit(solution)/shard_map/gate_up/pallas_call | solution.py:124
  21.9 3.9 %gate_up.14 = (f32[128,896]{1,0:T(8,128)S(1)}, f32[128,896]{1,0:T(8,128)S(1)}, f32[128,128]{1,0:T(8,128)S(1)}) custom-call(f32[2,16,1,512]{3,2,1,0:T(1,128)S(1)} %reshape.10.refs_0_, bf16[2,8192,896]{2,1,0:T(8,128)(2,1)} %refs_1_.23, bf16[2,8192,896]{2,1,0:T(8,128)(2,1)} %refs_2_.23, ...), custom_call_target="tpu_custom_call", output_to_operand_aliasing={{0}: (7, {}), {1}: (8, {}), {2}: (9, {})} | custom-call | flops 939524096 | bytes 7340032 | tf_op jit(solution)/shard_map/gate_up/pallas_call | solution.py:124
  28.0 3.9 %gate_up.15 = (f32[128,896]{1,0:T(8,128)S(1)}, f32[128,896]{1,0:T(8,128)S(1)}, f32[128,128]{1,0:T(8,128)S(1)}) custom-call(f32[2,16,1,512]{3,2,1,0:T(1,128)S(1)} %reshape.10.refs_0_, bf16[2,8192,896]{2,1,0:T(8,128)(2,1)} %refs_1_.23, bf16[2,8192,896]{2,1,0:T(8,128)(2,1)} %refs_2_.23, ...), custom_call_target="tpu_custom_call", output_to_operand_aliasing={{0}: (7, {}), {1}: (8, {}), {2}: (9, {})} | custom-call | flops 939524096 | bytes 7340032 | tf_op jit(solution)/shard_map/gate_up/pallas_call | solution.py:124
  32.5 3.2 %gate_up.16 = (f32[128,896]{1,0:T(8,128)S(1)}, f32[128,896]{1,0:T(8,128)S(1)}, f32[128,128]{1,0:T(8,128)S(1)}) custom-call(f32[2,16,1,512]{3,2,1,0:T(1,128)S(1)} %reshape.10.refs_0_, bf16[2,8192,896]{2,1,0:T(8,128)(2,1)} %refs_1_.23, bf16[2,8192,896]{2,1,0:T(8,128)(2,1)} %refs_2_.23, ...), custom_call_target="tpu_custom_call", output_to_operand_aliasing={{0}: (7, {}), {1}: (8, {}), {2}: (9, {})} | custom-call | flops 704643072 | bytes 5505024 | tf_op jit(solution)/shard_map/gate_up/pallas_call | solution.py:124
  39.7 2.5 %down.13 = (f32[128,512]{1,0:T(8,128)S(1)}, f32[128,512]{1,0:T(8,128)S(1)}, bf16[128,512]{1,0:T(8,128)(2,1)S(1)}, bf16[128,512]{1,0:T(8,128)(2,1)S(1)}) custom-call(bf16[128,896]{1,0:T(8,128)(2,1)S(1)} %gate_up.17.hid_ref, bf16[2,896,8192]{2,1,0:T(8,128)(2,1)} %w_hbm.19), custom_call_target="tpu_custom_call" | custom-call | flops 469762048 | bytes 3670016 | tf_op jit(solution)/shard_map/down/pallas_call | solution.py:164
  53.0 3.9 %collective-permute-done.29 = bf16[64,512]{1,0:T(8,128)(2,1)S(1)} collective-permute-done((bf16[64,512]{1,0:T(8,128)(2,1)S(1)}, bf16[64,512]{1,0:T(8,128)(2,1)S(1)}, u32[]{:S(2)}, u32[]{:S(2)}) %collective-permute-start.29) | collective-permute-done | bytes 65568 | tf_op jit(solution)/shard_map/ppermute | solution.py:192
  58.5 3.3 %collective-permute-done.23 = bf16[128,512]{1,0:T(8,128)(2,1)S(1)} collective-permute-done((bf16[128,512]{1,0:T(8,128)(2,1)S(1)}, bf16[128,512]{1,0:T(8,128)(2,1)S(1)}, u32[]{:S(2)}, u32[]{:S(2)}) %collective-permute-start.23) | collective-permute-done | bytes 131104 | tf_op jit(solution)/shard_map/ppermute | solution.py:192
  63.9 2.8 %collective-permute-done.30 = bf16[128,512]{1,0:T(8,128)(2,1)S(1)} collective-permute-done((bf16[128,512]{1,0:T(8,128)(2,1)S(1)}, bf16[128,512]{1,0:T(8,128)(2,1)S(1)}, u32[]{:S(2)}, u32[]{:S(2)}) %collective-permute-start.30) | collective-permute-done | bytes 131104 | tf_op jit(solution)/shard_map/ppermute | solution.py:192
  69.3 3.6 %collective-permute-done.31 = bf16[128,512]{1,0:T(8,128)(2,1)S(1)} collective-permute-done((bf16[128,512]{1,0:T(8,128)(2,1)S(1)}, bf16[128,512]{1,0:T(8,128)(2,1)S(1)}, u32[]{:S(2)}, u32[]{:S(2)}) %collective-permute-start.31) | collective-permute-done | bytes 131104 | tf_op jit(solution)/shard_map/ppermute | solution.py:192
  73.1 5.9 %collective-permute-done.32 = bf16[128,512]{1,0:T(8,128)(2,1)S(1)} collective-permute-done((bf16[128,512]{1,0:T(8,128)(2,1)S(1)}, bf16[128,512]{1,0:T(8,128)(2,1)S(1)}, u32[]{:S(2)}, u32[]{:S(2)}) %collective-permute-start.32) | collective-permute-done | bytes 131104 | tf_op jit(solution)/shard_map/ppermute | solution.py:192
  81.2 2.9 %collective-permute-done.33.refs_4_ = bf16[128,512]{1,0:T(8,128)(2,1)S(1)} collective-permute-done((bf16[128,512]{1,0:T(8,128)(2,1)S(1)}, bf16[128,512]{1,0:T(8,128)(2,1)S(1)}, u32[]{:S(2)}, u32[]{:S(2)}) %collective-permute-start.33) | collective-permute-done | bytes 131104 | tf_op jit(solution)/shard_map/ppermute | solution.py:192
  93.7 3.3 %gate_up.19 = (f32[128,896]{1,0:T(8,128)S(1)}, f32[128,896]{1,0:T(8,128)S(1)}, f32[128,128]{1,0:T(8,128)S(1)}) custom-call(f32[2,16,1,512]{3,2,1,0:T(1,128)S(1)} %reshape.10.refs_0_, bf16[2,8192,896]{2,1,0:T(8,128)(2,1)} %refs_1_.23, bf16[2,8192,896]{2,1,0:T(8,128)(2,1)} %refs_2_.23, ...), custom_call_target="tpu_custom_call", output_to_operand_aliasing={{0}: (6, {}), {1}: (7, {}), {2}: (8, {})} | custom-call | flops 704643072 | bytes 5505024 | tf_op jit(solution)/shard_map/gate_up/pallas_call | solution.py:124
  97.6 3.9 %gate_up.20 = (f32[128,896]{1,0:T(8,128)S(1)}, f32[128,896]{1,0:T(8,128)S(1)}, f32[128,128]{1,0:T(8,128)S(1)}) custom-call(f32[2,16,1,512]{3,2,1,0:T(1,128)S(1)} %reshape.10.refs_0_, bf16[2,8192,896]{2,1,0:T(8,128)(2,1)} %refs_1_.23, bf16[2,8192,896]{2,1,0:T(8,128)(2,1)} %refs_2_.23, ...), custom_call_target="tpu_custom_call", output_to_operand_aliasing={{0}: (7, {}), {1}: (8, {}), {2}: (9, {})} | custom-call | flops 939524096 | bytes 7340032 | tf_op jit(solution)/shard_map/gate_up/pallas_call | solution.py:124
  103.9 3.9 %gate_up.21 = (f32[128,896]{1,0:T(8,128)S(1)}, f32[128,896]{1,0:T(8,128)S(1)}, f32[128,128]{1,0:T(8,128)S(1)}) custom-call(f32[2,16,1,512]{3,2,1,0:T(1,128)S(1)} %reshape.10.refs_0_, bf16[2,8192,896]{2,1,0:T(8,128)(2,1)} %refs_1_.23, bf16[2,8192,896]{2,1,0:T(8,128)(2,1)} %refs_2_.23, ...), custom_call_target="tpu_custom_call", output_to_operand_aliasing={{0}: (7, {}), {1}: (8, {}), {2}: (9, {})} | custom-call | flops 939524096 | bytes 7340032 | tf_op jit(solution)/shard_map/gate_up/pallas_call | solution.py:124
  108.4 3.2 %gate_up.22 = (f32[128,896]{1,0:T(8,128)S(1)}, f32[128,896]{1,0:T(8,128)S(1)}, f32[128,128]{1,0:T(8,128)S(1)}) custom-call(f32[2,16,1,512]{3,2,1,0:T(1,128)S(1)} %reshape.10.refs_0_, bf16[2,8192,896]{2,1,0:T(8,128)(2,1)} %refs_1_.23, bf16[2,8192,896]{2,1,0:T(8,128)(2,1)} %refs_2_.23, ...), custom_call_target="tpu_custom_call", output_to_operand_aliasing={{0}: (7, {}), {1}: (8, {}), {2}: (9, {})} | custom-call | flops 704643072 | bytes 5505024 | tf_op jit(solution)/shard_map/gate_up/pallas_call | solution.py:124
  115.6 2.5 %down.18 = (f32[128,512]{1,0:T(8,128)S(1)}, f32[128,512]{1,0:T(8,128)S(1)}, bf16[128,512]{1,0:T(8,128)(2,1)S(1)}, bf16[128,512]{1,0:T(8,128)(2,1)S(1)}) custom-call(bf16[128,896]{1,0:T(8,128)(2,1)S(1)} %gate_up.23.hid_ref, bf16[2,896,8192]{2,1,0:T(8,128)(2,1)} %w_hbm.19), custom_call_target="tpu_custom_call" | custom-call | flops 469762048 | bytes 3670016 | tf_op jit(solution)/shard_map/down/pallas_call | solution.py:164
  122.9 2.5 %down.16 = (f32[128,512]{1,0:T(8,128)S(1)}, f32[128,512]{1,0:T(8,128)S(1)}, bf16[128,512]{1,0:T(8,128)(2,1)S(1)}, bf16[128,512]{1,0:T(8,128)(2,1)S(1)}) custom-call(bf16[128,896]{1,0:T(8,128)(2,1)S(1)} %gate_up.23.hid_ref, bf16[2,896,8192]{2,1,0:T(8,128)(2,1)} %w_hbm.19), custom_call_target="tpu_custom_call" | custom-call | flops 469762048 | bytes 3670016 | tf_op jit(solution)/shard_map/down/pallas_call | solution.py:164
  128.6 3.8 %collective-permute-done.62 = bf16[64,512]{1,0:T(8,128)(2,1)S(1)} collective-permute-done((bf16[64,512]{1,0:T(8,128)(2,1)S(1)}, bf16[64,512]{1,0:T(8,128)(2,1)S(1)}, u32[]{:S(2)}, u32[]{:S(2)}) %collective-permute-start.62) | collective-permute-done | bytes 65568 | tf_op jit(solution)/shard_map/ppermute | solution.py:192
  134.1 3.2 %collective-permute-done.56 = bf16[128,512]{1,0:T(8,128)(2,1)S(1)} collective-permute-done((bf16[128,512]{1,0:T(8,128)(2,1)S(1)}, bf16[128,512]{1,0:T(8,128)(2,1)S(1)}, u32[]{:S(2)}, u32[]{:S(2)}) %collective-permute-start.56) | collective-permute-done | bytes 131104 | tf_op jit(solution)/shard_map/ppermute | solution.py:192
  139.5 2.8 %collective-permute-done.63 = bf16[128,512]{1,0:T(8,128)(2,1)S(1)} collective-permute-done((bf16[128,512]{1,0:T(8,128)(2,1)S(1)}, bf16[128,512]{1,0:T(8,128)(2,1)S(1)}, u32[]{:S(2)}, u32[]{:S(2)}) %collective-permute-start.63) | collective-permute-done | bytes 131104 | tf_op jit(solution)/shard_map/ppermute | solution.py:192
  144.9 3.6 %collective-permute-done.64 = bf16[128,512]{1,0:T(8,128)(2,1)S(1)} collective-permute-done((bf16[128,512]{1,0:T(8,128)(2,1)S(1)}, bf16[128,512]{1,0:T(8,128)(2,1)S(1)}, u32[]{:S(2)}, u32[]{:S(2)}) %collective-permute-start.64) | collective-permute-done | bytes 131104 | tf_op jit(solution)/shard_map/ppermute | solution.py:192
  149.0 4.6 %collective-permute-done.65 = bf16[128,512]{1,0:T(8,128)(2,1)S(1)} collective-permute-done((bf16[128,512]{1,0:T(8,128)(2,1)S(1)}, bf16[128,512]{1,0:T(8,128)(2,1)S(1)}, u32[]{:S(2)}, u32[]{:S(2)}) %collective-permute-start.65) | collective-permute-done | bytes 131104 | tf_op jit(solution)/shard_map/ppermute | solution.py:192
  (155 shorter events, 70.6 us)
Async XLA Ops:
  8.7 8.7 %collective-permute-start.16 = (bf16[128,512]{1,0:T(8,128)(2,1)}, bf16[128,512]{1,0:T(8,128)(2,1)S(1)}, u32[]{:S(2)}, u32[]{:S(2)}) collective-permute-start(bf16[128,512]{1,0:T(8,128)(2,1)} %bitcast.5), channel_id=1, source_target_pairs={{0,1},{1,0},{2,3},{3,2},{4,5},{5,4},{6,7},{7,6},{8,9},{9,8},{10,11... | collective-permute-start | bytes 393224 | tf_op jit(solution)/shard_map/ppermute | solution.py:192
  8.7 9.3 %collective-permute-start.14 = (bf16[128,512]{1,0:T(8,128)(2,1)S(1)}, bf16[128,512]{1,0:T(8,128)(2,1)S(1)}, u32[]{:S(2)}, u32[]{:S(2)}) collective-permute-start(bf16[128,512]{1,0:T(8,128)(2,1)S(1)} %collective-permute-done.refs_4_), channel_id=1, source_target_pairs={{0,1},{1,0},{2,3},{3,2},{4,5},{5,4},{6,7},{7,6},{8,9},{9,8},{10,11... | collective-permute-start | bytes 393224 | tf_op jit(solution)/shard_map/ppermute | solution.py:192
  11.6 9.7 %collective-permute-start.2 = (bf16[128,512]{1,0:T(8,128)(2,1)S(1)}, bf16[128,512]{1,0:T(8,128)(2,1)S(1)}, u32[]{:S(2)}, u32[]{:S(2)}) collective-permute-start(bf16[128,512]{1,0:T(8,128)(2,1)S(1)} %collective-permute-done.1.refs_5_), channel_id=1, source_target_pairs={{0,4},{1,5},{4,8},{5,9},{8,12},{9,13},{12,14},{13,15},{14,10},{15,... | collective-permute-start | bytes 393224 | tf_op jit(solution)/shard_map/ppermute | solution.py:192
  13.4 8.4 %collective-permute-start.7 = (bf16[128,512]{1,0:T(8,128)(2,1)S(1)}, bf16[128,512]{1,0:T(8,128)(2,1)S(1)}, u32[]{:S(2)}, u32[]{:S(2)}) collective-permute-start(bf16[128,512]{1,0:T(8,128)(2,1)S(1)} %collective-permute-done.6.refs_6_), channel_id=1, source_target_pairs={{4,0},{5,1},{8,4},{9,5},{12,8},{13,9},{14,12},{15,13},{10,14},{11,... | collective-permute-start | bytes 393224 | tf_op jit(solution)/shard_map/ppermute | solution.py:192
  17.4 10.3 %collective-permute-start.12 = (bf16[128,512]{1,0:T(8,128)(2,1)S(1)}, bf16[128,512]{1,0:T(8,128)(2,1)S(1)}, u32[]{:S(2)}, u32[]{:S(2)}) collective-permute-start(bf16[128,512]{1,0:T(8,128)(2,1)S(1)} %collective-permute-done.1.refs_5_), channel_id=1, source_target_pairs={{0,1},{1,0},{2,3},{3,2},{4,5},{5,4},{6,7},{7,6},{8,9},{9,8},{10,11... | collective-permute-start | bytes 393224 | tf_op jit(solution)/shard_map/ppermute | solution.py:192
  18.0 10.0 %collective-permute-start.13 = (bf16[128,512]{1,0:T(8,128)(2,1)S(1)}, bf16[128,512]{1,0:T(8,128)(2,1)S(1)}, u32[]{:S(2)}, u32[]{:S(2)}) collective-permute-start(bf16[128,512]{1,0:T(8,128)(2,1)S(1)} %collective-permute-done.6.refs_6_), channel_id=1, source_target_pairs={{0,1},{1,0},{2,3},{3,2},{4,5},{5,4},{6,7},{7,6},{8,9},{9,8},{10,11... | collective-permute-start | bytes 393224 | tf_op jit(solution)/shard_map/ppermute | solution.py:192
  21.4 11.2 %collective-permute-start.10 = (bf16[128,512]{1,0:T(8,128)(2,1)S(1)}, bf16[128,512]{1,0:T(8,128)(2,1)S(1)}, u32[]{:S(2)}, u32[]{:S(2)}) collective-permute-start(bf16[128,512]{1,0:T(8,128)(2,1)S(1)} %collective-permute-done.2.refs_5_), channel_id=1, source_target_pairs={{0,1},{1,0},{2,3},{3,2},{4,5},{5,4},{6,7},{7,6},{8,9},{9,8},{10,11... | collective-permute-start | bytes 393224 | tf_op jit(solution)/shard_map/ppermute | solution.py:192
  21.9 10.7 %collective-permute-start.11 = (bf16[128,512]{1,0:T(8,128)(2,1)S(1)}, bf16[128,512]{1,0:T(8,128)(2,1)S(1)}, u32[]{:S(2)}, u32[]{:S(2)}) collective-permute-start(bf16[128,512]{1,0:T(8,128)(2,1)S(1)} %collective-permute-done.7.refs_6_), channel_id=1, source_target_pairs={{0,1},{1,0},{2,3},{3,2},{4,5},{5,4},{6,7},{7,6},{8,9},{9,8},{10,11... | collective-permute-start | bytes 393224 | tf_op jit(solution)/shard_map/ppermute | solution.py:192
  42.2 10.1 %collective-permute-start.20 = (bf16[128,512]{1,0:T(8,128)(2,1)S(1)}, bf16[128,512]{1,0:T(8,128)(2,1)S(1)}, u32[]{:S(2)}, u32[]{:S(2)}) collective-permute-start(bf16[128,512]{1,0:T(8,128)(2,1)S(1)} %get-tuple-element.89), channel_id=1, source_target_pairs={{0,1},{1,0},{2,3},{3,2},{4,5},{5,4},{6,7},{7,6},{8,9},{9,8},{10,11... | collective-permute-start | bytes 393224 | tf_op jit(solution)/shard_map/ppermute | solution.py:192
  45.1 13.3 %collective-permute-start.19 = (bf16[128,512]{1,0:T(8,128)(2,1)S(1)}, bf16[128,512]{1,0:T(8,128)(2,1)S(1)}, u32[]{:S(2)}, u32[]{:S(2)}) collective-permute-start(bf16[128,512]{1,0:T(8,128)(2,1)S(1)} %get-tuple-element.87), channel_id=1, source_target_pairs={{0,1},{1,0},{2,3},{3,2},{4,5},{5,4},{6,7},{7,6},{8,9},{9,8},{10,11... | collective-permute-start | bytes 393224 | tf_op jit(solution)/shard_map/ppermute | solution.py:192
  49.8 17.3 %collective-permute-start.18 = (bf16[128,512]{1,0:T(8,128)(2,1)S(1)}, bf16[128,512]{1,0:T(8,128)(2,1)S(1)}, u32[]{:S(2)}, u32[]{:S(2)}) collective-permute-start(bf16[128,512]{1,0:T(8,128)(2,1)S(1)} %get-tuple-element.85), channel_id=1, source_target_pairs={{0,1},{1,0},{2,3},{3,2},{4,5},{5,4},{6,7},{7,6},{8,9},{9,8},{10,11... | collective-permute-start | bytes 393224 | tf_op jit(solution)/shard_map/ppermute | solution.py:192
  52.3 9.9 %collective-permute-start.27 = (bf16[128,512]{1,0:T(8,128)(2,1)S(1)}, bf16[128,512]{1,0:T(8,128)(2,1)S(1)}, u32[]{:S(2)}, u32[]{:S(2)}) collective-permute-start(bf16[128,512]{1,0:T(8,128)(2,1)S(1)} %get-tuple-element.95), channel_id=1, source_target_pairs={{0,1},{1,0},{2,3},{3,2},{4,5},{5,4},{6,7},{7,6},{8,9},{9,8},{10,11... | collective-permute-start | bytes 393224 | tf_op jit(solution)/shard_map/ppermute | solution.py:192
  52.8 16.5 %collective-permute-start.26 = (bf16[128,512]{1,0:T(8,128)(2,1)S(1)}, bf16[128,512]{1,0:T(8,128)(2,1)S(1)}, u32[]{:S(2)}, u32[]{:S(2)}) collective-permute-start(bf16[128,512]{1,0:T(8,128)(2,1)S(1)} %get-tuple-element.93), channel_id=1, source_target_pairs={{0,1},{1,0},{2,3},{3,2},{4,5},{5,4},{6,7},{7,6},{8,9},{9,8},{10,11... | collective-permute-start | bytes 393224 | tf_op jit(solution)/shard_map/ppermute | solution.py:192
  58.5 14.7 %collective-permute-start.17 = (bf16[128,512]{1,0:T(8,128)(2,1)S(1)}, bf16[128,512]{1,0:T(8,128)(2,1)S(1)}, u32[]{:S(2)}, u32[]{:S(2)}) collective-permute-start(bf16[128,512]{1,0:T(8,128)(2,1)S(1)} %get-tuple-element.83), channel_id=1, source_target_pairs={{0,1},{1,0},{2,3},{3,2},{4,5},{5,4},{6,7},{7,6},{8,9},{9,8},{10,11... | collective-permute-start | bytes 393224 | tf_op jit(solution)/shard_map/ppermute | solution.py:192
  93.1 10.2 %collective-permute-start.45 = (bf16[128,512]{1,0:T(8,128)(2,1)S(1)}, bf16[128,512]{1,0:T(8,128)(2,1)S(1)}, u32[]{:S(2)}, u32[]{:S(2)}) collective-permute-start(bf16[128,512]{1,0:T(8,128)(2,1)S(1)} %collective-permute-done.34.refs_5_), channel_id=1, source_target_pairs={{0,1},{1,0},{2,3},{3,2},{4,5},{5,4},{6,7},{7,6},{8,9},{9,8},{10,11... | collective-permute-start | bytes 393224 | tf_op jit(solution)/shard_map/ppermute | solution.py:192
  93.6 10.3 %collective-permute-start.46 = (bf16[128,512]{1,0:T(8,128)(2,1)S(1)}, bf16[128,512]{1,0:T(8,128)(2,1)S(1)}, u32[]{:S(2)}, u32[]{:S(2)}) collective-permute-start(bf16[128,512]{1,0:T(8,128)(2,1)S(1)} %collective-permute-done.39.refs_6_), channel_id=1, source_target_pairs={{0,1},{1,0},{2,3},{3,2},{4,5},{5,4},{6,7},{7,6},{8,9},{9,8},{10,11... | collective-permute-start | bytes 393224 | tf_op jit(solution)/shard_map/ppermute | solution.py:192
  97.0 11.4 %collective-permute-start.43 = (bf16[128,512]{1,0:T(8,128)(2,1)S(1)}, bf16[128,512]{1,0:T(8,128)(2,1)S(1)}, u32[]{:S(2)}, u32[]{:S(2)}) collective-permute-start(bf16[128,512]{1,0:T(8,128)(2,1)S(1)} %collective-permute-done.35.refs_5_), channel_id=1, source_target_pairs={{0,1},{1,0},{2,3},{3,2},{4,5},{5,4},{6,7},{7,6},{8,9},{9,8},{10,11... | collective-permute-start | bytes 393224 | tf_op jit(solution)/shard_map/ppermute | solution.py:192
  97.5 10.9 %collective-permute-start.44 = (bf16[128,512]{1,0:T(8,128)(2,1)S(1)}, bf16[128,512]{1,0:T(8,128)(2,1)S(1)}, u32[]{:S(2)}, u32[]{:S(2)}) collective-permute-start(bf16[128,512]{1,0:T(8,128)(2,1)S(1)} %collective-permute-done.40.refs_6_), channel_id=1, source_target_pairs={{0,1},{1,0},{2,3},{3,2},{4,5},{5,4},{6,7},{7,6},{8,9},{9,8},{10,11... | collective-permute-start | bytes 393224 | tf_op jit(solution)/shard_map/ppermute | solution.py:192
  118.1 9.7 %collective-permute-start.53 = (bf16[128,512]{1,0:T(8,128)(2,1)S(1)}, bf16[128,512]{1,0:T(8,128)(2,1)S(1)}, u32[]{:S(2)}, u32[]{:S(2)}) collective-permute-start(bf16[128,512]{1,0:T(8,128)(2,1)S(1)} %get-tuple-element.120), channel_id=1, source_target_pairs={{0,1},{1,0},{2,3},{3,2},{4,5},{5,4},{6,7},{7,6},{8,9},{9,8},{10,11... | collective-permute-start | bytes 393224 | tf_op jit(solution)/shard_map/ppermute | solution.py:192
  121.0 13.0 %collective-permute-start.52 = (bf16[128,512]{1,0:T(8,128)(2,1)S(1)}, bf16[128,512]{1,0:T(8,128)(2,1)S(1)}, u32[]{:S(2)}, u32[]{:S(2)}) collective-permute-start(bf16[128,512]{1,0:T(8,128)(2,1)S(1)} %get-tuple-element.118), channel_id=1, source_target_pairs={{0,1},{1,0},{2,3},{3,2},{4,5},{5,4},{6,7},{7,6},{8,9},{9,8},{10,11... | collective-permute-start | bytes 393224 | tf_op jit(solution)/shard_map/ppermute | solution.py:192
  125.4 17.4 %collective-permute-start.51 = (bf16[128,512]{1,0:T(8,128)(2,1)S(1)}, bf16[128,512]{1,0:T(8,128)(2,1)S(1)}, u32[]{:S(2)}, u32[]{:S(2)}) collective-permute-start(bf16[128,512]{1,0:T(8,128)(2,1)S(1)} %get-tuple-element.116), channel_id=1, source_target_pairs={{0,1},{1,0},{2,3},{3,2},{4,5},{5,4},{6,7},{7,6},{8,9},{9,8},{10,11... | collective-permute-start | bytes 393224 | tf_op jit(solution)/shard_map/ppermute | solution.py:192
  127.8 10.0 %collective-permute-start.60 = (bf16[128,512]{1,0:T(8,128)(2,1)S(1)}, bf16[128,512]{1,0:T(8,128)(2,1)S(1)}, u32[]{:S(2)}, u32[]{:S(2)}) collective-permute-start(bf16[128,512]{1,0:T(8,128)(2,1)S(1)} %get-tuple-element.126), channel_id=1, source_target_pairs={{0,1},{1,0},{2,3},{3,2},{4,5},{5,4},{6,7},{7,6},{8,9},{9,8},{10,11... | collective-permute-start | bytes 393224 | tf_op jit(solution)/shard_map/ppermute | solution.py:192
  128.5 16.4 %collective-permute-start.59 = (bf16[128,512]{1,0:T(8,128)(2,1)S(1)}, bf16[128,512]{1,0:T(8,128)(2,1)S(1)}, u32[]{:S(2)}, u32[]{:S(2)}) collective-permute-start(bf16[128,512]{1,0:T(8,128)(2,1)S(1)} %get-tuple-element.124), channel_id=1, source_target_pairs={{0,1},{1,0},{2,3},{3,2},{4,5},{5,4},{6,7},{7,6},{8,9},{9,8},{10,11... | collective-permute-start | bytes 393224 | tf_op jit(solution)/shard_map/ppermute | solution.py:192
  134.1 15.0 %collective-permute-start.50 = (bf16[128,512]{1,0:T(8,128)(2,1)S(1)}, bf16[128,512]{1,0:T(8,128)(2,1)S(1)}, u32[]{:S(2)}, u32[]{:S(2)}) collective-permute-start(bf16[128,512]{1,0:T(8,128)(2,1)S(1)} %get-tuple-element.114), channel_id=1, source_target_pairs={{0,1},{1,0},{2,3},{3,2},{4,5},{5,4},{6,7},{7,6},{8,9},{9,8},{10,11... | collective-permute-start | bytes 393224 | tf_op jit(solution)/shard_map/ppermute | solution.py:192
  (43 other events, 228.2 us)

commit v2 on v0

v2 whole, which is shorter than its diff:
```python
import functools

import jax
import jax.numpy as jnp
from jax import lax
from jax.experimental import pallas as pl
from jax.experimental.pallas import tpu as pltpu
from jax.sharding import PartitionSpec as P

AXIS = "width"
EPS = 1e-05
VMEM = pl.BlockSpec(memory_space=pltpu.VMEM)
HBM = pl.BlockSpec(memory_space=pl.ANY)
LIMIT = 20 * 1024 * 1024
DIRECT = ()
AHEAD = {
    (0, "gather1"): 4, (0, "gather2"): 4, (0, "gather3"): 4, (0, "gather4"): 4, (0, "gathered"): 2,
    (0, "scatter2"): 2, (0, "scatter1"): 4, (0, "scatter0"): 4,
    (1, "gather1"): 4, (1, "gather2"): 4, (1, "gather3"): 2,
}


def place_of(chip, chips):
    half = chip // 2
    return half + (chip - 2 * half) * (chips - 1 - 2 * half)


def chip_at(place, chips):
    far = (place >= chips // 2) * 1
    return 2 * place + far * (2 * chips - 1 - 4 * place)


def shard_at(offset, sibling, chips):
    me = lax.axis_index(AXIS)
    chip = me // 2
    core = me - 2 * chip
    place = lax.rem(place_of(chip, chips) + (offset + chips), chips)
    far = jnp.where(place >= chips // 2, 1, 0)
    there = 2 * place + far * (2 * chips - 1 - 4 * place)
    return 2 * there + (1 - core if sibling else core)


def view(key, ref, chips):
    kind, layer, offset, sibling = key
    size = ref.shape[2 if kind == "d" else 1] // (2 * chips)
    span = pl.ds(pl.multiple_of(shard_at(offset, sibling, chips) * size, size), size)
    return ref.at[layer, :, span] if kind == "d" else ref.at[layer, span, :]


def stage_kernel(chips, job, raw, stream, fetch, names_in, names_out, *refs):
    named = dict(zip(names_in, refs))
    out = dict(zip(names_out, refs[len(names_in) :]))
    scratch = list(refs[len(names_in) + len(names_out) :])
    copies = {}
    if raw or stream or fetch:
        sems = scratch.pop()
        for e, name in enumerate(raw):
            copies[name] = pltpu.make_async_copy(named["raw", name], out[name], sems.at[len(stream + fetch) + e])
            copies[name].start()
            named[name] = out[name]
        for e, key in enumerate(stream + fetch):
            if key in stream:
                named[key] = scratch.pop(0)
            to = named[key] if key in stream else out[key]
            copies[key] = pltpu.make_async_copy(view(key, named["hbm", key[0]], chips), to, sems.at[e])
            copies[key].start()

    def block(key):
        if key in copies:
            copies[key].wait()
        return named[key][...]

    for name in raw:
        copies[name].wait()
    job(block, named, out, scratch)
    for key in fetch:
        copies[key].wait()


def stage(chips, weights, blocks, job, keys, inputs, outputs, aliases, scratch, ahead, flops, name, raw=()):
    ins = dict(inputs)
    stream = []
    units = [unit for unit in weights["units"] if unit[0] not in keys]
    fetch = [key for unit in units[:ahead] for key in unit]
    weights["units"] = units[ahead:]
    for key in keys:
        if key in blocks:
            ins[key] = blocks.pop(key)
        else:
            stream.append(key)
    _, features, hid = weights["g"].shape
    size = features // (2 * chips)
    shapes = {key: (hid, size) if key[0] == "d" else (size, hid) for key in stream + fetch}
    kinds = sorted({key[0] for key in stream + fetch})
    names_in = list(ins) + [("hbm", kind) for kind in kinds] + [("raw", key) for key in raw]
    out_shape = dict(outputs)
    for key in raw:
        out_shape[key] = jax.ShapeDtypeStruct(raw[key].shape, raw[key].dtype)
    for key in fetch:
        out_shape[key] = jax.ShapeDtypeStruct(shapes[key], jnp.bfloat16)
    names_out = list(out_shape)
    scratch = [pltpu.VMEM(shapes[key], jnp.bfloat16) for key in stream] + scratch
    if raw or stream or fetch:
        scratch.append(pltpu.SemaphoreType.DMA((len(stream + fetch) + len(raw),)))
    results = pl.pallas_call(
        functools.partial(stage_kernel, chips, job, list(raw), stream, fetch, names_in, names_out),
        out_shape=list(out_shape.values()),
        in_specs=[VMEM] * len(ins) + [HBM] * (len(kinds) + len(raw)),
        out_specs=[VMEM] * len(names_out),
        scratch_shapes=scratch,
        input_output_aliases={names_in.index(a): names_out.index(b) for a, b in aliases.items()},
        compiler_params=pltpu.CompilerParams(vmem_limit_bytes=LIMIT),
        cost_estimate=pl.CostEstimate(
            flops=flops, bytes_accessed=sum(2 * a * b for a, b in shapes.values()), transcendentals=0
        ),
        name=name,
    )(
        *ins.values(),
        *(pltpu.with_memory_space_constraint(x, pltpu.HBM) for x in [*(weights[k] for k in kinds), *dict(raw).values()]),
    )
    results = dict(zip(names_out, results))
    for key in fetch:
        blocks[key] = results.pop(key)
    return results


def multiply(layer, chips, work, pieces, block, named, out):
    ys = {}
    for shard in [shard for shard in pieces if any(shard in shards for shards in work.values())]:
        parts = [named["x", shard, i][...] for i in range(pieces[shard])]
        x = (parts[0] if len(parts) == 1 else jnp.concatenate(parts, 0)).astype(jnp.float32)
        if shard in work["gate"]:
            square = x * x
            q = square[:, :128]
            for lane in range(128, x.shape[1], 128):
                q = q + square[:, lane : lane + 128]
            if shard != work["gate"][0]:
                out["squares"][...] += q
            elif ("old", "squares") in named:
                out["squares"][...] = named["old", "squares"][...] + q
            else:
                out["squares"][...] = q
        ys[shard] = (x * named["gain"][layer : layer + 1, pl.ds(pl.multiple_of(shard_at(*shard, chips) * x.shape[1], x.shape[1]), x.shape[1])]).astype(jnp.bfloat16)
    for name, kind in (("up", "u"), ("gate", "g")):
        for e, shard in enumerate(work[name]):
            value = jnp.dot(ys[shard], block((kind, layer, *shard)), preferred_element_type=jnp.float32)
            if e:
                out[name][...] += value
            elif ("old", name) in named:
                out[name][...] = named["old", name][...] + value
            else:
                out[name][...] = value


def ring_body(chips, stream_in, norm_gain, w_gate, w_up, w_down):
    micro, seqs, cols = stream_in.shape
    rows = micro * seqs
    part = rows // 2
    layers, features, hid = w_gate.shape
    far = chips // 2
    ring = [chip_at(place, chips) for place in range(chips)]
    right = [(2 * ring[i] + c, 2 * ring[(i + 1) % chips] + c) for i in range(chips) for c in range(2)]
    left = [(b, a) for a, b in right]
    right2 = [(2 * ring[i] + c, 2 * ring[(i + 2) % chips] + c) for i in range(chips) for c in range(2)]
    left2 = [(b, a) for a, b in right2]
    swap = [(i, i ^ 1) for i in range(2 * chips)]
    f32, bf16 = jnp.float32, jnp.bfloat16
    weights = {"g": w_gate, "u": w_up, "d": w_down}
    blocks = {}
    kept = {}
    flops = 2 * rows * cols * hid

    def send(x, perm):
        return lax.ppermute(x, AXIS, perm)

    def fence(*groups):
        found = []

        def walk(value, visit):
            if isinstance(value, dict):
                return {key: walk(part, visit) for key, part in value.items()}
            if isinstance(value, (list, tuple)):
                return type(value)(walk(part, visit) for part in value)
            return visit(value) if isinstance(value, jax.Array) else value

        walk(groups, lambda x: found.append(x))
        kept = iter(lax.optimization_barrier(found))
        out = walk(groups, lambda x: next(kept))
        return out if len(out) > 1 else out[0]

    sums = {
        "gate": jax.ShapeDtypeStruct((rows, hid), f32),
        "up": jax.ShapeDtypeStruct((rows, hid), f32),
        "squares": jax.ShapeDtypeStruct((rows, 128), f32),
    }

    def direct(layer):
        return far == 4 and layer in DIRECT

    def both(offset):
        return [offset, -offset] if offset > 0 else [0] if offset == 0 else []

    def stages(layer):
        if direct(layer):
            return [
                [(0, False)], [(0, True), (-1, False), (1, False), (-2, False), (2, False)],
                [(-1, True), (1, True), (-2, True), (2, True), (-3, False), (3, False), (4, False)],
                [(-3, True), (3, True), (4, True)],
            ]
        shards = [[(0, False)], [(0, True), (-1, False), (1, False)]]
        shards += [[(1 - s, True), (s - 1, True), (-s, False), (s, False)] for s in range(2, far)]
        return shards + [[(1 - far, True), (far - 1, True), (far, False)], [(far, True)]]

    units = []
    for layer in range(layers):
        units += [[("g", layer, *shard), ("u", layer, *shard)] for shards in stages(layer) for shard in shards]
        units += [[("d", layer, o, True), ("d", layer, o, False)] for step in range(far, -1, -1) for o in
                  ([far] if step == far else both(step))]
    weights["units"] = units

    def ahead(layer, name):
        return AHEAD.get((layer, name), 0)

    def shards_in(layer, xs, work, acc):
        ins = {"gain": kept["gain"]} if kept else {}
        ins.update({("x", shard, i): x for shard, arrays in xs.items() for i, x in enumerate(arrays) if kept})
        ins.update({("old", name): value for name, value in acc.items()})
        keys = [(kind, layer, *s) for name, kind in (("up", "u"), ("gate", "g")) for s in work[name]]
        return ins, keys, {shard: len(arrays) for shard, arrays in xs.items()}

    def gate_up(layer, xs, acc, fetch):
        work = {"gate": list(xs), "up": list(xs)}
        ins, keys, pieces = shards_in(layer, xs, work, acc)
        outs = {name: s for name, s in sums.items() if name in acc or work.get(name, work["gate"])}

        def job(block, named, out, scratch):
            multiply(layer, chips, work, pieces, block, named, out)

        raw = {} if kept else {"gain": norm_gain, ("x", (0, False), 0): stream}
        out = stage(
            chips, weights, blocks, job, keys, ins, outs, {("old", name): name for name in acc}, [], fetch,
            len(keys) * flops, "gate_up", raw,
        )
        for name in raw:
            kept[name] = out.pop(name)
        return out

    def finish(layer, xs, acc, fetch):
        work = {"gate": list(xs), "up": list(xs)}
        ins, keys, pieces = shards_in(layer, xs, work, acc)

        def job(block, named, out, scratch):
            into = dict(zip(sums, scratch))
            multiply(layer, chips, work, pieces, block, named, into)
            meansq = jnp.sum(into["squares"][...], axis=1, keepdims=True) / features
            scale = lax.rsqrt(meansq + EPS)
            g = into["gate"][...] * scale
            hidden = (g / (1.0 + jnp.exp(-g)) * (into["up"][...] * scale)).astype(bf16)
            out["hidden"][...] = hidden
            project(layer, [far], hidden, block, out)

        outs = {"hidden": jax.ShapeDtypeStruct((rows, hid), bf16), **chunk_shapes([far])}
        scratch = [pltpu.VMEM(s.shape, s.dtype) for s in sums.values()]
        return stage(
            chips, weights, blocks, job, keys + [("d", layer, far, s) for s in (True, False)], ins, outs, {},
            scratch, fetch, (len(keys) + 2) * flops, "hidden",
        )

    def chunk_shapes(offsets):
        outs = {("sib", o): jax.ShapeDtypeStruct((rows, cols), bf16) for o in offsets}
        outs.update({("own", o): jax.ShapeDtypeStruct((rows, cols), f32) for o in offsets})
        return outs

    def project(layer, offsets, hidden, block, out):
        for o in offsets:
            sib = jnp.dot(hidden, block(("d", layer, o, True)), preferred_element_type=f32)
            out["sib", o][...] = sib.astype(bf16)
            out["own", o][...] = jnp.dot(hidden, block(("d", layer, o, False)), preferred_element_type=f32)

    def down(layer, offsets, hidden, fetch):
        def job(block, named, out, scratch):
            project(layer, offsets, named["hidden"][...], block, out)

        keys = [("d", layer, o, s) for o in offsets for s in (True, False)]
        return stage(
            chips, weights, blocks, job, keys, {"hidden": hidden}, chunk_shapes(offsets), {}, [], fetch,
            len(keys) * flops, "down",
        )

    stream = stream_in.reshape(rows, cols)
    for layer in range(layers):
        acc = {}
        held = {(0, False): (stream,)}
        crossing = {(0, True): (stream,)}
        if direct(layer):
            moved = {
                (-2, False): (send(stream, right2),), (2, False): (send(stream, left2),),
                (-1, False): (send(stream, right),), (1, False): (send(stream, left),),
            }
            crossed = {shard: tuple(send(x, swap) for x in xs) for shard, xs in crossing.items()}
            acc = gate_up(layer, held, acc, ahead(layer, "gather1"))
            acc, moved, crossed = fence(acc, moved, crossed)
            held = {**crossed, **moved}
            (r,), (l,) = moved[-2, False], moved[2, False]
            crossing = {(o, True): xs for (o, _), xs in moved.items()}
            moved = {
                (-3, False): (send(r, right),), (3, False): (send(l, left),),
                (4, False): (send(r[:part], right2), send(l[part:], left2)),
            }
            crossed = {shard: tuple(send(x, swap) for x in xs) for shard, xs in crossing.items()}
            acc = gate_up(layer, held, acc, ahead(layer, "gather2"))
            acc, moved, crossed = fence(acc, moved, crossed)
            held = {**crossed, **moved}
            crossing = {(o, True): xs for (o, _), xs in moved.items()}
        else:
            r = l = stream
            for step in range(1, far + 1):
                if step > 1:
                    r, acc, held = fence(r, acc, held)
                    l, held = fence(l, held)
                    crossing = {(1 - step, True): (r,), (step - 1, True): (l,)}
                    held = {**held, (1 - step, False): (r,), (step - 1, False): (l,)}
                if step == far:
                    r, l = r[:part], l[part:]
                r, l = send(r, right), send(l, left)
                crossed = {shard: tuple(send(x, swap) for x in xs) for shard, xs in crossing.items()}
                acc = gate_up(layer, held, acc, ahead(layer, "gather%d" % step))
                held = crossed
            r, l, acc, held = fence(r, l, acc, held)
            held = {**held, (far, False): (r, l)}
            crossing = {(far, True): (r, l)}
        crossed = {shard: tuple(send(x, swap) for x in xs) for shard, xs in crossing.items()}
        acc = gate_up(layer, held, acc, ahead(layer, "gathered"))
        acc, crossed = fence(acc, crossed)
        found = finish(layer, crossed, acc, ahead(layer, "hidden"))
        hidden, found = fence(found.pop("hidden"), found)
        c = send(found["sib", far], swap)
        own = found["own", far]
        found = down(layer, both(far - 1), hidden, ahead(layer, "scatter%d" % far))
        c, found = fence(c, found)
        total = (own + c.astype(f32)).astype(bf16)
        hidden, total = fence(hidden, total)
        r, l = total[:part], total[part:]
        for step in range(far - 1, -1, -1):
            r, l = send(r, right), send(l, left)
            if not step:
                if ahead(layer, "scatter0"):
                    count = ahead(layer, "scatter0")
                    stage(chips, weights, blocks, lambda *given: None, [], {"hidden": hidden}, {}, {}, [], count, 0, "ahead")
                break
            c = [send(found["sib", o], swap) for o in both(step)]
            own = [found["own", o] for o in both(step)]
            found = down(layer, both(step - 1), hidden, ahead(layer, "scatter%d" % step))
            if step == far - 1:
                hole = jnp.zeros((part, cols), bf16)
                r, l = jnp.concatenate([r, hole], 0), jnp.concatenate([hole, l], 0)
            l, c, found = fence(l, c, found)
            l = fence((own[1] + c[1].astype(f32) + l.astype(f32)).astype(bf16))
            r, _ = fence(r, l)
            r = (own[0] + c[0].astype(f32) + r.astype(f32)).astype(bf16)
            hidden, r = fence(hidden, r)
            if step == 1:
                c = send(found["sib", 0], swap)
        r, l, c, _ = fence(r, l, c, dict(blocks))
        branch = found["own", 0] + c.astype(f32) + r.astype(f32) + l.astype(f32)
        stream = (stream.astype(f32) + branch).astype(bf16)
    return stream.reshape(micro, seqs, cols)


def plain_body(stream_in, norm_gain, w_gate, w_up, w_down):
    micro, seqs, cols = stream_in.shape
    layers = w_gate.shape[0]
    f32, bf16 = jnp.float32, jnp.bfloat16
    stream = stream_in.reshape(micro * seqs, cols)
    for layer in range(layers):
        whole = lax.all_gather(stream, AXIS, axis=1, tiled=True).astype(f32)
        meansq = jnp.mean(whole * whole, axis=1, keepdims=True)
        normed = (whole * lax.rsqrt(meansq + EPS) * norm_gain[layer]).astype(bf16)
        gate_out = jnp.dot(normed, w_gate[layer], preferred_element_type=f32)
        up_out = jnp.dot(normed, w_up[layer], preferred_element_type=f32)
        hidden = (jax.nn.silu(gate_out) * up_out).astype(bf16)
        partials = jnp.dot(hidden, w_down[layer], preferred_element_type=f32)
        branch = lax.psum_scatter(partials, AXIS, scatter_dimension=1, tiled=True)
        stream = (stream.astype(f32) + branch).astype(bf16)
    return stream.reshape(micro, seqs, cols)


def solution(mesh):
    devices = mesh.shape[AXIS]

    def body(stream_in, *rest):
        cols = stream_in.shape[2]
        if devices % 8 == 0 and cols % 128 == 0:
            return ring_body(devices // 2, stream_in, *rest)
        return plain_body(stream_in, *rest)

    return jax.shard_map(
        body,
        mesh=mesh,
        in_specs=(
            P(None, "groups", AXIS),
            P(),
            P(None, None, AXIS),
            P(None, None, AXIS),
            P(None, AXIS, None),
        ),
        out_specs=P(None, "groups", AXIS),
        check_vma=False,
    )
```

time: 417 us -> 116 us (0.28)
  waiting for transfers between devices: 299 us -> 17.3 us
  matrix products: 90.2 us -> 0 us
  Pallas kernels: 0 us -> 55.5 us
  starting transfers between devices: 0.3 us -> 40.8 us
  between operations: 13.2 us -> 0.65 us
  other arithmetic: 9.94 us -> 1.43 us
    psum x2 -> x0, waiting for transfers between devices: 222 us -> none  [body(): branch = lax.psum(partials, 'width')]
    dot_general x8 -> x0, matrix products: 90.2 us -> none  [the longest x4 63.7 us: body(): jnp.dot(hidden, w_down[depth], preferred_element_type=jnp.float32)]
    all_gather x2 -> x0, waiting for transfers between devices: 76.1 us -> none  [body(): lax.all_gather(stream_in[micro_index], 'width', axis=1, tiled=True)]
    pallas_call x0 -> x21, Pallas kernels: none -> 55.5 us  [stage(): pl.pallas_call(functools.partial(stage_kernel, chips, job, list(raw), str...]
    ppermute x0 -> x66, starting transfers between devices: none -> 40.8 us  [send(): return lax.ppermute(x, AXIS, perm)]
    ppermute x0 -> x66, waiting for transfers between devices: none -> 17.3 us  [send(): return lax.ppermute(x, AXIS, perm)]
    reduce_sum x3 -> x0, other arithmetic: 7.33 us -> none  [body(): meansq = jnp.mean(stream_f * stream_f, axis=1, keepdims=True)]
  transfers between devices with their start and end apart: 4 -> 66, of which waited for: 4 -> 18; matrix products, arithmetic and copies ran while one was open for 1% -> 0% of each run, Pallas kernels for 0% -> 46%
where the time goes in v2:
time: 116 us
  Pallas kernels  55.5 us (48%)
  starting transfers between devices  40.8 us (35%)
  waiting for transfers between devices  17.3 us (15%)
  other arithmetic  1.43 us (1%)
    pallas_call x21, Pallas kernels, stage(): pl.pallas_call(functools.partial(stage_kernel, chips, job, list(raw), str...  55.5 us
    ppermute x66, starting transfers between devices, send(): return lax.ppermute(x, AXIS, perm)  40.8 us
    ppermute x66, waiting for transfers between devices, send(): return lax.ppermute(x, AXIS, perm)  17.3 us
  transfers between devices with their start and end apart: 66, of which 18 were waited for; matrix products, arithmetic and copies ran while one was open for 0% of the time, Pallas kernels for 46%

profile of v2, /device:TPU:0, one launch (start us, length us, event | category | flops | bytes accessed | tf_op | source)
XLA Modules:
  0.0 115.7 jit_solution(12118169079749312662)
XLA Ops:
  0.0 3.0 %collective-permute-start = (bf16[128,512]{1,0:T(8,128)(2,1)}, bf16[128,512]{1,0:T(8,128)(2,1)S(1)}, u32[]{:S(2)}, u32[]{:S(2)}) collective-permute-start(bf16[128,512]{1,0:T(8,128)(2,1)} %bitcast.3), channel_id=1, source_target_pairs={{0,4},{1,5},{4,8},{5,9},{8,12},{9,13},{12,14},{13,15},{14,10},{15,... | collective-permute-start | bytes 393224 | tf_op jit(solution)/shard_map/ppermute | solution.py:174
  3.0 4.5 %gate_up.10 = (f32[128,896]{1,0:T(8,128)S(1)}, f32[128,896]{1,0:T(8,128)S(1)}, f32[128,128]{1,0:T(8,128)S(1)}, f32[2,8192]{1,0:T(2,128)S(1)}, bf16[128,512]{1,0:...) custom-call(bf16[2,8192,896]{2,1,0:T(8,128)(2,1)} %refs_14_.5, ...), custom_call_target="tpu_custom_call" | custom-call | flops 234881024 | bytes 9175040 | tf_op jit(solution)/shard_map/gate_up/pallas_call | solution.py:105
  7.5 1.6 %collective-permute-done.3.refs_3_ = bf16[128,512]{1,0:T(8,128)(2,1)S(1)} collective-permute-done((bf16[128,512]{1,0:T(8,128)(2,1)}, bf16[128,512]{1,0:T(8,128)(2,1)S(1)}, u32[]{:S(2)}, u32[]{:S(2)}) %collective-permute-start.3) | collective-permute-done | bytes 131104 | tf_op jit(solution)/shard_map/ppermute | solution.py:174
  11.4 4.1 %gate_up.11 = (f32[128,896]{1,0:T(8,128)S(1)}, f32[128,896]{1,0:T(8,128)S(1)}, f32[128,128]{1,0:T(8,128)S(1)}, bf16[512,896]{1,0:T(8,128)(2,1)S(1)}, bf16[512,89...) custom-call(f32[2,8192]{1,0:T(2,128)S(1)} %get-tuple-element.295.ref, ...), custom_call_target="tpu_custom_call", output_to_operand_aliasing={{0}: (4, {}), {1}: (5, {}), {2}: (6, {})} | custom-call | flops 704643072 | bytes 7340032 | tf_op jit(solution)/shard_map/gate_up/pallas_call | solution.py:105
  18.9 4.3 %gate_up.12 = (f32[128,896]{1,0:T(8,128)S(1)}, f32[128,896]{1,0:T(8,128)S(1)}, f32[128,128]{1,0:T(8,128)S(1)}, bf16[512,896]{1,0:T(8,128)(2,1)S(1)}, bf16[512,89...) custom-call(f32[2,8192]{1,0:T(2,128)S(1)} %get-tuple-element.295.ref, ...), custom_call_target="tpu_custom_call", output_to_operand_aliasing={{0}: (5, {}), {1}: (6, {}), {2}: (7, {})} | custom-call | flops 939524096 | bytes 7340032 | tf_op jit(solution)/shard_map/gate_up/pallas_call | solution.py:105
  26.7 4.1 %gate_up.13 = (f32[128,896]{1,0:T(8,128)S(1)}, f32[128,896]{1,0:T(8,128)S(1)}, f32[128,128]{1,0:T(8,128)S(1)}, bf16[512,896]{1,0:T(8,128)(2,1)S(1)}, bf16[512,89...) custom-call(f32[2,8192]{1,0:T(2,128)S(1)} %get-tuple-element.295.ref, ...), custom_call_target="tpu_custom_call", output_to_operand_aliasing={{0}: (5, {}), {1}: (6, {}), {2}: (7, {})} | custom-call | flops 939524096 | bytes 7340032 | tf_op jit(solution)/shard_map/gate_up/pallas_call | solution.py:105
  31.5 2.8 %gate_up.14 = (f32[128,896]{1,0:T(8,128)S(1)}, f32[128,896]{1,0:T(8,128)S(1)}, f32[128,128]{1,0:T(8,128)S(1)}, bf16[896,512]{1,0:T(8,128)(2,1)S(1)}, bf16[896,51...) custom-call(f32[2,8192]{1,0:T(2,128)S(1)} %get-tuple-element.295.ref, ...), custom_call_target="tpu_custom_call", output_to_operand_aliasing={{0}: (5, {}), {1}: (6, {}), {2}: (7, {})} | custom-call | flops 704643072 | bytes 3670016 | tf_op jit(solution)/shard_map/gate_up/pallas_call | solution.py:105
  39.3 2.5 %down.9 = (bf16[128,512]{1,0:T(8,128)(2,1)S(1)}, bf16[128,512]{1,0:T(8,128)(2,1)S(1)}, f32[128,512]{1,0:T(8,128)S(1)}, f32[128,512]{1,0:T(8,128)S(1)}) custom-call(bf16[128,896]{1,0:T(8,128)(2,1)S(1)} %get-tuple-element.447.refs_0_, bf16[2,896,8192]{2,1,0:T(8,128)(2,1)} %refs_1_.13), custom_call_target="tpu_custom_call" | custom-call | flops 469762048 | bytes 3670016 | tf_op jit(solution)/shard_map/down/pallas_call | solution.py:105
  43.1 1.6 %collective-permute-start.28 = (bf16[128,512]{1,0:T(8,128)(2,1)S(1)}, bf16[128,512]{1,0:T(8,128)(2,1)S(1)}, u32[]{:S(2)}, u32[]{:S(2)}) collective-permute-start(bf16[128,512]{1,0:T(8,128)(2,1)S(1)} %add_convert_fusion.13), channel_id=1, source_target_pairs={{0,4},{1,5},{4,8},{5,9},{8,12},{9,13},{12,14},{13,15},{14,10},{15,... | collective-permute-start | bytes 393224 | tf_op jit(solution)/shard_map/ppermute | solution.py:174
  44.8 3.2 %down.10 = (bf16[128,512]{1,0:T(8,128)(2,1)S(1)}, bf16[128,512]{1,0:T(8,128)(2,1)S(1)}, f32[128,512]{1,0:T(8,128)S(1)}, f32[128,512]{1,0:T(8,128)S(1)}, bf16[896...) custom-call(bf16[128,896]{1,0:T(8,128)(2,1)S(1)} %get-tuple-element., ...), custom_call_target="tpu_custom_call" | custom-call | flops 469762048 | bytes 7340032 | tf_op jit(solution)/shard_map/down/pallas_call | solution.py:105
  49.2 1.6 %collective-permute-start.29 = (bf16[128,512]{1,0:T(8,128)(2,1)S(1)}, bf16[128,512]{1,0:T(8,128)(2,1)S(1)}, u32[]{:S(2)}, u32[]{:S(2)}) collective-permute-start(bf16[128,512]{1,0:T(8,128)(2,1)S(1)} %add_convert_fusion.11), channel_id=1, source_target_pairs={{0,4},{1,5},{4,8},{5,9},{8,12},{9,13},{12,14},{13,15},{14,10},{15,... | collective-permute-start | bytes 393224 | tf_op jit(solution)/shard_map/ppermute | solution.py:174
  50.8 3.5 %down.11 = (bf16[128,512]{1,0:T(8,128)(2,1)S(1)}, f32[128,512]{1,0:T(8,128)S(1)}, bf16[512,896]{1,0:T(8,128)(2,1)S(1)}, bf16[512,896]{1,0:T(8,128)(2,1)S(1)}, bf...) custom-call(bf16[128,896]{1,0:T(8,128)(2,1)S(1)} %get-tuple-element., ...), custom_call_target="tpu_custom_call" | custom-call | flops 234881024 | bytes 7340032 | tf_op jit(solution)/shard_map/down/pallas_call | solution.py:105
  55.0 1.6 %collective-permute-start.30 = (bf16[128,512]{1,0:T(8,128)(2,1)S(1)}, bf16[128,512]{1,0:T(8,128)(2,1)S(1)}, u32[]{:S(2)}, u32[]{:S(2)}) collective-permute-start(bf16[128,512]{1,0:T(8,128)(2,1)S(1)} %add_convert_fusion.9), channel_id=1, source_target_pairs={{0,4},{1,5},{4,8},{5,9},{8,12},{9,13},{12,14},{13,15},{14,10},{15,... | collective-permute-start | bytes 393224 | tf_op jit(solution)/shard_map/ppermute | solution.py:174
  56.6 3.2 %ahead.1 = (bf16[512,896]{1,0:T(8,128)(2,1)S(1)}, bf16[512,896]{1,0:T(8,128)(2,1)S(1)}, bf16[512,896]{1,0:T(8,128)(2,1)S(1)}, bf16[512,896]{1,0:T(8,128)(2,1)S(1...) custom-call(bf16[128,896]{1,0:T(8,128)(2,1)S(1)} %get-tuple-element., ...), custom_call_target="tpu_custom_call" | custom-call | bytes 7340032 | tf_op jit(solution)/shard_map/ahead/pallas_call | solution.py:105
  62.2 3.5 %gate_up.15 = (f32[128,896]{1,0:T(8,128)S(1)}, f32[128,896]{1,0:T(8,128)S(1)}, f32[128,128]{1,0:T(8,128)S(1)}, bf16[512,896]{1,0:T(8,128)(2,1)S(1)}, bf16[512,89...) custom-call(f32[2,8192]{1,0:T(2,128)S(1)} %get-tuple-element.295.ref, ...), custom_call_target="tpu_custom_call" | custom-call | flops 234881024 | bytes 7340032 | tf_op jit(solution)/shard_map/gate_up/pallas_call | solution.py:105
  65.9 1.8 %collective-permute-done.36.refs_3_ = bf16[128,512]{1,0:T(8,128)(2,1)S(1)} collective-permute-done((bf16[128,512]{1,0:T(8,128)(2,1)S(1)}, bf16[128,512]{1,0:T(8,128)(2,1)S(1)}, u32[]{:S(2)}, u32[]{:S(2)}) %collective-permute-start.36) | collective-permute-done | bytes 131104 | tf_op jit(solution)/shard_map/ppermute | solution.py:174
  67.6 1.6 %collective-permute-start.35 = (bf16[128,512]{1,0:T(8,128)(2,1)S(1)}, bf16[128,512]{1,0:T(8,128)(2,1)S(1)}, u32[]{:S(2)}, u32[]{:S(2)}) collective-permute-start(bf16[128,512]{1,0:T(8,128)(2,1)S(1)} %collective-permute-done.33.refs_2_), channel_id=1, source_target_pairs={{0,4},{1,5},{4,8},{5,9},{8,12},{9,13},{12,14},{13,15},{14,10},{15,... | collective-permute-start | bytes 393224 | tf_op jit(solution)/shard_map/ppermute | solution.py:174
  69.9 4.1 %gate_up.16 = (f32[128,896]{1,0:T(8,128)S(1)}, f32[128,896]{1,0:T(8,128)S(1)}, f32[128,128]{1,0:T(8,128)S(1)}, bf16[512,896]{1,0:T(8,128)(2,1)S(1)}, bf16[512,89...) custom-call(f32[2,8192]{1,0:T(2,128)S(1)} %get-tuple-element.295.ref, ...), custom_call_target="tpu_custom_call", output_to_operand_aliasing={{0}: (4, {}), {1}: (5, {}), {2}: (6, {})} | custom-call | flops 704643072 | bytes 7340032 | tf_op jit(solution)/shard_map/gate_up/pallas_call | solution.py:105
  77.4 3.2 %gate_up.17 = (f32[128,896]{1,0:T(8,128)S(1)}, f32[128,896]{1,0:T(8,128)S(1)}, f32[128,128]{1,0:T(8,128)S(1)}, bf16[896,512]{1,0:T(8,128)(2,1)S(1)}, bf16[896,51...) custom-call(f32[2,8192]{1,0:T(2,128)S(1)} %get-tuple-element.295.ref, ...), custom_call_target="tpu_custom_call", output_to_operand_aliasing={{0}: (5, {}), {1}: (6, {}), {2}: (7, {})} | custom-call | flops 939524096 | bytes 3670016 | tf_op jit(solution)/shard_map/gate_up/pallas_call | solution.py:105
  93.0 1.6 %collective-permute-start.57 = (bf16[64,512]{1,0:T(8,128)(2,1)S(1)}, bf16[64,512]{1,0:T(8,128)(2,1)S(1)}, u32[]{:S(2)}, u32[]{:S(2)}) collective-permute-start(bf16[64,512]{1,0:T(8,128)(2,1)S(1)} %get-tuple-element.586), channel_id=1, source_target_pairs={{0,4},{1,5},{4,8},{5,9},{8,12},{9,13},{12,14},{13,15},{14,10},{15,... | collective-permute-start | bytes 196616 | tf_op jit(solution)/shard_map/ppermute | solution.py:174
  94.6 2.5 %down.13 = (bf16[128,512]{1,0:T(8,128)(2,1)S(1)}, bf16[128,512]{1,0:T(8,128)(2,1)S(1)}, f32[128,512]{1,0:T(8,128)S(1)}, f32[128,512]{1,0:T(8,128)S(1)}) custom-call(bf16[128,896]{1,0:T(8,128)(2,1)S(1)} %get-tuple-element.569.refs_0_, bf16[2,896,8192]{2,1,0:T(8,128)(2,1)} %refs_1_.13), custom_call_target="tpu_custom_call" | custom-call | flops 469762048 | bytes 3670016 | tf_op jit(solution)/shard_map/down/pallas_call | solution.py:105
  100.0 2.5 %down.14 = (bf16[128,512]{1,0:T(8,128)(2,1)S(1)}, bf16[128,512]{1,0:T(8,128)(2,1)S(1)}, f32[128,512]{1,0:T(8,128)S(1)}, f32[128,512]{1,0:T(8,128)S(1)}) custom-call(bf16[128,896]{1,0:T(8,128)(2,1)S(1)} %get-tuple-element.569.refs_0_, bf16[2,896,8192]{2,1,0:T(8,128)(2,1)} %refs_1_.13), custom_call_target="tpu_custom_call" | custom-call | flops 469762048 | bytes 3670016 | tf_op jit(solution)/shard_map/down/pallas_call | solution.py:105
  106.0 1.8 %down.15 = (bf16[128,512]{1,0:T(8,128)(2,1)S(1)}, f32[128,512]{1,0:T(8,128)S(1)}) custom-call(bf16[128,896]{1,0:T(8,128)(2,1)S(1)} %get-tuple-element.569.refs_0_, bf16[2,896,8192]{2,1,0:T(8,128)(2,1)} %refs_1_.13), custom_call_target="tpu_custom_call" | custom-call | flops 234881024 | bytes 1835008 | tf_op jit(solution)/shard_map/down/pallas_call | solution.py:105
  111.6 3.4 %collective-permute-done.63 = bf16[128,512]{1,0:T(8,128)(2,1)S(1)} collective-permute-done((bf16[128,512]{1,0:T(8,128)(2,1)S(1)}, bf16[128,512]{1,0:T(8,128)(2,1)S(1)}, u32[]{:S(2)}, u32[]{:S(2)}) %collective-permute-start.63) | collective-permute-done | bytes 131104 | tf_op jit(solution)/shard_map/ppermute | solution.py:174
  (157 shorter events, 47.4 us)
Async XLA Ops:
  0.0 7.5 %collective-permute-start = (bf16[128,512]{1,0:T(8,128)(2,1)}, bf16[128,512]{1,0:T(8,128)(2,1)S(1)}, u32[]{:S(2)}, u32[]{:S(2)}) collective-permute-start(bf16[128,512]{1,0:T(8,128)(2,1)} %bitcast.3), channel_id=1, source_target_pairs={{0,4},{1,5},{4,8},{5,9},{8,12},{9,13},{12,14},{13,15},{14,10},{15,... | collective-permute-start | bytes 393224 | tf_op jit(solution)/shard_map/ppermute | solution.py:174
  3.0 6.1 %collective-permute-start.3 = (bf16[128,512]{1,0:T(8,128)(2,1)}, bf16[128,512]{1,0:T(8,128)(2,1)S(1)}, u32[]{:S(2)}, u32[]{:S(2)}) collective-permute-start(bf16[128,512]{1,0:T(8,128)(2,1)} %bitcast.5), channel_id=1, source_target_pairs={{4,0},{5,1},{8,4},{9,5},{12,8},{13,9},{14,12},{15,13},{10,14},{11,... | collective-permute-start | bytes 393224 | tf_op jit(solution)/shard_map/ppermute | solution.py:174
  9.1 6.4 %collective-permute-start.5 = (bf16[128,512]{1,0:T(8,128)(2,1)S(1)}, bf16[128,512]{1,0:T(8,128)(2,1)S(1)}, u32[]{:S(2)}, u32[]{:S(2)}) collective-permute-start(bf16[128,512]{1,0:T(8,128)(2,1)S(1)} %collective-permute-done.3.refs_3_), channel_id=1, source_target_pairs={{0,1},{1,0},{2,3},{3,2},{4,5},{5,4},{6,7},{7,6},{8,9},{9,8},{10,11... | collective-permute-start | bytes 393224 | tf_op jit(solution)/shard_map/ppermute | solution.py:174
  9.2 6.4 %collective-permute-start.2 = (bf16[128,512]{1,0:T(8,128)(2,1)S(1)}, bf16[128,512]{1,0:T(8,128)(2,1)S(1)}, u32[]{:S(2)}, u32[]{:S(2)}) collective-permute-start(bf16[128,512]{1,0:T(8,128)(2,1)S(1)} %collective-permute-done.refs_2_), channel_id=1, source_target_pairs={{0,4},{1,5},{4,8},{5,9},{8,12},{9,13},{12,14},{13,15},{14,10},{15,... | collective-permute-start | bytes 393224 | tf_op jit(solution)/shard_map/ppermute | solution.py:174
  11.0 5.7 %collective-permute-start.7 = (bf16[128,512]{1,0:T(8,128)(2,1)S(1)}, bf16[128,512]{1,0:T(8,128)(2,1)S(1)}, u32[]{:S(2)}, u32[]{:S(2)}) collective-permute-start(bf16[128,512]{1,0:T(8,128)(2,1)S(1)} %collective-permute-done.3.refs_3_), channel_id=1, source_target_pairs={{4,0},{5,1},{8,4},{9,5},{12,8},{13,9},{14,12},{15,13},{10,14},{11,... | collective-permute-start | bytes 393224 | tf_op jit(solution)/shard_map/ppermute | solution.py:174
  16.6 6.6 %collective-permute-start.9 = (bf16[128,512]{1,0:T(8,128)(2,1)S(1)}, bf16[128,512]{1,0:T(8,128)(2,1)S(1)}, u32[]{:S(2)}, u32[]{:S(2)}) collective-permute-start(bf16[128,512]{1,0:T(8,128)(2,1)S(1)} %collective-permute-done.7.refs_4_), channel_id=1, source_target_pairs={{0,1},{1,0},{2,3},{3,2},{4,5},{5,4},{6,7},{7,6},{8,9},{9,8},{10,11... | collective-permute-start | bytes 393224 | tf_op jit(solution)/shard_map/ppermute | solution.py:174
  16.6 6.6 %collective-permute-start.6 = (bf16[128,512]{1,0:T(8,128)(2,1)S(1)}, bf16[128,512]{1,0:T(8,128)(2,1)S(1)}, u32[]{:S(2)}, u32[]{:S(2)}) collective-permute-start(bf16[128,512]{1,0:T(8,128)(2,1)S(1)} %collective-permute-done.2.refs_3_), channel_id=1, source_target_pairs={{0,4},{1,5},{4,8},{5,9},{8,12},{9,13},{12,14},{13,15},{14,10},{15,... | collective-permute-start | bytes 393224 | tf_op jit(solution)/shard_map/ppermute | solution.py:174
  18.4 5.7 %collective-permute-start.11 = (bf16[128,512]{1,0:T(8,128)(2,1)S(1)}, bf16[128,512]{1,0:T(8,128)(2,1)S(1)}, u32[]{:S(2)}, u32[]{:S(2)}) collective-permute-start(bf16[128,512]{1,0:T(8,128)(2,1)S(1)} %collective-permute-done.7.refs_4_), channel_id=1, source_target_pairs={{4,0},{5,1},{8,4},{9,5},{12,8},{13,9},{14,12},{15,13},{10,14},{11,... | collective-permute-start | bytes 393224 | tf_op jit(solution)/shard_map/ppermute | solution.py:174
  24.1 6.8 %collective-permute-start.14 = (bf16[128,512]{1,0:T(8,128)(2,1)S(1)}, bf16[128,512]{1,0:T(8,128)(2,1)S(1)}, u32[]{:S(2)}, u32[]{:S(2)}) collective-permute-start(bf16[128,512]{1,0:T(8,128)(2,1)S(1)} %collective-permute-done.11.refs_4_), channel_id=1, source_target_pairs={{0,1},{1,0},{2,3},{3,2},{4,5},{5,4},{6,7},{7,6},{8,9},{9,8},{10,11... | collective-permute-start | bytes 393224 | tf_op jit(solution)/shard_map/ppermute | solution.py:174
  24.1 6.8 %collective-permute-start.13 = (bf16[128,512]{1,0:T(8,128)(2,1)S(1)}, bf16[128,512]{1,0:T(8,128)(2,1)S(1)}, u32[]{:S(2)}, u32[]{:S(2)}) collective-permute-start(bf16[128,512]{1,0:T(8,128)(2,1)S(1)} %collective-permute-done.6.refs_3_), channel_id=1, source_target_pairs={{0,1},{1,0},{2,3},{3,2},{4,5},{5,4},{6,7},{7,6},{8,9},{9,8},{10,11... | collective-permute-start | bytes 393224 | tf_op jit(solution)/shard_map/ppermute | solution.py:174
  24.7 6.2 %collective-permute-start.12 = (bf16[64,512]{1,0:T(8,128)(2,1)S(1)}, bf16[64,512]{1,0:T(8,128)(2,1)S(1)}, u32[]{:S(2)}, u32[]{:S(2)}) collective-permute-start(bf16[64,512]{1,0:T(8,128)(2,1)S(1)} %slice.25), channel_id=1, source_target_pairs={{4,0},{5,1},{8,4},{9,5},{12,8},{13,9},{14,12},{15,13},{10,14},{11,... | collective-permute-start | bytes 196616 | tf_op jit(solution)/shard_map/ppermute | solution.py:174
  25.2 5.7 %collective-permute-start.10 = (bf16[64,512]{1,0:T(8,128)(2,1)S(1)}, bf16[64,512]{1,0:T(8,128)(2,1)S(1)}, u32[]{:S(2)}, u32[]{:S(2)}) collective-permute-start(bf16[64,512]{1,0:T(8,128)(2,1)S(1)} %slice.24), channel_id=1, source_target_pairs={{0,4},{1,5},{4,8},{5,9},{8,12},{9,13},{12,14},{13,15},{14,10},{15,... | collective-permute-start | bytes 196616 | tf_op jit(solution)/shard_map/ppermute | solution.py:174
  42.1 5.9 %collective-permute-start.21 = (bf16[128,512]{1,0:T(8,128)(2,1)S(1)}, bf16[128,512]{1,0:T(8,128)(2,1)S(1)}, u32[]{:S(2)}, u32[]{:S(2)}) collective-permute-start(bf16[128,512]{1,0:T(8,128)(2,1)S(1)} %add_convert_fusion.14), channel_id=1, source_target_pairs={{4,0},{5,1},{8,4},{9,5},{12,8},{13,9},{14,12},{15,13},{10,14},{11,... | collective-permute-start | bytes 393224 | tf_op jit(solution)/shard_map/ppermute | solution.py:174
  48.1 6.2 %collective-permute-start.25 = (bf16[128,512]{1,0:T(8,128)(2,1)S(1)}, bf16[128,512]{1,0:T(8,128)(2,1)S(1)}, u32[]{:S(2)}, u32[]{:S(2)}) collective-permute-start(bf16[128,512]{1,0:T(8,128)(2,1)S(1)} %add_convert_fusion.12), channel_id=1, source_target_pairs={{4,0},{5,1},{8,4},{9,5},{12,8},{13,9},{14,12},{15,13},{10,14},{11,... | collective-permute-start | bytes 393224 | tf_op jit(solution)/shard_map/ppermute | solution.py:174
  48.6 5.7 %collective-permute-start.26 = (bf16[128,512]{1,0:T(8,128)(2,1)S(1)}, bf16[128,512]{1,0:T(8,128)(2,1)S(1)}, u32[]{:S(2)}, u32[]{:S(2)}) collective-permute-start(bf16[128,512]{1,0:T(8,128)(2,1)S(1)} %get-tuple-element.416), channel_id=1, source_target_pairs={{0,1},{1,0},{2,3},{3,2},{4,5},{5,4},{6,7},{7,6},{8,9},{9,8},{10,11... | collective-permute-start | bytes 393224 | tf_op jit(solution)/shard_map/ppermute | solution.py:174
  48.6 5.7 %collective-permute-start.27 = (bf16[128,512]{1,0:T(8,128)(2,1)S(1)}, bf16[128,512]{1,0:T(8,128)(2,1)S(1)}, u32[]{:S(2)}, u32[]{:S(2)}) collective-permute-start(bf16[128,512]{1,0:T(8,128)(2,1)S(1)} %get-tuple-element.417), channel_id=1, source_target_pairs={{0,1},{1,0},{2,3},{3,2},{4,5},{5,4},{6,7},{7,6},{8,9},{9,8},{10,11... | collective-permute-start | bytes 393224 | tf_op jit(solution)/shard_map/ppermute | solution.py:174
  49.2 5.8 %collective-permute-start.29 = (bf16[128,512]{1,0:T(8,128)(2,1)S(1)}, bf16[128,512]{1,0:T(8,128)(2,1)S(1)}, u32[]{:S(2)}, u32[]{:S(2)}) collective-permute-start(bf16[128,512]{1,0:T(8,128)(2,1)S(1)} %add_convert_fusion.11), channel_id=1, source_target_pairs={{0,4},{1,5},{4,8},{5,9},{8,12},{9,13},{12,14},{13,15},{14,10},{15,... | collective-permute-start | bytes 393224 | tf_op jit(solution)/shard_map/ppermute | solution.py:174
  60.1 5.7 %collective-permute-start.33 = (bf16[128,512]{1,0:T(8,128)(2,1)S(1)}, bf16[128,512]{1,0:T(8,128)(2,1)S(1)}, u32[]{:S(2)}, u32[]{:S(2)}) collective-permute-start(bf16[128,512]{1,0:T(8,128)(2,1)S(1)} %add_convert_fusion.8.refs_1_), channel_id=1, source_target_pairs={{0,4},{1,5},{4,8},{5,9},{8,12},{9,13},{12,14},{13,15},{14,10},{15,... | collective-permute-start | bytes 393224 | tf_op jit(solution)/shard_map/ppermute | solution.py:174
  61.8 5.9 %collective-permute-start.36 = (bf16[128,512]{1,0:T(8,128)(2,1)S(1)}, bf16[128,512]{1,0:T(8,128)(2,1)S(1)}, u32[]{:S(2)}, u32[]{:S(2)}) collective-permute-start(bf16[128,512]{1,0:T(8,128)(2,1)S(1)} %add_convert_fusion.8.refs_1_), channel_id=1, source_target_pairs={{4,0},{5,1},{8,4},{9,5},{12,8},{13,9},{14,12},{15,13},{10,14},{11,... | collective-permute-start | bytes 393224 | tf_op jit(solution)/shard_map/ppermute | solution.py:174
  67.6 6.4 %collective-permute-start.38 = (bf16[128,512]{1,0:T(8,128)(2,1)S(1)}, bf16[128,512]{1,0:T(8,128)(2,1)S(1)}, u32[]{:S(2)}, u32[]{:S(2)}) collective-permute-start(bf16[128,512]{1,0:T(8,128)(2,1)S(1)} %collective-permute-done.36.refs_3_), channel_id=1, source_target_pairs={{0,1},{1,0},{2,3},{3,2},{4,5},{5,4},{6,7},{7,6},{8,9},{9,8},{10,11... | collective-permute-start | bytes 393224 | tf_op jit(solution)/shard_map/ppermute | solution.py:174
  67.6 6.4 %collective-permute-start.35 = (bf16[128,512]{1,0:T(8,128)(2,1)S(1)}, bf16[128,512]{1,0:T(8,128)(2,1)S(1)}, u32[]{:S(2)}, u32[]{:S(2)}) collective-permute-start(bf16[128,512]{1,0:T(8,128)(2,1)S(1)} %collective-permute-done.33.refs_2_), channel_id=1, source_target_pairs={{0,4},{1,5},{4,8},{5,9},{8,12},{9,13},{12,14},{13,15},{14,10},{15,... | collective-permute-start | bytes 393224 | tf_op jit(solution)/shard_map/ppermute | solution.py:174
  69.5 5.7 %collective-permute-start.40 = (bf16[128,512]{1,0:T(8,128)(2,1)S(1)}, bf16[128,512]{1,0:T(8,128)(2,1)S(1)}, u32[]{:S(2)}, u32[]{:S(2)}) collective-permute-start(bf16[128,512]{1,0:T(8,128)(2,1)S(1)} %collective-permute-done.36.refs_3_), channel_id=1, source_target_pairs={{4,0},{5,1},{8,4},{9,5},{12,8},{13,9},{14,12},{15,13},{10,14},{11,... | collective-permute-start | bytes 393224 | tf_op jit(solution)/shard_map/ppermute | solution.py:174
  75.1 5.9 %collective-permute-start.39 = (bf16[128,512]{1,0:T(8,128)(2,1)S(1)}, bf16[128,512]{1,0:T(8,128)(2,1)S(1)}, u32[]{:S(2)}, u32[]{:S(2)}) collective-permute-start(bf16[128,512]{1,0:T(8,128)(2,1)S(1)} %collective-permute-done.35.refs_3_), channel_id=1, source_target_pairs={{0,4},{1,5},{4,8},{5,9},{8,12},{9,13},{12,14},{13,15},{14,10},{15,... | collective-permute-start | bytes 393224 | tf_op jit(solution)/shard_map/ppermute | solution.py:174
  108.0 7.0 %collective-permute-start.64 = (bf16[128,512]{1,0:T(8,128)(2,1)S(1)}, bf16[128,512]{1,0:T(8,128)(2,1)S(1)}, u32[]{:S(2)}, u32[]{:S(2)}) collective-permute-start(bf16[128,512]{1,0:T(8,128)(2,1)S(1)} %add_convert_fusion.2), channel_id=1, source_target_pairs={{4,0},{5,1},{8,4},{9,5},{12,8},{13,9},{14,12},{15,13},{10,14},{11,... | collective-permute-start | bytes 393224 | tf_op jit(solution)/shard_map/ppermute | solution.py:174
  (43 other events, 192.3 us)

commit v3 on v2

--- a/solution.py
+++ b/solution.py
@@ -12,11 +12,10 @@
 VMEM = pl.BlockSpec(memory_space=pltpu.VMEM)
 HBM = pl.BlockSpec(memory_space=pl.ANY)
 LIMIT = 20 * 1024 * 1024
-DIRECT = ()
 AHEAD = {
-    (0, "gather1"): 4, (0, "gather2"): 4, (0, "gather3"): 4, (0, "gather4"): 4, (0, "gathered"): 2,
-    (0, "scatter2"): 2, (0, "scatter1"): 4, (0, "scatter0"): 4,
-    (1, "gather1"): 4, (1, "gather2"): 4, (1, "gather3"): 2,
+    (0, "gather1"): 4, (0, "gather2"): 4, (0, "gather3"): 4, (0, "gather4"): 3, (0, "gathered"): 0, (0, "last"): 3,
+    (0, "scatter2"): 2, (0, "scatter1"): 4, (0, "scatter0"): 7,
+    (1, "gather1"): 3, (1, "gather2"): 1, (1, "gather3"): 1, (1, "gather4"): 2,
 }
 
 
@@ -124,45 +123,36 @@
     return results
 
 
-def multiply(layer, chips, work, pieces, block, named, out):
+def multiply(layer, chips, shards, block, named, out):
+    def add(name, value, e):
+        if e:
+            out[name][...] += value
+        elif ("old", name) in named:
+            out[name][...] = named["old", name][...] + value
+        else:
+            out[name][...] = value
+
     ys = {}
-    for shard in [shard for shard in pieces if any(shard in shards for shards in work.values())]:
-        parts = [named["x", shard, i][...] for i in range(pieces[shard])]
-        x = (parts[0] if len(parts) == 1 else jnp.concatenate(parts, 0)).astype(jnp.float32)
-        if shard in work["gate"]:
-            square = x * x
-            q = square[:, :128]
-            for lane in range(128, x.shape[1], 128):
-                q = q + square[:, lane : lane + 128]
-            if shard != work["gate"][0]:
-                out["squares"][...] += q
-            elif ("old", "squares") in named:
-                out["squares"][...] = named["old", "squares"][...] + q
-            else:
-                out["squares"][...] = q
-        ys[shard] = (x * named["gain"][layer : layer + 1, pl.ds(pl.multiple_of(shard_at(*shard, chips) * x.shape[1], x.shape[1]), x.shape[1])]).astype(jnp.bfloat16)
+    for e, shard in enumerate(shards):
+        x = named["x", shard][...].astype(jnp.float32)
+        size = x.shape[1]
+        square = x * x
+        add("squares", sum(square[:, lane : lane + 128] for lane in range(0, size, 128)), e)
+        span = pl.ds(pl.multiple_of(shard_at(*shard, chips) * size, size), size)
+        ys[shard] = (x * named["gain"][layer : layer + 1, span]).astype(jnp.bfloat16)
     for name, kind in (("up", "u"), ("gate", "g")):
-        for e, shard in enumerate(work[name]):
-            value = jnp.dot(ys[shard], block((kind, layer, *shard)), preferred_element_type=jnp.float32)
-            if e:
-                out[name][...] += value
-            elif ("old", name) in named:
-                out[name][...] = named["old", name][...] + value
-            else:
-                out[name][...] = value
+        for e, shard in enumerate(shards):
+            add(name, jnp.dot(ys[shard], block((kind, layer, *shard)), preferred_element_type=jnp.float32), e)
 
 
 def ring_body(chips, stream_in, norm_gain, w_gate, w_up, w_down):
     micro, seqs, cols = stream_in.shape
     rows = micro * seqs
-    part = rows // 2
     layers, features, hid = w_gate.shape
     far = chips // 2
     ring = [chip_at(place, chips) for place in range(chips)]
     right = [(2 * ring[i] + c, 2 * ring[(i + 1) % chips] + c) for i in range(chips) for c in range(2)]
     left = [(b, a) for a, b in right]
-    right2 = [(2 * ring[i] + c, 2 * ring[(i + 2) % chips] + c) for i in range(chips) for c in range(2)]
-    left2 = [(b, a) for a, b in right2]
     swap = [(i, i ^ 1) for i in range(2 * chips)]
     f32, bf16 = jnp.float32, jnp.bfloat16
     weights = {"g": w_gate, "u": w_up, "d": w_down}
@@ -194,26 +184,16 @@
         "squares": jax.ShapeDtypeStruct((rows, 128), f32),
     }
 
-    def direct(layer):
-        return far == 4 and layer in DIRECT
-
     def both(offset):
         return [offset, -offset] if offset > 0 else [0] if offset == 0 else []
 
-    def stages(layer):
-        if direct(layer):
-            return [
-                [(0, False)], [(0, True), (-1, False), (1, False), (-2, False), (2, False)],
-                [(-1, True), (1, True), (-2, True), (2, True), (-3, False), (3, False), (4, False)],
-                [(-3, True), (3, True), (4, True)],
-            ]
-        shards = [[(0, False)], [(0, True), (-1, False), (1, False)]]
-        shards += [[(1 - s, True), (s - 1, True), (-s, False), (s, False)] for s in range(2, far)]
-        return shards + [[(1 - far, True), (far - 1, True), (far, False)], [(far, True)]]
+    stages = [[(0, False)], [(0, True), (-1, False), (1, False)]]
+    stages += [[(1 - s, True), (s - 1, True), (-s, False), (s, False)] for s in range(2, far)]
+    stages += [[(1 - far, True)], [(far - 1, True), (far, False)], [(far, True)]]
 
     units = []
     for layer in range(layers):
-        units += [[("g", layer, *shard), ("u", layer, *shard)] for shards in stages(layer) for shard in shards]
+        units += [[("g", layer, *shard), ("u", layer, *shard)] for shards in stages for shard in shards]
         units += [[("d", layer, o, True), ("d", layer, o, False)] for step in range(far, -1, -1) for o in
                   ([far] if step == far else both(step))]
     weights["units"] = units
@@ -221,22 +201,21 @@
     def ahead(layer, name):
         return AHEAD.get((layer, name), 0)
 
-    def shards_in(layer, xs, work, acc):
+    def shards_in(layer, xs, acc):
         ins = {"gain": kept["gain"]} if kept else {}
-        ins.update({("x", shard, i): x for shard, arrays in xs.items() for i, x in enumerate(arrays) if kept})
+        ins.update({("x", shard): x for shard, x in xs.items() if kept})
         ins.update({("old", name): value for name, value in acc.items()})
-        keys = [(kind, layer, *s) for name, kind in (("up", "u"), ("gate", "g")) for s in work[name]]
-        return ins, keys, {shard: len(arrays) for shard, arrays in xs.items()}
+        keys = [(kind, layer, *shard) for kind in "ug" for shard in xs]
+        return ins, keys
 
     def gate_up(layer, xs, acc, fetch):
-        work = {"gate": list(xs), "up": list(xs)}
-        ins, keys, pieces = shards_in(layer, xs, work, acc)
-        outs = {name: s for name, s in sums.items() if name in acc or work.get(name, work["gate"])}
+        ins, keys = shards_in(layer, xs, acc)
+        outs = sums
 
         def job(block, named, out, scratch):
-            multiply(layer, chips, work, pieces, block, named, out)
-
-        raw = {} if kept else {"gain": norm_gain, ("x", (0, False), 0): stream}
+            multiply(layer, chips, list(xs), block, named, out)
+
+        raw = {} if kept else {"gain": norm_gain, ("x", (0, False)): stream}
         out = stage(
             chips, weights, blocks, job, keys, ins, outs, {("old", name): name for name in acc}, [], fetch,
             len(keys) * flops, "gate_up", raw,
@@ -246,12 +225,11 @@
         return out
 
     def finish(layer, xs, acc, fetch):
-        work = {"gate": list(xs), "up": list(xs)}
-        ins, keys, pieces = shards_in(layer, xs, work, acc)
+        ins, keys = shards_in(layer, xs, acc)
 
         def job(block, named, out, scratch):
             into = dict(zip(sums, scratch))
-            multiply(layer, chips, work, pieces, block, named, into)
+            multiply(layer, chips, list(xs), block, named, into)
             meansq = jnp.sum(into["squares"][...], axis=1, keepdims=True) / features
             scale = lax.rsqrt(meansq + EPS)
             g = into["gate"][...] * scale
@@ -289,48 +267,30 @@
 
     stream = stream_in.reshape(rows, cols)
     for layer in range(layers):
+        r = l = stream
         acc = {}
-        held = {(0, False): (stream,)}
-        crossing = {(0, True): (stream,)}
-        if direct(layer):
-            moved = {
-                (-2, False): (send(stream, right2),), (2, False): (send(stream, left2),),
-                (-1, False): (send(stream, right),), (1, False): (send(stream, left),),
-            }
-            crossed = {shard: tuple(send(x, swap) for x in xs) for shard, xs in crossing.items()}
-            acc = gate_up(layer, held, acc, ahead(layer, "gather1"))
-            acc, moved, crossed = fence(acc, moved, crossed)
-            held = {**crossed, **moved}
-            (r,), (l,) = moved[-2, False], moved[2, False]
-            crossing = {(o, True): xs for (o, _), xs in moved.items()}
-            moved = {
-                (-3, False): (send(r, right),), (3, False): (send(l, left),),
-                (4, False): (send(r[:part], right2), send(l[part:], left2)),
-            }
-            crossed = {shard: tuple(send(x, swap) for x in xs) for shard, xs in crossing.items()}
-            acc = gate_up(layer, held, acc, ahead(layer, "gather2"))
-            acc, moved, crossed = fence(acc, moved, crossed)
-            held = {**crossed, **moved}
-            crossing = {(o, True): xs for (o, _), xs in moved.items()}
-        else:
-            r = l = stream
-            for step in range(1, far + 1):
-                if step > 1:
-                    r, acc, held = fence(r, acc, held)
-                    l, held = fence(l, held)
-                    crossing = {(1 - step, True): (r,), (step - 1, True): (l,)}
-                    held = {**held, (1 - step, False): (r,), (step - 1, False): (l,)}
-                if step == far:
-                    r, l = r[:part], l[part:]
-                r, l = send(r, right), send(l, left)
-                crossed = {shard: tuple(send(x, swap) for x in xs) for shard, xs in crossing.items()}
-                acc = gate_up(layer, held, acc, ahead(layer, "gather%d" % step))
-                held = crossed
-            r, l, acc, held = fence(r, l, acc, held)
-            held = {**held, (far, False): (r, l)}
-            crossing = {(far, True): (r, l)}
-        crossed = {shard: tuple(send(x, swap) for x in xs) for shard, xs in crossing.items()}
-        acc = gate_up(layer, held, acc, ahead(layer, "gathered"))
+        held = {(0, False): stream}
+        crossed = {(0, True): send(stream, swap)}
+        for step in range(1, far + 1):
+            r = send(r, right)
+            if step < far:
+                l = send(l, left)
+            acc = gate_up(layer, held, acc, ahead(layer, "gather%d" % step))
+            if step == far:
+                l, acc, crossed = fence(l, acc, crossed)
+                late = send(l, swap)
+                acc = gate_up(layer, {(far - 1, False): l, **crossed}, acc, ahead(layer, "gathered"))
+                r, late, acc = fence(r, late, acc)
+                break
+            r, acc = fence(r, acc)
+            held = {**crossed, (-step, False): r}
+            crossed = {(-step, True): send(r, swap)}
+            if step + 1 < far:
+                l, held = fence(l, held)
+                held[step, False] = l
+                crossed[step, True] = send(l, swap)
+        crossed = {(far, True): send(r, swap)}
+        acc = gate_up(layer, {(far - 1, True): late, (far, False): r}, acc, ahead(layer, "last"))
         acc, crossed = fence(acc, crossed)
         found = finish(layer, crossed, acc, ahead(layer, "hidden"))
         hidden, found = fence(found.pop("hidden"), found)
@@ -340,7 +300,7 @@
         c, found = fence(c, found)
         total = (own + c.astype(f32)).astype(bf16)
         hidden, total = fence(hidden, total)
-        r, l = total[:part], total[part:]
+        r, l = total[: rows // 2], total[rows // 2 :]
         for step in range(far - 1, -1, -1):
             r, l = send(r, right), send(l, left)
             if not step:
@@ -351,12 +311,13 @@
             c = [send(found["sib", o], swap) for o in both(step)]
             own = [found["own", o] for o in both(step)]
             found = down(layer, both(step - 1), hidden, ahead(layer, "scatter%d" % step))
+            l, c, found = fence(l, c, found)
             if step == far - 1:
-                hole = jnp.zeros((part, cols), bf16)
-                r, l = jnp.concatenate([r, hole], 0), jnp.concatenate([hole, l], 0)
-            l, c, found = fence(l, c, found)
+                l = jnp.concatenate([jnp.zeros_like(l), l], 0)
             l = fence((own[1] + c[1].astype(f32) + l.astype(f32)).astype(bf16))
             r, _ = fence(r, l)
+            if step == far - 1:
+                r = jnp.concatenate([r, jnp.zeros_like(r)], 0)
             r = (own[0] + c[0].astype(f32) + r.astype(f32)).astype(bf16)
             hidden, r = fence(hidden, r)
             if step == 1:
@@ -390,7 +351,7 @@
 
     def body(stream_in, *rest):
         cols = stream_in.shape[2]
-        if devices % 8 == 0 and cols % 128 == 0:
+        if devices >= 16 and devices % 4 == 0 and cols % 128 == 0:
             return ring_body(devices // 2, stream_in, *rest)
         return plain_body(stream_in, *rest)
 

time: 116 us -> 109 us (0.940)
  waiting for transfers between devices: 17.3 us -> 9.9 us
  Pallas kernels: 55.5 us -> 57.2 us
    ppermute x66 -> x62, waiting for transfers between devices: 17.3 us -> 9.9 us  [send(): return lax.ppermute(x, AXIS, perm)]
    pallas_call x21 -> x23, Pallas kernels: 55.5 us -> 57.2 us  [stage(): pl.pallas_call(functools.partial(stage_kernel, chips, job, list(raw), str...]
    ppermute x66 -> x62, starting transfers between devices: 40.8 us -> 40.1 us  [send(): return lax.ppermute(x, AXIS, perm)]
  transfers between devices with their start and end apart: 66 -> 62, of which waited for: 18 -> 13; matrix products, arithmetic and copies ran while one was open for 0% -> 0% of each run, Pallas kernels for 46% -> 51%
where the time goes in v3:
time: 109 us
  Pallas kernels  57.2 us (52%)
  starting transfers between devices  40.1 us (37%)
  waiting for transfers between devices  9.9 us (9%)
  other arithmetic  1.39 us (1%)
    pallas_call x23, Pallas kernels, stage(): pl.pallas_call(functools.partial(stage_kernel, chips, job, list(raw), str...  57.2 us
    ppermute x62, starting transfers between devices, send(): return lax.ppermute(x, AXIS, perm)  40.1 us
    ppermute x62, waiting for transfers between devices, send(): return lax.ppermute(x, AXIS, perm)  9.9 us
  transfers between devices with their start and end apart: 62, of which 13 were waited for; matrix products, arithmetic and copies ran while one was open for 0% of the time, Pallas kernels for 51%

profile of v3, /device:TPU:0, one launch (start us, length us, event | category | flops | bytes accessed | tf_op | source)
XLA Modules:
  0.0 109.2 jit_solution(13144653832830807701)
XLA Ops:
  0.0 3.0 %collective-permute-start = (bf16[128,512]{1,0:T(8,128)(2,1)}, bf16[128,512]{1,0:T(8,128)(2,1)S(1)}, u32[]{:S(2)}, u32[]{:S(2)}) collective-permute-start(bf16[128,512]{1,0:T(8,128)(2,1)} %bitcast.3), channel_id=1, source_target_pairs={{0,4},{1,5},{4,8},{5,9},{8,12},{9,13},{12,14},{13,15},{14,10},{15,... | collective-permute-start | bytes 393224 | tf_op jit(solution)/shard_map/ppermute | solution.py:164
  3.0 4.5 %gate_up.12 = (f32[128,896]{1,0:T(8,128)S(1)}, f32[128,896]{1,0:T(8,128)S(1)}, f32[128,128]{1,0:T(8,128)S(1)}, f32[2,8192]{1,0:T(2,128)S(1)}, bf16[128,512]{1,0:...) custom-call(bf16[2,8192,896]{2,1,0:T(8,128)(2,1)} %refs_13_.6, ...), custom_call_target="tpu_custom_call" | custom-call | flops 234881024 | bytes 9175040 | tf_op jit(solution)/shard_map/gate_up/pallas_call | solution.py:104
  7.5 2.1 %collective-permute-start.1 = (bf16[128,512]{1,0:T(8,128)(2,1)S(1)}, bf16[128,512]{1,0:T(8,128)(2,1)S(1)}, u32[]{:S(2)}, u32[]{:S(2)}) collective-permute-start(bf16[128,512]{1,0:T(8,128)(2,1)S(1)} %collective-permute-done.refs_2_), channel_id=1, source_target_pairs={{0,4},{1,5},{4,8},{5,9},{8,12},{9,13},{12,14},{13,15},{14,10},{15,... | collective-permute-start | bytes 393224 | tf_op jit(solution)/shard_map/ppermute | solution.py:164
  10.2 4.1 %gate_up.13 = (f32[128,896]{1,0:T(8,128)S(1)}, f32[128,896]{1,0:T(8,128)S(1)}, f32[128,128]{1,0:T(8,128)S(1)}, bf16[512,896]{1,0:T(8,128)(2,1)S(1)}, bf16[512,89...) custom-call(f32[2,8192]{1,0:T(2,128)S(1)} %get-tuple-element.293.ref, ...), custom_call_target="tpu_custom_call", output_to_operand_aliasing={{0}: (4, {}), {1}: (5, {}), {2}: (6, {})} | custom-call | flops 704643072 | bytes 7340032 | tf_op jit(solution)/shard_map/gate_up/pallas_call | solution.py:104
  14.3 1.7 %collective-permute-start.4 = (bf16[128,512]{1,0:T(8,128)(2,1)S(1)}, bf16[128,512]{1,0:T(8,128)(2,1)S(1)}, u32[]{:S(2)}, u32[]{:S(2)}) collective-permute-start(bf16[128,512]{1,0:T(8,128)(2,1)S(1)} %collective-permute-done.1.refs_3_), channel_id=1, source_target_pairs={{0,4},{1,5},{4,8},{5,9},{8,12},{9,13},{12,14},{13,15},{14,10},{15,... | collective-permute-start | bytes 393224 | tf_op jit(solution)/shard_map/ppermute | solution.py:164
  16.7 4.3 %gate_up.14 = (f32[128,896]{1,0:T(8,128)S(1)}, f32[128,896]{1,0:T(8,128)S(1)}, f32[128,128]{1,0:T(8,128)S(1)}, bf16[512,896]{1,0:T(8,128)(2,1)S(1)}, bf16[512,89...) custom-call(f32[2,8192]{1,0:T(2,128)S(1)} %get-tuple-element.293.ref, ...), custom_call_target="tpu_custom_call", output_to_operand_aliasing={{0}: (5, {}), {1}: (6, {}), {2}: (7, {})} | custom-call | flops 939524096 | bytes 7340032 | tf_op jit(solution)/shard_map/gate_up/pallas_call | solution.py:104
  21.5 1.7 %collective-permute-start.8 = (bf16[128,512]{1,0:T(8,128)(2,1)S(1)}, bf16[128,512]{1,0:T(8,128)(2,1)S(1)}, u32[]{:S(2)}, u32[]{:S(2)}) collective-permute-start(bf16[128,512]{1,0:T(8,128)(2,1)S(1)} %collective-permute-done.4.refs_3_), channel_id=1, source_target_pairs={{0,4},{1,5},{4,8},{5,9},{8,12},{9,13},{12,14},{13,15},{14,10},{15,... | collective-permute-start | bytes 393224 | tf_op jit(solution)/shard_map/ppermute | solution.py:164
  23.3 3.6 %gate_up.15 = (f32[128,896]{1,0:T(8,128)S(1)}, f32[128,896]{1,0:T(8,128)S(1)}, f32[128,128]{1,0:T(8,128)S(1)}, bf16[512,896]{1,0:T(8,128)(2,1)S(1)}, bf16[512,89...) custom-call(f32[2,8192]{1,0:T(2,128)S(1)} %get-tuple-element.293.ref, ...), custom_call_target="tpu_custom_call", output_to_operand_aliasing={{0}: (4, {}), {1}: (5, {}), {2}: (6, {})} | custom-call | flops 704643072 | bytes 5505024 | tf_op jit(solution)/shard_map/gate_up/pallas_call | solution.py:104
  28.4 3.3 %gate_up.17 = (f32[128,896]{1,0:T(8,128)S(1)}, f32[128,896]{1,0:T(8,128)S(1)}, f32[128,128]{1,0:T(8,128)S(1)}, bf16[896,512]{1,0:T(8,128)(2,1)S(1)}, bf16[896,51...) custom-call(f32[2,8192]{1,0:T(2,128)S(1)} %get-tuple-element.293.ref, ...), custom_call_target="tpu_custom_call", output_to_operand_aliasing={{0}: (3, {}), {1}: (4, {}), {2}: (5, {})} | custom-call | flops 469762048 | bytes 5505024 | tf_op jit(solution)/shard_map/gate_up/pallas_call | solution.py:104
  36.7 2.5 %down.9 = (bf16[128,512]{1,0:T(8,128)(2,1)S(1)}, bf16[128,512]{1,0:T(8,128)(2,1)S(1)}, f32[128,512]{1,0:T(8,128)S(1)}, f32[128,512]{1,0:T(8,128)S(1)}) custom-call(bf16[128,896]{1,0:T(8,128)(2,1)S(1)} %get-tuple-element.444.refs_0_, bf16[2,896,8192]{2,1,0:T(8,128)(2,1)} %refs_1_.13), custom_call_target="tpu_custom_call" | custom-call | flops 469762048 | bytes 3670016 | tf_op jit(solution)/shard_map/down/pallas_call | solution.py:104
  40.3 1.7 %collective-permute-start.26 = (bf16[128,512]{1,0:T(8,128)(2,1)S(1)}, bf16[128,512]{1,0:T(8,128)(2,1)S(1)}, u32[]{:S(2)}, u32[]{:S(2)}) collective-permute-start(bf16[128,512]{1,0:T(8,128)(2,1)S(1)} %add_convert_fusion.13), channel_id=1, source_target_pairs={{0,4},{1,5},{4,8},{5,9},{8,12},{9,13},{12,14},{13,15},{14,10},{15,... | collective-permute-start | bytes 393224 | tf_op jit(solution)/shard_map/ppermute | solution.py:164
  42.0 3.2 %down.10 = (bf16[128,512]{1,0:T(8,128)(2,1)S(1)}, bf16[128,512]{1,0:T(8,128)(2,1)S(1)}, f32[128,512]{1,0:T(8,128)S(1)}, f32[128,512]{1,0:T(8,128)S(1)}, bf16[896...) custom-call(bf16[128,896]{1,0:T(8,128)(2,1)S(1)} %get-tuple-element., ...), custom_call_target="tpu_custom_call" | custom-call | flops 469762048 | bytes 7340032 | tf_op jit(solution)/shard_map/down/pallas_call | solution.py:104
  46.3 1.7 %collective-permute-start.27 = (bf16[128,512]{1,0:T(8,128)(2,1)S(1)}, bf16[128,512]{1,0:T(8,128)(2,1)S(1)}, u32[]{:S(2)}, u32[]{:S(2)}) collective-permute-start(bf16[128,512]{1,0:T(8,128)(2,1)S(1)} %add_convert_fusion.11), channel_id=1, source_target_pairs={{0,4},{1,5},{4,8},{5,9},{8,12},{9,13},{12,14},{13,15},{14,10},{15,... | collective-permute-start | bytes 393224 | tf_op jit(solution)/shard_map/ppermute | solution.py:164
  48.0 3.5 %down.11 = (bf16[128,512]{1,0:T(8,128)(2,1)S(1)}, f32[128,512]{1,0:T(8,128)S(1)}, bf16[512,896]{1,0:T(8,128)(2,1)S(1)}, bf16[512,896]{1,0:T(8,128)(2,1)S(1)}, bf...) custom-call(bf16[128,896]{1,0:T(8,128)(2,1)S(1)} %get-tuple-element., ...), custom_call_target="tpu_custom_call" | custom-call | flops 234881024 | bytes 7340032 | tf_op jit(solution)/shard_map/down/pallas_call | solution.py:104
  53.8 4.8 %ahead.1 = (bf16[512,896]{1,0:T(8,128)(2,1)S(1)}, bf16[512,896]{1,0:T(8,128)(2,1)S(1)}, bf16[512,896]{1,0:T(8,128)(2,1)S(1)}, bf16[512,896]{1,0:T(8,128)(2,1)S(1...) custom-call(bf16[128,896]{1,0:T(8,128)(2,1)S(1)} %get-tuple-element., ...), custom_call_target="tpu_custom_call" | custom-call | bytes 12845056 | tf_op jit(solution)/shard_map/ahead/pallas_call | solution.py:104
  58.7 1.7 %collective-permute-start.31 = (bf16[128,512]{1,0:T(8,128)(2,1)S(1)}, bf16[128,512]{1,0:T(8,128)(2,1)S(1)}, u32[]{:S(2)}, u32[]{:S(2)}) collective-permute-start(bf16[128,512]{1,0:T(8,128)(2,1)S(1)} %add_convert_fusion.8.refs_1_), channel_id=1, source_target_pairs={{0,4},{1,5},{4,8},{5,9},{8,12},{9,13},{12,14},{13,15},{14,10},{15,... | collective-permute-start | bytes 393224 | tf_op jit(solution)/shard_map/ppermute | solution.py:164
  61.0 2.9 %gate_up.18 = (f32[128,896]{1,0:T(8,128)S(1)}, f32[128,896]{1,0:T(8,128)S(1)}, f32[128,128]{1,0:T(8,128)S(1)}, bf16[512,896]{1,0:T(8,128)(2,1)S(1)}, bf16[512,89...) custom-call(f32[2,8192]{1,0:T(2,128)S(1)} %get-tuple-element.293.ref, ...), custom_call_target="tpu_custom_call" | custom-call | flops 234881024 | bytes 5505024 | tf_op jit(solution)/shard_map/gate_up/pallas_call | solution.py:104
  67.0 2.4 %gate_up.19 = (f32[128,896]{1,0:T(8,128)S(1)}, f32[128,896]{1,0:T(8,128)S(1)}, f32[128,128]{1,0:T(8,128)S(1)}, bf16[512,896]{1,0:T(8,128)(2,1)S(1)}, bf16[512,896]{1,0:T(8,128)(2,1)S(1)}) custom-call(f32[2,8192]{1,0:T(2,128)S(1)} %get-tuple-element.293.refs_0_, ...), custom_call_target="tpu_custom_call", output_to_operand_aliasing={{0}: (4, {}), {1}: (5, {}), {2}: (6, {})} | custom-call | flops 704643072 | bytes 1835008 | tf_op jit(solution)/shard_map/gate_up/pallas_call | solution.py:104
  72.9 2.7 %gate_up.20 = (f32[128,896]{1,0:T(8,128)S(1)}, f32[128,896]{1,0:T(8,128)S(1)}, f32[128,128]{1,0:T(8,128)S(1)}, bf16[896,512]{1,0:T(8,128)(2,1)S(1)}, bf16[896,512]{1,0:T(8,128)(2,1)S(1)}) custom-call(f32[2,8192]{1,0:T(2,128)S(1)} %get-tuple-element.293.refs_0_, ...), custom_call_target="tpu_custom_call", output_to_operand_aliasing={{0}: (5, {}), {1}: (6, {}), {2}: (7, {})} | custom-call | flops 939524096 | bytes 1835008 | tf_op jit(solution)/shard_map/gate_up/pallas_call | solution.py:104
  77.6 3.0 %gate_up.21 = (f32[128,896]{1,0:T(8,128)S(1)}, f32[128,896]{1,0:T(8,128)S(1)}, f32[128,128]{1,0:T(8,128)S(1)}, bf16[896,512]{1,0:T(8,128)(2,1)S(1)}, bf16[896,51...) custom-call(f32[2,8192]{1,0:T(2,128)S(1)} %get-tuple-element.293.ref, ...), custom_call_target="tpu_custom_call", output_to_operand_aliasing={{0}: (4, {}), {1}: (5, {}), {2}: (6, {})} | custom-call | flops 704643072 | bytes 3670016 | tf_op jit(solution)/shard_map/gate_up/pallas_call | solution.py:104
  88.3 2.5 %down.13 = (bf16[128,512]{1,0:T(8,128)(2,1)S(1)}, bf16[128,512]{1,0:T(8,128)(2,1)S(1)}, f32[128,512]{1,0:T(8,128)S(1)}, f32[128,512]{1,0:T(8,128)S(1)}) custom-call(bf16[128,896]{1,0:T(8,128)(2,1)S(1)} %get-tuple-element.565.refs_0_, bf16[2,896,8192]{2,1,0:T(8,128)(2,1)} %refs_1_.13), custom_call_target="tpu_custom_call" | custom-call | flops 469762048 | bytes 3670016 | tf_op jit(solution)/shard_map/down/pallas_call | solution.py:104
  93.6 2.5 %down.14 = (bf16[128,512]{1,0:T(8,128)(2,1)S(1)}, bf16[128,512]{1,0:T(8,128)(2,1)S(1)}, f32[128,512]{1,0:T(8,128)S(1)}, f32[128,512]{1,0:T(8,128)S(1)}) custom-call(bf16[128,896]{1,0:T(8,128)(2,1)S(1)} %get-tuple-element.565.refs_0_, bf16[2,896,8192]{2,1,0:T(8,128)(2,1)} %refs_1_.13), custom_call_target="tpu_custom_call" | custom-call | flops 469762048 | bytes 3670016 | tf_op jit(solution)/shard_map/down/pallas_call | solution.py:104
  99.6 1.8 %down.15 = (bf16[128,512]{1,0:T(8,128)(2,1)S(1)}, f32[128,512]{1,0:T(8,128)S(1)}) custom-call(bf16[128,896]{1,0:T(8,128)(2,1)S(1)} %get-tuple-element.565.refs_0_, bf16[2,896,8192]{2,1,0:T(8,128)(2,1)} %refs_1_.13), custom_call_target="tpu_custom_call" | custom-call | flops 234881024 | bytes 1835008 | tf_op jit(solution)/shard_map/down/pallas_call | solution.py:104
  105.1 3.3 %collective-permute-done.59 = bf16[128,512]{1,0:T(8,128)(2,1)S(1)} collective-permute-done((bf16[128,512]{1,0:T(8,128)(2,1)S(1)}, bf16[128,512]{1,0:T(8,128)(2,1)S(1)}, u32[]{:S(2)}, u32[]{:S(2)}) %collective-permute-start.59) | collective-permute-done | bytes 131104 | tf_op jit(solution)/shard_map/ppermute | solution.py:164
  (143 shorter events, 40.0 us)
Async XLA Ops:
  0.0 7.5 %collective-permute-start = (bf16[128,512]{1,0:T(8,128)(2,1)}, bf16[128,512]{1,0:T(8,128)(2,1)S(1)}, u32[]{:S(2)}, u32[]{:S(2)}) collective-permute-start(bf16[128,512]{1,0:T(8,128)(2,1)} %bitcast.3), channel_id=1, source_target_pairs={{0,4},{1,5},{4,8},{5,9},{8,12},{9,13},{12,14},{13,15},{14,10},{15,... | collective-permute-start | bytes 393224 | tf_op jit(solution)/shard_map/ppermute | solution.py:164
  3.0 6.6 %collective-permute-start.2 = (bf16[128,512]{1,0:T(8,128)(2,1)}, bf16[128,512]{1,0:T(8,128)(2,1)S(1)}, u32[]{:S(2)}, u32[]{:S(2)}) collective-permute-start(bf16[128,512]{1,0:T(8,128)(2,1)} %bitcast.4), channel_id=1, source_target_pairs={{4,0},{5,1},{8,4},{9,5},{12,8},{13,9},{14,12},{15,13},{10,14},{11,... | collective-permute-start | bytes 393224 | tf_op jit(solution)/shard_map/ppermute | solution.py:164
  3.0 6.6 %collective-permute-start.3 = (bf16[128,512]{1,0:T(8,128)(2,1)}, bf16[128,512]{1,0:T(8,128)(2,1)S(1)}, u32[]{:S(2)}, u32[]{:S(2)}) collective-permute-start(bf16[128,512]{1,0:T(8,128)(2,1)} %bitcast.5), channel_id=1, source_target_pairs={{0,1},{1,0},{2,3},{3,2},{4,5},{5,4},{6,7},{7,6},{8,9},{9,8},{10,11... | collective-permute-start | bytes 393224 | tf_op jit(solution)/shard_map/ppermute | solution.py:164
  7.5 6.8 %collective-permute-start.1 = (bf16[128,512]{1,0:T(8,128)(2,1)S(1)}, bf16[128,512]{1,0:T(8,128)(2,1)S(1)}, u32[]{:S(2)}, u32[]{:S(2)}) collective-permute-start(bf16[128,512]{1,0:T(8,128)(2,1)S(1)} %collective-permute-done.refs_2_), channel_id=1, source_target_pairs={{0,4},{1,5},{4,8},{5,9},{8,12},{9,13},{12,14},{13,15},{14,10},{15,... | collective-permute-start | bytes 393224 | tf_op jit(solution)/shard_map/ppermute | solution.py:164
  9.6 6.4 %collective-permute-start.7 = (bf16[128,512]{1,0:T(8,128)(2,1)S(1)}, bf16[128,512]{1,0:T(8,128)(2,1)S(1)}, u32[]{:S(2)}, u32[]{:S(2)}) collective-permute-start(bf16[128,512]{1,0:T(8,128)(2,1)S(1)} %collective-permute-done.2.refs_3_), channel_id=1, source_target_pairs={{0,1},{1,0},{2,3},{3,2},{4,5},{5,4},{6,7},{7,6},{8,9},{9,8},{10,11... | collective-permute-start | bytes 393224 | tf_op jit(solution)/shard_map/ppermute | solution.py:164
  9.8 6.2 %collective-permute-start.5 = (bf16[128,512]{1,0:T(8,128)(2,1)S(1)}, bf16[128,512]{1,0:T(8,128)(2,1)S(1)}, u32[]{:S(2)}, u32[]{:S(2)}) collective-permute-start(bf16[128,512]{1,0:T(8,128)(2,1)S(1)} %collective-permute-done.2.refs_3_), channel_id=1, source_target_pairs={{4,0},{5,1},{8,4},{9,5},{12,8},{13,9},{14,12},{15,13},{10,14},{11,... | collective-permute-start | bytes 393224 | tf_op jit(solution)/shard_map/ppermute | solution.py:164
  10.2 5.9 %collective-permute-start.6 = (bf16[128,512]{1,0:T(8,128)(2,1)S(1)}, bf16[128,512]{1,0:T(8,128)(2,1)S(1)}, u32[]{:S(2)}, u32[]{:S(2)}) collective-permute-start(bf16[128,512]{1,0:T(8,128)(2,1)S(1)} %collective-permute-done.refs_2_), channel_id=1, source_target_pairs={{0,1},{1,0},{2,3},{3,2},{4,5},{5,4},{6,7},{7,6},{8,9},{9,8},{10,11... | collective-permute-start | bytes 393224 | tf_op jit(solution)/shard_map/ppermute | solution.py:164
  14.3 6.7 %collective-permute-start.4 = (bf16[128,512]{1,0:T(8,128)(2,1)S(1)}, bf16[128,512]{1,0:T(8,128)(2,1)S(1)}, u32[]{:S(2)}, u32[]{:S(2)}) collective-permute-start(bf16[128,512]{1,0:T(8,128)(2,1)S(1)} %collective-permute-done.1.refs_3_), channel_id=1, source_target_pairs={{0,4},{1,5},{4,8},{5,9},{8,12},{9,13},{12,14},{13,15},{14,10},{15,... | collective-permute-start | bytes 393224 | tf_op jit(solution)/shard_map/ppermute | solution.py:164
  16.1 7.2 %collective-permute-start.11 = (bf16[128,512]{1,0:T(8,128)(2,1)S(1)}, bf16[128,512]{1,0:T(8,128)(2,1)S(1)}, u32[]{:S(2)}, u32[]{:S(2)}) collective-permute-start(bf16[128,512]{1,0:T(8,128)(2,1)S(1)} %collective-permute-done.5.refs_4_), channel_id=1, source_target_pairs={{0,1},{1,0},{2,3},{3,2},{4,5},{5,4},{6,7},{7,6},{8,9},{9,8},{10,11... | collective-permute-start | bytes 393224 | tf_op jit(solution)/shard_map/ppermute | solution.py:164
  16.4 10.5 %collective-permute-start.9 = (bf16[128,512]{1,0:T(8,128)(2,1)S(1)}, bf16[128,512]{1,0:T(8,128)(2,1)S(1)}, u32[]{:S(2)}, u32[]{:S(2)}) collective-permute-start(bf16[128,512]{1,0:T(8,128)(2,1)S(1)} %collective-permute-done.5.refs_4_), channel_id=1, source_target_pairs={{4,0},{5,1},{8,4},{9,5},{12,8},{13,9},{14,12},{15,13},{10,14},{11,... | collective-permute-start | bytes 393224 | tf_op jit(solution)/shard_map/ppermute | solution.py:164
  16.7 6.6 %collective-permute-start.10 = (bf16[128,512]{1,0:T(8,128)(2,1)S(1)}, bf16[128,512]{1,0:T(8,128)(2,1)S(1)}, u32[]{:S(2)}, u32[]{:S(2)}) collective-permute-start(bf16[128,512]{1,0:T(8,128)(2,1)S(1)} %collective-permute-done.1.refs_3_), channel_id=1, source_target_pairs={{0,1},{1,0},{2,3},{3,2},{4,5},{5,4},{6,7},{7,6},{8,9},{9,8},{10,11... | collective-permute-start | bytes 393224 | tf_op jit(solution)/shard_map/ppermute | solution.py:164
  21.0 5.9 %collective-permute-start.12 = (bf16[128,512]{1,0:T(8,128)(2,1)S(1)}, bf16[128,512]{1,0:T(8,128)(2,1)S(1)}, u32[]{:S(2)}, u32[]{:S(2)}) collective-permute-start(bf16[128,512]{1,0:T(8,128)(2,1)S(1)} %collective-permute-done.4.refs_3_), channel_id=1, source_target_pairs={{0,1},{1,0},{2,3},{3,2},{4,5},{5,4},{6,7},{7,6},{8,9},{9,8},{10,11... | collective-permute-start | bytes 393224 | tf_op jit(solution)/shard_map/ppermute | solution.py:164
  21.5 6.2 %collective-permute-start.8 = (bf16[128,512]{1,0:T(8,128)(2,1)S(1)}, bf16[128,512]{1,0:T(8,128)(2,1)S(1)}, u32[]{:S(2)}, u32[]{:S(2)}) collective-permute-start(bf16[128,512]{1,0:T(8,128)(2,1)S(1)} %collective-permute-done.4.refs_3_), channel_id=1, source_target_pairs={{0,4},{1,5},{4,8},{5,9},{8,12},{9,13},{12,14},{13,15},{14,10},{15,... | collective-permute-start | bytes 393224 | tf_op jit(solution)/shard_map/ppermute | solution.py:164
  39.3 5.9 %collective-permute-start.19 = (bf16[128,512]{1,0:T(8,128)(2,1)S(1)}, bf16[128,512]{1,0:T(8,128)(2,1)S(1)}, u32[]{:S(2)}, u32[]{:S(2)}) collective-permute-start(bf16[128,512]{1,0:T(8,128)(2,1)S(1)} %add_convert_fusion.14), channel_id=1, source_target_pairs={{4,0},{5,1},{8,4},{9,5},{12,8},{13,9},{14,12},{15,13},{10,14},{11,... | collective-permute-start | bytes 393224 | tf_op jit(solution)/shard_map/ppermute | solution.py:164
  45.3 6.2 %collective-permute-start.23 = (bf16[128,512]{1,0:T(8,128)(2,1)S(1)}, bf16[128,512]{1,0:T(8,128)(2,1)S(1)}, u32[]{:S(2)}, u32[]{:S(2)}) collective-permute-start(bf16[128,512]{1,0:T(8,128)(2,1)S(1)} %add_convert_fusion.12), channel_id=1, source_target_pairs={{4,0},{5,1},{8,4},{9,5},{12,8},{13,9},{14,12},{15,13},{10,14},{11,... | collective-permute-start | bytes 393224 | tf_op jit(solution)/shard_map/ppermute | solution.py:164
  45.8 5.8 %collective-permute-start.25 = (bf16[128,512]{1,0:T(8,128)(2,1)S(1)}, bf16[128,512]{1,0:T(8,128)(2,1)S(1)}, u32[]{:S(2)}, u32[]{:S(2)}) collective-permute-start(bf16[128,512]{1,0:T(8,128)(2,1)S(1)} %get-tuple-element.414), channel_id=1, source_target_pairs={{0,1},{1,0},{2,3},{3,2},{4,5},{5,4},{6,7},{7,6},{8,9},{9,8},{10,11... | collective-permute-start | bytes 393224 | tf_op jit(solution)/shard_map/ppermute | solution.py:164
  46.3 5.8 %collective-permute-start.27 = (bf16[128,512]{1,0:T(8,128)(2,1)S(1)}, bf16[128,512]{1,0:T(8,128)(2,1)S(1)}, u32[]{:S(2)}, u32[]{:S(2)}) collective-permute-start(bf16[128,512]{1,0:T(8,128)(2,1)S(1)} %add_convert_fusion.11), channel_id=1, source_target_pairs={{0,4},{1,5},{4,8},{5,9},{8,12},{9,13},{12,14},{13,15},{14,10},{15,... | collective-permute-start | bytes 393224 | tf_op jit(solution)/shard_map/ppermute | solution.py:164
  51.6 7.0 %collective-permute-start.29 = (bf16[128,512]{1,0:T(8,128)(2,1)S(1)}, bf16[128,512]{1,0:T(8,128)(2,1)S(1)}, u32[]{:S(2)}, u32[]{:S(2)}) collective-permute-start(bf16[128,512]{1,0:T(8,128)(2,1)S(1)} %add_convert_fusion.10), channel_id=1, source_target_pairs={{4,0},{5,1},{8,4},{9,5},{12,8},{13,9},{14,12},{15,13},{10,14},{11,... | collective-permute-start | bytes 393224 | tf_op jit(solution)/shard_map/ppermute | solution.py:164
  52.2 6.4 %collective-permute-start.28 = (bf16[128,512]{1,0:T(8,128)(2,1)S(1)}, bf16[128,512]{1,0:T(8,128)(2,1)S(1)}, u32[]{:S(2)}, u32[]{:S(2)}) collective-permute-start(bf16[128,512]{1,0:T(8,128)(2,1)S(1)} %add_convert_fusion.9), channel_id=1, source_target_pairs={{0,4},{1,5},{4,8},{5,9},{8,12},{9,13},{12,14},{13,15},{14,10},{15,... | collective-permute-start | bytes 393224 | tf_op jit(solution)/shard_map/ppermute | solution.py:164
  58.7 6.0 %collective-permute-start.31 = (bf16[128,512]{1,0:T(8,128)(2,1)S(1)}, bf16[128,512]{1,0:T(8,128)(2,1)S(1)}, u32[]{:S(2)}, u32[]{:S(2)}) collective-permute-start(bf16[128,512]{1,0:T(8,128)(2,1)S(1)} %add_convert_fusion.8.refs_1_), channel_id=1, source_target_pairs={{0,4},{1,5},{4,8},{5,9},{8,12},{9,13},{12,14},{13,15},{14,10},{15,... | collective-permute-start | bytes 393224 | tf_op jit(solution)/shard_map/ppermute | solution.py:164
  60.4 5.8 %collective-permute-start.34 = (bf16[128,512]{1,0:T(8,128)(2,1)S(1)}, bf16[128,512]{1,0:T(8,128)(2,1)S(1)}, u32[]{:S(2)}, u32[]{:S(2)}) collective-permute-start(bf16[128,512]{1,0:T(8,128)(2,1)S(1)} %add_convert_fusion.8.refs_1_), channel_id=1, source_target_pairs={{0,1},{1,0},{2,3},{3,2},{4,5},{5,4},{6,7},{7,6},{8,9},{9,8},{10,11... | collective-permute-start | bytes 393224 | tf_op jit(solution)/shard_map/ppermute | solution.py:164
  66.3 5.9 %collective-permute-start.36 = (bf16[128,512]{1,0:T(8,128)(2,1)S(1)}, bf16[128,512]{1,0:T(8,128)(2,1)S(1)}, u32[]{:S(2)}, u32[]{:S(2)}) collective-permute-start(bf16[128,512]{1,0:T(8,128)(2,1)S(1)} %collective-permute-done.33.refs_3_), channel_id=1, source_target_pairs={{4,0},{5,1},{8,4},{9,5},{12,8},{13,9},{14,12},{15,13},{10,14},{11,... | collective-permute-start | bytes 393224 | tf_op jit(solution)/shard_map/ppermute | solution.py:164
  72.2 8.3 %collective-permute-start.40 = (bf16[128,512]{1,0:T(8,128)(2,1)S(1)}, bf16[128,512]{1,0:T(8,128)(2,1)S(1)}, u32[]{:S(2)}, u32[]{:S(2)}) collective-permute-start(bf16[128,512]{1,0:T(8,128)(2,1)S(1)} %collective-permute-done.36.refs_4_), channel_id=1, source_target_pairs={{4,0},{5,1},{8,4},{9,5},{12,8},{13,9},{14,12},{15,13},{10,14},{11,... | collective-permute-start | bytes 393224 | tf_op jit(solution)/shard_map/ppermute | solution.py:164
  101.5 6.9 %collective-permute-start.60 = (bf16[128,512]{1,0:T(8,128)(2,1)S(1)}, bf16[128,512]{1,0:T(8,128)(2,1)S(1)}, u32[]{:S(2)}, u32[]{:S(2)}) collective-permute-start(bf16[128,512]{1,0:T(8,128)(2,1)S(1)} %add_convert_fusion.2), channel_id=1, source_target_pairs={{4,0},{5,1},{8,4},{9,5},{12,8},{13,9},{14,12},{15,13},{10,14},{11,... | collective-permute-start | bytes 393224 | tf_op jit(solution)/shard_map/ppermute | solution.py:164
  (39 other events, 177.8 us)

commit v4 on v3

--- a/solution.py
+++ b/solution.py
@@ -14,8 +14,8 @@
 LIMIT = 20 * 1024 * 1024
 AHEAD = {
     (0, "gather1"): 4, (0, "gather2"): 4, (0, "gather3"): 4, (0, "gather4"): 3, (0, "gathered"): 0, (0, "last"): 3,
-    (0, "scatter2"): 2, (0, "scatter1"): 4, (0, "scatter0"): 7,
-    (1, "gather1"): 3, (1, "gather2"): 1, (1, "gather3"): 1, (1, "gather4"): 2,
+    (0, "scatter2"): 2, (0, "scatter1"): 4, (0, "scatter0"): 6,
+    (1, "gather1"): 4, (1, "gather2"): 2, (1, "gather4"): 2,
 }
 
 

time: 109 us -> 108 us (level)
  transfers between devices with their start and end apart: 62 -> 62, of which waited for: 13 -> 13; matrix products, arithmetic and copies ran while one was open for 0% -> 0% of each run, Pallas kernels for 51% -> 50%
where the time goes in v4:
time: 108 us
  Pallas kernels  56.2 us (52%)
  starting transfers between devices  40.2 us (37%)
  waiting for transfers between devices  9.81 us (9%)
  other arithmetic  1.39 us (1%)
    pallas_call x23, Pallas kernels, stage(): pl.pallas_call(functools.partial(stage_kernel, chips, job, list(raw), str...  56.2 us
    ppermute x62, starting transfers between devices, send(): return lax.ppermute(x, AXIS, perm)  40.2 us
    ppermute x62, waiting for transfers between devices, send(): return lax.ppermute(x, AXIS, perm)  9.81 us
  transfers between devices with their start and end apart: 62, of which 13 were waited for; matrix products, arithmetic and copies ran while one was open for 0% of the time, Pallas kernels for 50%

profile of v4, /device:TPU:0, one launch (start us, length us, event | category | flops | bytes accessed | tf_op | source)
XLA Modules:
  0.0 108.2 jit_solution(7177239099465565891)
XLA Ops:
  0.0 3.0 %collective-permute-start = (bf16[128,512]{1,0:T(8,128)(2,1)}, bf16[128,512]{1,0:T(8,128)(2,1)S(1)}, u32[]{:S(2)}, u32[]{:S(2)}) collective-permute-start(bf16[128,512]{1,0:T(8,128)(2,1)} %bitcast.3), channel_id=1, source_target_pairs={{0,4},{1,5},{4,8},{5,9},{8,12},{9,13},{12,14},{13,15},{14,10},{15,... | collective-permute-start | bytes 393224 | tf_op jit(solution)/shard_map/ppermute | solution.py:164
  3.0 4.5 %gate_up.12 = (f32[128,896]{1,0:T(8,128)S(1)}, f32[128,896]{1,0:T(8,128)S(1)}, f32[128,128]{1,0:T(8,128)S(1)}, f32[2,8192]{1,0:T(2,128)S(1)}, bf16[128,512]{1,0:...) custom-call(bf16[2,8192,896]{2,1,0:T(8,128)(2,1)} %refs_14_.5, ...), custom_call_target="tpu_custom_call" | custom-call | flops 234881024 | bytes 9175040 | tf_op jit(solution)/shard_map/gate_up/pallas_call | solution.py:104
  7.5 2.1 %collective-permute-start.1 = (bf16[128,512]{1,0:T(8,128)(2,1)S(1)}, bf16[128,512]{1,0:T(8,128)(2,1)S(1)}, u32[]{:S(2)}, u32[]{:S(2)}) collective-permute-start(bf16[128,512]{1,0:T(8,128)(2,1)S(1)} %collective-permute-done.refs_2_), channel_id=1, source_target_pairs={{0,4},{1,5},{4,8},{5,9},{8,12},{9,13},{12,14},{13,15},{14,10},{15,... | collective-permute-start | bytes 393224 | tf_op jit(solution)/shard_map/ppermute | solution.py:164
  10.2 4.1 %gate_up.13 = (f32[128,896]{1,0:T(8,128)S(1)}, f32[128,896]{1,0:T(8,128)S(1)}, f32[128,128]{1,0:T(8,128)S(1)}, bf16[512,896]{1,0:T(8,128)(2,1)S(1)}, bf16[512,89...) custom-call(f32[2,8192]{1,0:T(2,128)S(1)} %get-tuple-element.293.ref, ...), custom_call_target="tpu_custom_call", output_to_operand_aliasing={{0}: (4, {}), {1}: (5, {}), {2}: (6, {})} | custom-call | flops 704643072 | bytes 7340032 | tf_op jit(solution)/shard_map/gate_up/pallas_call | solution.py:104
  14.3 1.7 %collective-permute-start.4 = (bf16[128,512]{1,0:T(8,128)(2,1)S(1)}, bf16[128,512]{1,0:T(8,128)(2,1)S(1)}, u32[]{:S(2)}, u32[]{:S(2)}) collective-permute-start(bf16[128,512]{1,0:T(8,128)(2,1)S(1)} %collective-permute-done.1.refs_3_), channel_id=1, source_target_pairs={{0,4},{1,5},{4,8},{5,9},{8,12},{9,13},{12,14},{13,15},{14,10},{15,... | collective-permute-start | bytes 393224 | tf_op jit(solution)/shard_map/ppermute | solution.py:164
  16.7 4.3 %gate_up.14 = (f32[128,896]{1,0:T(8,128)S(1)}, f32[128,896]{1,0:T(8,128)S(1)}, f32[128,128]{1,0:T(8,128)S(1)}, bf16[512,896]{1,0:T(8,128)(2,1)S(1)}, bf16[512,89...) custom-call(f32[2,8192]{1,0:T(2,128)S(1)} %get-tuple-element.293.ref, ...), custom_call_target="tpu_custom_call", output_to_operand_aliasing={{0}: (5, {}), {1}: (6, {}), {2}: (7, {})} | custom-call | flops 939524096 | bytes 7340032 | tf_op jit(solution)/shard_map/gate_up/pallas_call | solution.py:104
  21.5 1.7 %collective-permute-start.8 = (bf16[128,512]{1,0:T(8,128)(2,1)S(1)}, bf16[128,512]{1,0:T(8,128)(2,1)S(1)}, u32[]{:S(2)}, u32[]{:S(2)}) collective-permute-start(bf16[128,512]{1,0:T(8,128)(2,1)S(1)} %collective-permute-done.4.refs_3_), channel_id=1, source_target_pairs={{0,4},{1,5},{4,8},{5,9},{8,12},{9,13},{12,14},{13,15},{14,10},{15,... | collective-permute-start | bytes 393224 | tf_op jit(solution)/shard_map/ppermute | solution.py:164
  23.3 3.6 %gate_up.15 = (f32[128,896]{1,0:T(8,128)S(1)}, f32[128,896]{1,0:T(8,128)S(1)}, f32[128,128]{1,0:T(8,128)S(1)}, bf16[512,896]{1,0:T(8,128)(2,1)S(1)}, bf16[512,89...) custom-call(f32[2,8192]{1,0:T(2,128)S(1)} %get-tuple-element.293.ref, ...), custom_call_target="tpu_custom_call", output_to_operand_aliasing={{0}: (4, {}), {1}: (5, {}), {2}: (6, {})} | custom-call | flops 704643072 | bytes 5505024 | tf_op jit(solution)/shard_map/gate_up/pallas_call | solution.py:104
  28.4 3.3 %gate_up.17 = (f32[128,896]{1,0:T(8,128)S(1)}, f32[128,896]{1,0:T(8,128)S(1)}, f32[128,128]{1,0:T(8,128)S(1)}, bf16[896,512]{1,0:T(8,128)(2,1)S(1)}, bf16[896,51...) custom-call(f32[2,8192]{1,0:T(2,128)S(1)} %get-tuple-element.293.ref, ...), custom_call_target="tpu_custom_call", output_to_operand_aliasing={{0}: (3, {}), {1}: (4, {}), {2}: (5, {})} | custom-call | flops 469762048 | bytes 5505024 | tf_op jit(solution)/shard_map/gate_up/pallas_call | solution.py:104
  35.1 1.6 %collective-permute-start.22 = (bf16[64,512]{1,0:T(8,128)(2,1)S(1)}, bf16[64,512]{1,0:T(8,128)(2,1)S(1)}, u32[]{:S(2)}, u32[]{:S(2)}) collective-permute-start(bf16[64,512]{1,0:T(8,128)(2,1)S(1)} %get-tuple-element.583), channel_id=1, source_target_pairs={{0,4},{1,5},{4,8},{5,9},{8,12},{9,13},{12,14},{13,15},{14,10},{15,... | collective-permute-start | bytes 196616 | tf_op jit(solution)/shard_map/ppermute | solution.py:164
  36.7 2.5 %down.9 = (bf16[128,512]{1,0:T(8,128)(2,1)S(1)}, bf16[128,512]{1,0:T(8,128)(2,1)S(1)}, f32[128,512]{1,0:T(8,128)S(1)}, f32[128,512]{1,0:T(8,128)S(1)}) custom-call(bf16[128,896]{1,0:T(8,128)(2,1)S(1)} %get-tuple-element.444.refs_0_, bf16[2,896,8192]{2,1,0:T(8,128)(2,1)} %refs_1_.13), custom_call_target="tpu_custom_call" | custom-call | flops 469762048 | bytes 3670016 | tf_op jit(solution)/shard_map/down/pallas_call | solution.py:104
  40.3 1.7 %collective-permute-start.26 = (bf16[128,512]{1,0:T(8,128)(2,1)S(1)}, bf16[128,512]{1,0:T(8,128)(2,1)S(1)}, u32[]{:S(2)}, u32[]{:S(2)}) collective-permute-start(bf16[128,512]{1,0:T(8,128)(2,1)S(1)} %add_convert_fusion.13), channel_id=1, source_target_pairs={{0,4},{1,5},{4,8},{5,9},{8,12},{9,13},{12,14},{13,15},{14,10},{15,... | collective-permute-start | bytes 393224 | tf_op jit(solution)/shard_map/ppermute | solution.py:164
  42.0 3.2 %down.10 = (bf16[128,512]{1,0:T(8,128)(2,1)S(1)}, bf16[128,512]{1,0:T(8,128)(2,1)S(1)}, f32[128,512]{1,0:T(8,128)S(1)}, f32[128,512]{1,0:T(8,128)S(1)}, bf16[896...) custom-call(bf16[128,896]{1,0:T(8,128)(2,1)S(1)} %get-tuple-element., ...), custom_call_target="tpu_custom_call" | custom-call | flops 469762048 | bytes 7340032 | tf_op jit(solution)/shard_map/down/pallas_call | solution.py:104
  46.3 1.7 %collective-permute-start.27 = (bf16[128,512]{1,0:T(8,128)(2,1)S(1)}, bf16[128,512]{1,0:T(8,128)(2,1)S(1)}, u32[]{:S(2)}, u32[]{:S(2)}) collective-permute-start(bf16[128,512]{1,0:T(8,128)(2,1)S(1)} %add_convert_fusion.11), channel_id=1, source_target_pairs={{0,4},{1,5},{4,8},{5,9},{8,12},{9,13},{12,14},{13,15},{14,10},{15,... | collective-permute-start | bytes 393224 | tf_op jit(solution)/shard_map/ppermute | solution.py:164
  48.0 3.5 %down.11 = (bf16[128,512]{1,0:T(8,128)(2,1)S(1)}, f32[128,512]{1,0:T(8,128)S(1)}, bf16[512,896]{1,0:T(8,128)(2,1)S(1)}, bf16[512,896]{1,0:T(8,128)(2,1)S(1)}, bf...) custom-call(bf16[128,896]{1,0:T(8,128)(2,1)S(1)} %get-tuple-element., ...), custom_call_target="tpu_custom_call" | custom-call | flops 234881024 | bytes 7340032 | tf_op jit(solution)/shard_map/down/pallas_call | solution.py:104
  53.8 4.2 %ahead.1 = (bf16[512,896]{1,0:T(8,128)(2,1)S(1)}, bf16[512,896]{1,0:T(8,128)(2,1)S(1)}, bf16[512,896]{1,0:T(8,128)(2,1)S(1)}, bf16[512,896]{1,0:T(8,128)(2,1)S(1...) custom-call(bf16[128,896]{1,0:T(8,128)(2,1)S(1)} %get-tuple-element., ...), custom_call_target="tpu_custom_call" | custom-call | bytes 11010048 | tf_op jit(solution)/shard_map/ahead/pallas_call | solution.py:104
  58.2 1.6 %collective-permute-start.31 = (bf16[128,512]{1,0:T(8,128)(2,1)S(1)}, bf16[128,512]{1,0:T(8,128)(2,1)S(1)}, u32[]{:S(2)}, u32[]{:S(2)}) collective-permute-start(bf16[128,512]{1,0:T(8,128)(2,1)S(1)} %add_convert_fusion.8.refs_1_), channel_id=1, source_target_pairs={{0,4},{1,5},{4,8},{5,9},{8,12},{9,13},{12,14},{13,15},{14,10},{15,... | collective-permute-start | bytes 393224 | tf_op jit(solution)/shard_map/ppermute | solution.py:164
  60.5 3.5 %gate_up.18 = (f32[128,896]{1,0:T(8,128)S(1)}, f32[128,896]{1,0:T(8,128)S(1)}, f32[128,128]{1,0:T(8,128)S(1)}, bf16[512,896]{1,0:T(8,128)(2,1)S(1)}, bf16[512,89...) custom-call(f32[2,8192]{1,0:T(2,128)S(1)} %get-tuple-element.293.ref, ...), custom_call_target="tpu_custom_call" | custom-call | flops 234881024 | bytes 7340032 | tf_op jit(solution)/shard_map/gate_up/pallas_call | solution.py:104
  66.4 2.7 %gate_up.19 = (f32[128,896]{1,0:T(8,128)S(1)}, f32[128,896]{1,0:T(8,128)S(1)}, f32[128,128]{1,0:T(8,128)S(1)}, bf16[512,896]{1,0:T(8,128)(2,1)S(1)}, bf16[512,89...) custom-call(f32[2,8192]{1,0:T(2,128)S(1)} %get-tuple-element.293.ref, ...), custom_call_target="tpu_custom_call", output_to_operand_aliasing={{0}: (4, {}), {1}: (5, {}), {2}: (6, {})} | custom-call | flops 704643072 | bytes 3670016 | tf_op jit(solution)/shard_map/gate_up/pallas_call | solution.py:104
  76.5 3.0 %gate_up.21 = (f32[128,896]{1,0:T(8,128)S(1)}, f32[128,896]{1,0:T(8,128)S(1)}, f32[128,128]{1,0:T(8,128)S(1)}, bf16[896,512]{1,0:T(8,128)(2,1)S(1)}, bf16[896,51...) custom-call(f32[2,8192]{1,0:T(2,128)S(1)} %get-tuple-element.293.ref, ...), custom_call_target="tpu_custom_call", output_to_operand_aliasing={{0}: (4, {}), {1}: (5, {}), {2}: (6, {})} | custom-call | flops 704643072 | bytes 3670016 | tf_op jit(solution)/shard_map/gate_up/pallas_call | solution.py:104
  87.3 2.5 %down.13 = (bf16[128,512]{1,0:T(8,128)(2,1)S(1)}, bf16[128,512]{1,0:T(8,128)(2,1)S(1)}, f32[128,512]{1,0:T(8,128)S(1)}, f32[128,512]{1,0:T(8,128)S(1)}) custom-call(bf16[128,896]{1,0:T(8,128)(2,1)S(1)} %get-tuple-element.565.refs_0_, bf16[2,896,8192]{2,1,0:T(8,128)(2,1)} %refs_1_.13), custom_call_target="tpu_custom_call" | custom-call | flops 469762048 | bytes 3670016 | tf_op jit(solution)/shard_map/down/pallas_call | solution.py:104
  92.6 2.5 %down.14 = (bf16[128,512]{1,0:T(8,128)(2,1)S(1)}, bf16[128,512]{1,0:T(8,128)(2,1)S(1)}, f32[128,512]{1,0:T(8,128)S(1)}, f32[128,512]{1,0:T(8,128)S(1)}) custom-call(bf16[128,896]{1,0:T(8,128)(2,1)S(1)} %get-tuple-element.565.refs_0_, bf16[2,896,8192]{2,1,0:T(8,128)(2,1)} %refs_1_.13), custom_call_target="tpu_custom_call" | custom-call | flops 469762048 | bytes 3670016 | tf_op jit(solution)/shard_map/down/pallas_call | solution.py:104
  98.6 1.8 %down.15 = (bf16[128,512]{1,0:T(8,128)(2,1)S(1)}, f32[128,512]{1,0:T(8,128)S(1)}) custom-call(bf16[128,896]{1,0:T(8,128)(2,1)S(1)} %get-tuple-element.565.refs_0_, bf16[2,896,8192]{2,1,0:T(8,128)(2,1)} %refs_1_.13), custom_call_target="tpu_custom_call" | custom-call | flops 234881024 | bytes 1835008 | tf_op jit(solution)/shard_map/down/pallas_call | solution.py:104
  104.1 3.4 %collective-permute-done.59 = bf16[128,512]{1,0:T(8,128)(2,1)S(1)} collective-permute-done((bf16[128,512]{1,0:T(8,128)(2,1)S(1)}, bf16[128,512]{1,0:T(8,128)(2,1)S(1)}, u32[]{:S(2)}, u32[]{:S(2)}) %collective-permute-start.59) | collective-permute-done | bytes 131104 | tf_op jit(solution)/shard_map/ppermute | solution.py:164
  (143 shorter events, 39.7 us)
Async XLA Ops:
  0.0 7.5 %collective-permute-start = (bf16[128,512]{1,0:T(8,128)(2,1)}, bf16[128,512]{1,0:T(8,128)(2,1)S(1)}, u32[]{:S(2)}, u32[]{:S(2)}) collective-permute-start(bf16[128,512]{1,0:T(8,128)(2,1)} %bitcast.3), channel_id=1, source_target_pairs={{0,4},{1,5},{4,8},{5,9},{8,12},{9,13},{12,14},{13,15},{14,10},{15,... | collective-permute-start | bytes 393224 | tf_op jit(solution)/shard_map/ppermute | solution.py:164
  3.0 6.6 %collective-permute-start.2 = (bf16[128,512]{1,0:T(8,128)(2,1)}, bf16[128,512]{1,0:T(8,128)(2,1)S(1)}, u32[]{:S(2)}, u32[]{:S(2)}) collective-permute-start(bf16[128,512]{1,0:T(8,128)(2,1)} %bitcast.4), channel_id=1, source_target_pairs={{4,0},{5,1},{8,4},{9,5},{12,8},{13,9},{14,12},{15,13},{10,14},{11,... | collective-permute-start | bytes 393224 | tf_op jit(solution)/shard_map/ppermute | solution.py:164
  3.0 6.6 %collective-permute-start.3 = (bf16[128,512]{1,0:T(8,128)(2,1)}, bf16[128,512]{1,0:T(8,128)(2,1)S(1)}, u32[]{:S(2)}, u32[]{:S(2)}) collective-permute-start(bf16[128,512]{1,0:T(8,128)(2,1)} %bitcast.5), channel_id=1, source_target_pairs={{0,1},{1,0},{2,3},{3,2},{4,5},{5,4},{6,7},{7,6},{8,9},{9,8},{10,11... | collective-permute-start | bytes 393224 | tf_op jit(solution)/shard_map/ppermute | solution.py:164
  7.5 6.8 %collective-permute-start.1 = (bf16[128,512]{1,0:T(8,128)(2,1)S(1)}, bf16[128,512]{1,0:T(8,128)(2,1)S(1)}, u32[]{:S(2)}, u32[]{:S(2)}) collective-permute-start(bf16[128,512]{1,0:T(8,128)(2,1)S(1)} %collective-permute-done.refs_2_), channel_id=1, source_target_pairs={{0,4},{1,5},{4,8},{5,9},{8,12},{9,13},{12,14},{13,15},{14,10},{15,... | collective-permute-start | bytes 393224 | tf_op jit(solution)/shard_map/ppermute | solution.py:164
  9.6 6.4 %collective-permute-start.7 = (bf16[128,512]{1,0:T(8,128)(2,1)S(1)}, bf16[128,512]{1,0:T(8,128)(2,1)S(1)}, u32[]{:S(2)}, u32[]{:S(2)}) collective-permute-start(bf16[128,512]{1,0:T(8,128)(2,1)S(1)} %collective-permute-done.2.refs_3_), channel_id=1, source_target_pairs={{0,1},{1,0},{2,3},{3,2},{4,5},{5,4},{6,7},{7,6},{8,9},{9,8},{10,11... | collective-permute-start | bytes 393224 | tf_op jit(solution)/shard_map/ppermute | solution.py:164
  9.8 6.2 %collective-permute-start.5 = (bf16[128,512]{1,0:T(8,128)(2,1)S(1)}, bf16[128,512]{1,0:T(8,128)(2,1)S(1)}, u32[]{:S(2)}, u32[]{:S(2)}) collective-permute-start(bf16[128,512]{1,0:T(8,128)(2,1)S(1)} %collective-permute-done.2.refs_3_), channel_id=1, source_target_pairs={{4,0},{5,1},{8,4},{9,5},{12,8},{13,9},{14,12},{15,13},{10,14},{11,... | collective-permute-start | bytes 393224 | tf_op jit(solution)/shard_map/ppermute | solution.py:164
  10.2 5.9 %collective-permute-start.6 = (bf16[128,512]{1,0:T(8,128)(2,1)S(1)}, bf16[128,512]{1,0:T(8,128)(2,1)S(1)}, u32[]{:S(2)}, u32[]{:S(2)}) collective-permute-start(bf16[128,512]{1,0:T(8,128)(2,1)S(1)} %collective-permute-done.refs_2_), channel_id=1, source_target_pairs={{0,1},{1,0},{2,3},{3,2},{4,5},{5,4},{6,7},{7,6},{8,9},{9,8},{10,11... | collective-permute-start | bytes 393224 | tf_op jit(solution)/shard_map/ppermute | solution.py:164
  14.3 6.7 %collective-permute-start.4 = (bf16[128,512]{1,0:T(8,128)(2,1)S(1)}, bf16[128,512]{1,0:T(8,128)(2,1)S(1)}, u32[]{:S(2)}, u32[]{:S(2)}) collective-permute-start(bf16[128,512]{1,0:T(8,128)(2,1)S(1)} %collective-permute-done.1.refs_3_), channel_id=1, source_target_pairs={{0,4},{1,5},{4,8},{5,9},{8,12},{9,13},{12,14},{13,15},{14,10},{15,... | collective-permute-start | bytes 393224 | tf_op jit(solution)/shard_map/ppermute | solution.py:164
  16.1 7.2 %collective-permute-start.11 = (bf16[128,512]{1,0:T(8,128)(2,1)S(1)}, bf16[128,512]{1,0:T(8,128)(2,1)S(1)}, u32[]{:S(2)}, u32[]{:S(2)}) collective-permute-start(bf16[128,512]{1,0:T(8,128)(2,1)S(1)} %collective-permute-done.5.refs_4_), channel_id=1, source_target_pairs={{0,1},{1,0},{2,3},{3,2},{4,5},{5,4},{6,7},{7,6},{8,9},{9,8},{10,11... | collective-permute-start | bytes 393224 | tf_op jit(solution)/shard_map/ppermute | solution.py:164
  16.4 10.5 %collective-permute-start.9 = (bf16[128,512]{1,0:T(8,128)(2,1)S(1)}, bf16[128,512]{1,0:T(8,128)(2,1)S(1)}, u32[]{:S(2)}, u32[]{:S(2)}) collective-permute-start(bf16[128,512]{1,0:T(8,128)(2,1)S(1)} %collective-permute-done.5.refs_4_), channel_id=1, source_target_pairs={{4,0},{5,1},{8,4},{9,5},{12,8},{13,9},{14,12},{15,13},{10,14},{11,... | collective-permute-start | bytes 393224 | tf_op jit(solution)/shard_map/ppermute | solution.py:164
  16.7 6.6 %collective-permute-start.10 = (bf16[128,512]{1,0:T(8,128)(2,1)S(1)}, bf16[128,512]{1,0:T(8,128)(2,1)S(1)}, u32[]{:S(2)}, u32[]{:S(2)}) collective-permute-start(bf16[128,512]{1,0:T(8,128)(2,1)S(1)} %collective-permute-done.1.refs_3_), channel_id=1, source_target_pairs={{0,1},{1,0},{2,3},{3,2},{4,5},{5,4},{6,7},{7,6},{8,9},{9,8},{10,11... | collective-permute-start | bytes 393224 | tf_op jit(solution)/shard_map/ppermute | solution.py:164
  21.0 5.9 %collective-permute-start.12 = (bf16[128,512]{1,0:T(8,128)(2,1)S(1)}, bf16[128,512]{1,0:T(8,128)(2,1)S(1)}, u32[]{:S(2)}, u32[]{:S(2)}) collective-permute-start(bf16[128,512]{1,0:T(8,128)(2,1)S(1)} %collective-permute-done.4.refs_3_), channel_id=1, source_target_pairs={{0,1},{1,0},{2,3},{3,2},{4,5},{5,4},{6,7},{7,6},{8,9},{9,8},{10,11... | collective-permute-start | bytes 393224 | tf_op jit(solution)/shard_map/ppermute | solution.py:164
  21.5 6.2 %collective-permute-start.8 = (bf16[128,512]{1,0:T(8,128)(2,1)S(1)}, bf16[128,512]{1,0:T(8,128)(2,1)S(1)}, u32[]{:S(2)}, u32[]{:S(2)}) collective-permute-start(bf16[128,512]{1,0:T(8,128)(2,1)S(1)} %collective-permute-done.4.refs_3_), channel_id=1, source_target_pairs={{0,4},{1,5},{4,8},{5,9},{8,12},{9,13},{12,14},{13,15},{14,10},{15,... | collective-permute-start | bytes 393224 | tf_op jit(solution)/shard_map/ppermute | solution.py:164
  39.3 5.9 %collective-permute-start.19 = (bf16[128,512]{1,0:T(8,128)(2,1)S(1)}, bf16[128,512]{1,0:T(8,128)(2,1)S(1)}, u32[]{:S(2)}, u32[]{:S(2)}) collective-permute-start(bf16[128,512]{1,0:T(8,128)(2,1)S(1)} %add_convert_fusion.14), channel_id=1, source_target_pairs={{4,0},{5,1},{8,4},{9,5},{12,8},{13,9},{14,12},{15,13},{10,14},{11,... | collective-permute-start | bytes 393224 | tf_op jit(solution)/shard_map/ppermute | solution.py:164
  45.3 6.2 %collective-permute-start.23 = (bf16[128,512]{1,0:T(8,128)(2,1)S(1)}, bf16[128,512]{1,0:T(8,128)(2,1)S(1)}, u32[]{:S(2)}, u32[]{:S(2)}) collective-permute-start(bf16[128,512]{1,0:T(8,128)(2,1)S(1)} %add_convert_fusion.12), channel_id=1, source_target_pairs={{4,0},{5,1},{8,4},{9,5},{12,8},{13,9},{14,12},{15,13},{10,14},{11,... | collective-permute-start | bytes 393224 | tf_op jit(solution)/shard_map/ppermute | solution.py:164
  46.3 5.8 %collective-permute-start.27 = (bf16[128,512]{1,0:T(8,128)(2,1)S(1)}, bf16[128,512]{1,0:T(8,128)(2,1)S(1)}, u32[]{:S(2)}, u32[]{:S(2)}) collective-permute-start(bf16[128,512]{1,0:T(8,128)(2,1)S(1)} %add_convert_fusion.11), channel_id=1, source_target_pairs={{0,4},{1,5},{4,8},{5,9},{8,12},{9,13},{12,14},{13,15},{14,10},{15,... | collective-permute-start | bytes 393224 | tf_op jit(solution)/shard_map/ppermute | solution.py:164
  51.6 6.5 %collective-permute-start.29 = (bf16[128,512]{1,0:T(8,128)(2,1)S(1)}, bf16[128,512]{1,0:T(8,128)(2,1)S(1)}, u32[]{:S(2)}, u32[]{:S(2)}) collective-permute-start(bf16[128,512]{1,0:T(8,128)(2,1)S(1)} %add_convert_fusion.10), channel_id=1, source_target_pairs={{4,0},{5,1},{8,4},{9,5},{12,8},{13,9},{14,12},{15,13},{10,14},{11,... | collective-permute-start | bytes 393224 | tf_op jit(solution)/shard_map/ppermute | solution.py:164
  52.2 5.9 %collective-permute-start.28 = (bf16[128,512]{1,0:T(8,128)(2,1)S(1)}, bf16[128,512]{1,0:T(8,128)(2,1)S(1)}, u32[]{:S(2)}, u32[]{:S(2)}) collective-permute-start(bf16[128,512]{1,0:T(8,128)(2,1)S(1)} %add_convert_fusion.9), channel_id=1, source_target_pairs={{0,4},{1,5},{4,8},{5,9},{8,12},{9,13},{12,14},{13,15},{14,10},{15,... | collective-permute-start | bytes 393224 | tf_op jit(solution)/shard_map/ppermute | solution.py:164
  58.2 6.0 %collective-permute-start.31 = (bf16[128,512]{1,0:T(8,128)(2,1)S(1)}, bf16[128,512]{1,0:T(8,128)(2,1)S(1)}, u32[]{:S(2)}, u32[]{:S(2)}) collective-permute-start(bf16[128,512]{1,0:T(8,128)(2,1)S(1)} %add_convert_fusion.8.refs_1_), channel_id=1, source_target_pairs={{0,4},{1,5},{4,8},{5,9},{8,12},{9,13},{12,14},{13,15},{14,10},{15,... | collective-permute-start | bytes 393224 | tf_op jit(solution)/shard_map/ppermute | solution.py:164
  59.8 5.9 %collective-permute-start.34 = (bf16[128,512]{1,0:T(8,128)(2,1)S(1)}, bf16[128,512]{1,0:T(8,128)(2,1)S(1)}, u32[]{:S(2)}, u32[]{:S(2)}) collective-permute-start(bf16[128,512]{1,0:T(8,128)(2,1)S(1)} %add_convert_fusion.8.refs_1_), channel_id=1, source_target_pairs={{0,1},{1,0},{2,3},{3,2},{4,5},{5,4},{6,7},{7,6},{8,9},{9,8},{10,11... | collective-permute-start | bytes 393224 | tf_op jit(solution)/shard_map/ppermute | solution.py:164
  65.8 5.9 %collective-permute-start.36 = (bf16[128,512]{1,0:T(8,128)(2,1)S(1)}, bf16[128,512]{1,0:T(8,128)(2,1)S(1)}, u32[]{:S(2)}, u32[]{:S(2)}) collective-permute-start(bf16[128,512]{1,0:T(8,128)(2,1)S(1)} %collective-permute-done.33.refs_3_), channel_id=1, source_target_pairs={{4,0},{5,1},{8,4},{9,5},{12,8},{13,9},{14,12},{15,13},{10,14},{11,... | collective-permute-start | bytes 393224 | tf_op jit(solution)/shard_map/ppermute | solution.py:164
  71.7 7.9 %collective-permute-start.40 = (bf16[128,512]{1,0:T(8,128)(2,1)S(1)}, bf16[128,512]{1,0:T(8,128)(2,1)S(1)}, u32[]{:S(2)}, u32[]{:S(2)}) collective-permute-start(bf16[128,512]{1,0:T(8,128)(2,1)S(1)} %collective-permute-done.36.refs_4_), channel_id=1, source_target_pairs={{4,0},{5,1},{8,4},{9,5},{12,8},{13,9},{14,12},{15,13},{10,14},{11,... | collective-permute-start | bytes 393224 | tf_op jit(solution)/shard_map/ppermute | solution.py:164
  75.0 5.9 %collective-permute-start.39 = (bf16[128,512]{1,0:T(8,128)(2,1)S(1)}, bf16[128,512]{1,0:T(8,128)(2,1)S(1)}, u32[]{:S(2)}, u32[]{:S(2)}) collective-permute-start(bf16[128,512]{1,0:T(8,128)(2,1)S(1)} %collective-permute-done.35.refs_3_), channel_id=1, source_target_pairs={{0,4},{1,5},{4,8},{5,9},{8,12},{9,13},{12,14},{13,15},{14,10},{15,... | collective-permute-start | bytes 393224 | tf_op jit(solution)/shard_map/ppermute | solution.py:164
  100.5 7.0 %collective-permute-start.60 = (bf16[128,512]{1,0:T(8,128)(2,1)S(1)}, bf16[128,512]{1,0:T(8,128)(2,1)S(1)}, u32[]{:S(2)}, u32[]{:S(2)}) collective-permute-start(bf16[128,512]{1,0:T(8,128)(2,1)S(1)} %add_convert_fusion.2), channel_id=1, source_target_pairs={{4,0},{5,1},{8,4},{9,5},{12,8},{13,9},{14,12},{15,13},{10,14},{11,... | collective-permute-start | bytes 393224 | tf_op jit(solution)/shard_map/ppermute | solution.py:164
  (39 other events, 175.5 us)

commit v5 on v4

--- a/solution.py
+++ b/solution.py
@@ -245,14 +245,14 @@
         )
 
     def chunk_shapes(offsets):
-        outs = {("sib", o): jax.ShapeDtypeStruct((rows, cols), bf16) for o in offsets}
+        outs = {"sib": jax.ShapeDtypeStruct((len(offsets) * rows, cols), bf16)}
         outs.update({("own", o): jax.ShapeDtypeStruct((rows, cols), f32) for o in offsets})
         return outs
 
     def project(layer, offsets, hidden, block, out):
-        for o in offsets:
+        for e, o in enumerate(offsets):
             sib = jnp.dot(hidden, block(("d", layer, o, True)), preferred_element_type=f32)
-            out["sib", o][...] = sib.astype(bf16)
+            out["sib"][e * rows : (e + 1) * rows, :] = sib.astype(bf16)
             out["own", o][...] = jnp.dot(hidden, block(("d", layer, o, False)), preferred_element_type=f32)
 
     def down(layer, offsets, hidden, fetch):
@@ -294,7 +294,7 @@
         acc, crossed = fence(acc, crossed)
         found = finish(layer, crossed, acc, ahead(layer, "hidden"))
         hidden, found = fence(found.pop("hidden"), found)
-        c = send(found["sib", far], swap)
+        c = send(found["sib"], swap)
         own = found["own", far]
         found = down(layer, both(far - 1), hidden, ahead(layer, "scatter%d" % far))
         c, found = fence(c, found)
@@ -308,20 +308,20 @@
                     count = ahead(layer, "scatter0")
                     stage(chips, weights, blocks, lambda *given: None, [], {"hidden": hidden}, {}, {}, [], count, 0, "ahead")
                 break
-            c = [send(found["sib", o], swap) for o in both(step)]
+            c = send(found["sib"], swap)
             own = [found["own", o] for o in both(step)]
             found = down(layer, both(step - 1), hidden, ahead(layer, "scatter%d" % step))
             l, c, found = fence(l, c, found)
             if step == far - 1:
                 l = jnp.concatenate([jnp.zeros_like(l), l], 0)
-            l = fence((own[1] + c[1].astype(f32) + l.astype(f32)).astype(bf16))
+            l = fence((own[1] + c[rows:].astype(f32) + l.astype(f32)).astype(bf16))
             r, _ = fence(r, l)
             if step == far - 1:
                 r = jnp.concatenate([r, jnp.zeros_like(r)], 0)
-            r = (own[0] + c[0].astype(f32) + r.astype(f32)).astype(bf16)
+            r = (own[0] + c[:rows].astype(f32) + r.astype(f32)).astype(bf16)
             hidden, r = fence(hidden, r)
             if step == 1:
-                c = send(found["sib", 0], swap)
+                c = send(found["sib"], swap)
         r, l, c, _ = fence(r, l, c, dict(blocks))
         branch = found["own", 0] + c.astype(f32) + r.astype(f32) + l.astype(f32)
         stream = (stream.astype(f32) + branch).astype(bf16)

time: 108 us -> 108 us (level)
  starting transfers between devices: 40.2 us -> 37.9 us
  waiting for transfers between devices: 9.81 us -> 11.7 us
    ppermute x62 -> x56, starting transfers between devices: 40.2 us -> 37.9 us  [send(): return lax.ppermute(x, AXIS, perm)]
    ppermute x62 -> x56, waiting for transfers between devices: 9.81 us -> 11.7 us  [send(): return lax.ppermute(x, AXIS, perm)]
  transfers between devices with their start and end apart: 62 -> 56, of which waited for: 13 -> 17; matrix products, arithmetic and copies ran while one was open for 0% -> 0% of each run, Pallas kernels for 50% -> 51%
where the time goes in v5:
time: 108 us
  Pallas kernels  56.2 us (52%)
  starting transfers between devices  37.9 us (35%)
  waiting for transfers between devices  11.7 us (11%)
  other arithmetic  1.39 us (1%)
    pallas_call x23, Pallas kernels, stage(): pl.pallas_call(functools.partial(stage_kernel, chips, job, list(raw), str...  56.2 us
    ppermute x56, starting transfers between devices, send(): return lax.ppermute(x, AXIS, perm)  37.9 us
    ppermute x56, waiting for transfers between devices, send(): return lax.ppermute(x, AXIS, perm)  11.7 us
  transfers between devices with their start and end apart: 56, of which 17 were waited for; matrix products, arithmetic and copies ran while one was open for 0% of the time, Pallas kernels for 51%

profile of v5, /device:TPU:0, one launch (start us, length us, event | category | flops | bytes accessed | tf_op | source)
XLA Modules:
  0.0 107.7 jit_solution(2622093877228364994)
XLA Ops:
  0.0 3.0 %collective-permute-start = (bf16[128,512]{1,0:T(8,128)(2,1)}, bf16[128,512]{1,0:T(8,128)(2,1)S(1)}, u32[]{:S(2)}, u32[]{:S(2)}) collective-permute-start(bf16[128,512]{1,0:T(8,128)(2,1)} %bitcast.3), channel_id=1, source_target_pairs={{0,4},{1,5},{4,8},{5,9},{8,12},{9,13},{12,14},{13,15},{14,10},{15,... | collective-permute-start | bytes 393224 | tf_op jit(solution)/shard_map/ppermute | solution.py:164
  3.0 4.5 %gate_up.12 = (f32[128,896]{1,0:T(8,128)S(1)}, f32[128,896]{1,0:T(8,128)S(1)}, f32[128,128]{1,0:T(8,128)S(1)}, f32[2,8192]{1,0:T(2,128)S(1)}, bf16[128,512]{1,0:...) custom-call(bf16[2,8192,896]{2,1,0:T(8,128)(2,1)} %refs_14_.5, ...), custom_call_target="tpu_custom_call" | custom-call | flops 234881024 | bytes 9175040 | tf_op jit(solution)/shard_map/gate_up/pallas_call | solution.py:104
  7.5 2.1 %collective-permute-start.1 = (bf16[128,512]{1,0:T(8,128)(2,1)S(1)}, bf16[128,512]{1,0:T(8,128)(2,1)S(1)}, u32[]{:S(2)}, u32[]{:S(2)}) collective-permute-start(bf16[128,512]{1,0:T(8,128)(2,1)S(1)} %collective-permute-done.refs_2_), channel_id=1, source_target_pairs={{0,4},{1,5},{4,8},{5,9},{8,12},{9,13},{12,14},{13,15},{14,10},{15,... | collective-permute-start | bytes 393224 | tf_op jit(solution)/shard_map/ppermute | solution.py:164
  10.2 4.1 %gate_up.13 = (f32[128,896]{1,0:T(8,128)S(1)}, f32[128,896]{1,0:T(8,128)S(1)}, f32[128,128]{1,0:T(8,128)S(1)}, bf16[512,896]{1,0:T(8,128)(2,1)S(1)}, bf16[512,89...) custom-call(f32[2,8192]{1,0:T(2,128)S(1)} %get-tuple-element.275.ref, ...), custom_call_target="tpu_custom_call", output_to_operand_aliasing={{0}: (4, {}), {1}: (5, {}), {2}: (6, {})} | custom-call | flops 704643072 | bytes 7340032 | tf_op jit(solution)/shard_map/gate_up/pallas_call | solution.py:104
  14.3 1.7 %collective-permute-start.4 = (bf16[128,512]{1,0:T(8,128)(2,1)S(1)}, bf16[128,512]{1,0:T(8,128)(2,1)S(1)}, u32[]{:S(2)}, u32[]{:S(2)}) collective-permute-start(bf16[128,512]{1,0:T(8,128)(2,1)S(1)} %collective-permute-done.1.refs_3_), channel_id=1, source_target_pairs={{0,4},{1,5},{4,8},{5,9},{8,12},{9,13},{12,14},{13,15},{14,10},{15,... | collective-permute-start | bytes 393224 | tf_op jit(solution)/shard_map/ppermute | solution.py:164
  16.7 4.3 %gate_up.14 = (f32[128,896]{1,0:T(8,128)S(1)}, f32[128,896]{1,0:T(8,128)S(1)}, f32[128,128]{1,0:T(8,128)S(1)}, bf16[512,896]{1,0:T(8,128)(2,1)S(1)}, bf16[512,89...) custom-call(f32[2,8192]{1,0:T(2,128)S(1)} %get-tuple-element.275.ref, ...), custom_call_target="tpu_custom_call", output_to_operand_aliasing={{0}: (5, {}), {1}: (6, {}), {2}: (7, {})} | custom-call | flops 939524096 | bytes 7340032 | tf_op jit(solution)/shard_map/gate_up/pallas_call | solution.py:104
  21.5 1.7 %collective-permute-start.8 = (bf16[128,512]{1,0:T(8,128)(2,1)S(1)}, bf16[128,512]{1,0:T(8,128)(2,1)S(1)}, u32[]{:S(2)}, u32[]{:S(2)}) collective-permute-start(bf16[128,512]{1,0:T(8,128)(2,1)S(1)} %collective-permute-done.4.refs_3_), channel_id=1, source_target_pairs={{0,4},{1,5},{4,8},{5,9},{8,12},{9,13},{12,14},{13,15},{14,10},{15,... | collective-permute-start | bytes 393224 | tf_op jit(solution)/shard_map/ppermute | solution.py:164
  23.3 3.6 %gate_up.15 = (f32[128,896]{1,0:T(8,128)S(1)}, f32[128,896]{1,0:T(8,128)S(1)}, f32[128,128]{1,0:T(8,128)S(1)}, bf16[512,896]{1,0:T(8,128)(2,1)S(1)}, bf16[512,89...) custom-call(f32[2,8192]{1,0:T(2,128)S(1)} %get-tuple-element.275.ref, ...), custom_call_target="tpu_custom_call", output_to_operand_aliasing={{0}: (4, {}), {1}: (5, {}), {2}: (6, {})} | custom-call | flops 704643072 | bytes 5505024 | tf_op jit(solution)/shard_map/gate_up/pallas_call | solution.py:104
  28.4 3.3 %gate_up.17 = (f32[128,896]{1,0:T(8,128)S(1)}, f32[128,896]{1,0:T(8,128)S(1)}, f32[128,128]{1,0:T(8,128)S(1)}, bf16[896,512]{1,0:T(8,128)(2,1)S(1)}, bf16[896,51...) custom-call(f32[2,8192]{1,0:T(2,128)S(1)} %get-tuple-element.275.ref, ...), custom_call_target="tpu_custom_call", output_to_operand_aliasing={{0}: (3, {}), {1}: (4, {}), {2}: (5, {})} | custom-call | flops 469762048 | bytes 5505024 | tf_op jit(solution)/shard_map/gate_up/pallas_call | solution.py:104
  36.6 2.5 %down.9 = (bf16[256,512]{1,0:T(8,128)(2,1)S(1)}, f32[128,512]{1,0:T(8,128)S(1)}, f32[128,512]{1,0:T(8,128)S(1)}) custom-call(bf16[128,896]{1,0:T(8,128)(2,1)S(1)} %get-tuple-element.417.refs_0_, bf16[2,896,8192]{2,1,0:T(8,128)(2,1)} %refs_1_.13), custom_call_target="tpu_custom_call" | custom-call | flops 469762048 | bytes 3670016 | tf_op jit(solution)/shard_map/down/pallas_call | solution.py:104
  39.6 1.7 %collective-permute-start.23 = (bf16[128,512]{1,0:T(8,128)(2,1)S(1)}, bf16[128,512]{1,0:T(8,128)(2,1)S(1)}, u32[]{:S(2)}, u32[]{:S(2)}) collective-permute-start(bf16[128,512]{1,0:T(8,128)(2,1)S(1)} %add_convert_fusion.13), channel_id=1, source_target_pairs={{0,4},{1,5},{4,8},{5,9},{8,12},{9,13},{12,14},{13,15},{14,10},{15,... | collective-permute-start | bytes 393224 | tf_op jit(solution)/shard_map/ppermute | solution.py:164
  41.3 3.2 %down.10 = (bf16[256,512]{1,0:T(8,128)(2,1)S(1)}, f32[128,512]{1,0:T(8,128)S(1)}, f32[128,512]{1,0:T(8,128)S(1)}, bf16[896,512]{1,0:T(8,128)(2,1)S(1)}, bf16[896...) custom-call(bf16[128,896]{1,0:T(8,128)(2,1)S(1)} %get-tuple-element.417.refs_0_, ...), custom_call_target="tpu_custom_call" | custom-call | flops 469762048 | bytes 7340032 | tf_op jit(solution)/shard_map/down/pallas_call | solution.py:104
  45.6 1.7 %collective-permute-start.24 = (bf16[128,512]{1,0:T(8,128)(2,1)S(1)}, bf16[128,512]{1,0:T(8,128)(2,1)S(1)}, u32[]{:S(2)}, u32[]{:S(2)}) collective-permute-start(bf16[128,512]{1,0:T(8,128)(2,1)S(1)} %add_convert_fusion.11), channel_id=1, source_target_pairs={{0,4},{1,5},{4,8},{5,9},{8,12},{9,13},{12,14},{13,15},{14,10},{15,... | collective-permute-start | bytes 393224 | tf_op jit(solution)/shard_map/ppermute | solution.py:164
  47.3 3.5 %down.11 = (bf16[128,512]{1,0:T(8,128)(2,1)S(1)}, f32[128,512]{1,0:T(8,128)S(1)}, bf16[512,896]{1,0:T(8,128)(2,1)S(1)}, bf16[512,896]{1,0:T(8,128)(2,1)S(1)}, bf...) custom-call(bf16[128,896]{1,0:T(8,128)(2,1)S(1)} %get-tuple-element., ...), custom_call_target="tpu_custom_call" | custom-call | flops 234881024 | bytes 7340032 | tf_op jit(solution)/shard_map/down/pallas_call | solution.py:104
  51.6 1.7 %collective-permute-start.25 = (bf16[128,512]{1,0:T(8,128)(2,1)S(1)}, bf16[128,512]{1,0:T(8,128)(2,1)S(1)}, u32[]{:S(2)}, u32[]{:S(2)}) collective-permute-start(bf16[128,512]{1,0:T(8,128)(2,1)S(1)} %add_convert_fusion.9), channel_id=1, source_target_pairs={{0,4},{1,5},{4,8},{5,9},{8,12},{9,13},{12,14},{13,15},{14,10},{15,... | collective-permute-start | bytes 393224 | tf_op jit(solution)/shard_map/ppermute | solution.py:164
  53.3 4.2 %ahead.1 = (bf16[512,896]{1,0:T(8,128)(2,1)S(1)}, bf16[512,896]{1,0:T(8,128)(2,1)S(1)}, bf16[512,896]{1,0:T(8,128)(2,1)S(1)}, bf16[512,896]{1,0:T(8,128)(2,1)S(1...) custom-call(bf16[128,896]{1,0:T(8,128)(2,1)S(1)} %get-tuple-element., ...), custom_call_target="tpu_custom_call" | custom-call | bytes 11010048 | tf_op jit(solution)/shard_map/ahead/pallas_call | solution.py:104
  57.7 1.7 %collective-permute-start.28 = (bf16[128,512]{1,0:T(8,128)(2,1)S(1)}, bf16[128,512]{1,0:T(8,128)(2,1)S(1)}, u32[]{:S(2)}, u32[]{:S(2)}) collective-permute-start(bf16[128,512]{1,0:T(8,128)(2,1)S(1)} %add_convert_fusion.8.refs_1_), channel_id=1, source_target_pairs={{0,4},{1,5},{4,8},{5,9},{8,12},{9,13},{12,14},{13,15},{14,10},{15,... | collective-permute-start | bytes 393224 | tf_op jit(solution)/shard_map/ppermute | solution.py:164
  60.0 3.5 %gate_up.18 = (f32[128,896]{1,0:T(8,128)S(1)}, f32[128,896]{1,0:T(8,128)S(1)}, f32[128,128]{1,0:T(8,128)S(1)}, bf16[512,896]{1,0:T(8,128)(2,1)S(1)}, bf16[512,89...) custom-call(f32[2,8192]{1,0:T(2,128)S(1)} %get-tuple-element.275.ref, ...), custom_call_target="tpu_custom_call" | custom-call | flops 234881024 | bytes 7340032 | tf_op jit(solution)/shard_map/gate_up/pallas_call | solution.py:104
  66.0 2.7 %gate_up.19 = (f32[128,896]{1,0:T(8,128)S(1)}, f32[128,896]{1,0:T(8,128)S(1)}, f32[128,128]{1,0:T(8,128)S(1)}, bf16[512,896]{1,0:T(8,128)(2,1)S(1)}, bf16[512,89...) custom-call(f32[2,8192]{1,0:T(2,128)S(1)} %get-tuple-element.275.ref, ...), custom_call_target="tpu_custom_call", output_to_operand_aliasing={{0}: (4, {}), {1}: (5, {}), {2}: (6, {})} | custom-call | flops 704643072 | bytes 3670016 | tf_op jit(solution)/shard_map/gate_up/pallas_call | solution.py:104
  76.1 3.0 %gate_up.21 = (f32[128,896]{1,0:T(8,128)S(1)}, f32[128,896]{1,0:T(8,128)S(1)}, f32[128,128]{1,0:T(8,128)S(1)}, bf16[896,512]{1,0:T(8,128)(2,1)S(1)}, bf16[896,51...) custom-call(f32[2,8192]{1,0:T(2,128)S(1)} %get-tuple-element.275.ref, ...), custom_call_target="tpu_custom_call", output_to_operand_aliasing={{0}: (4, {}), {1}: (5, {}), {2}: (6, {})} | custom-call | flops 704643072 | bytes 3670016 | tf_op jit(solution)/shard_map/gate_up/pallas_call | solution.py:104
  86.6 2.5 %down.13 = (bf16[256,512]{1,0:T(8,128)(2,1)S(1)}, f32[128,512]{1,0:T(8,128)S(1)}, f32[128,512]{1,0:T(8,128)S(1)}) custom-call(bf16[128,896]{1,0:T(8,128)(2,1)S(1)} %get-tuple-element.530.refs_0_, bf16[2,896,8192]{2,1,0:T(8,128)(2,1)} %refs_1_.13), custom_call_target="tpu_custom_call" | custom-call | flops 469762048 | bytes 3670016 | tf_op jit(solution)/shard_map/down/pallas_call | solution.py:104
  91.3 2.5 %down.14 = (bf16[256,512]{1,0:T(8,128)(2,1)S(1)}, f32[128,512]{1,0:T(8,128)S(1)}, f32[128,512]{1,0:T(8,128)S(1)}) custom-call(bf16[128,896]{1,0:T(8,128)(2,1)S(1)} %get-tuple-element.530.refs_0_, bf16[2,896,8192]{2,1,0:T(8,128)(2,1)} %refs_1_.13), custom_call_target="tpu_custom_call" | custom-call | flops 469762048 | bytes 3670016 | tf_op jit(solution)/shard_map/down/pallas_call | solution.py:104
  97.3 1.8 %down.15 = (bf16[128,512]{1,0:T(8,128)(2,1)S(1)}, f32[128,512]{1,0:T(8,128)S(1)}) custom-call(bf16[128,896]{1,0:T(8,128)(2,1)S(1)} %get-tuple-element.530.refs_0_, bf16[2,896,8192]{2,1,0:T(8,128)(2,1)} %refs_1_.13), custom_call_target="tpu_custom_call" | custom-call | flops 234881024 | bytes 1835008 | tf_op jit(solution)/shard_map/down/pallas_call | solution.py:104
  103.3 3.7 %collective-permute-done.53 = bf16[128,512]{1,0:T(8,128)(2,1)S(1)} collective-permute-done((bf16[128,512]{1,0:T(8,128)(2,1)S(1)}, bf16[128,512]{1,0:T(8,128)(2,1)S(1)}, u32[]{:S(2)}, u32[]{:S(2)}) %collective-permute-start.53) | collective-permute-done | bytes 131104 | tf_op jit(solution)/shard_map/ppermute | solution.py:164
  (131 shorter events, 39.0 us)
Async XLA Ops:
  0.0 7.5 %collective-permute-start = (bf16[128,512]{1,0:T(8,128)(2,1)}, bf16[128,512]{1,0:T(8,128)(2,1)S(1)}, u32[]{:S(2)}, u32[]{:S(2)}) collective-permute-start(bf16[128,512]{1,0:T(8,128)(2,1)} %bitcast.3), channel_id=1, source_target_pairs={{0,4},{1,5},{4,8},{5,9},{8,12},{9,13},{12,14},{13,15},{14,10},{15,... | collective-permute-start | bytes 393224 | tf_op jit(solution)/shard_map/ppermute | solution.py:164
  3.0 6.6 %collective-permute-start.2 = (bf16[128,512]{1,0:T(8,128)(2,1)}, bf16[128,512]{1,0:T(8,128)(2,1)S(1)}, u32[]{:S(2)}, u32[]{:S(2)}) collective-permute-start(bf16[128,512]{1,0:T(8,128)(2,1)} %bitcast.4), channel_id=1, source_target_pairs={{4,0},{5,1},{8,4},{9,5},{12,8},{13,9},{14,12},{15,13},{10,14},{11,... | collective-permute-start | bytes 393224 | tf_op jit(solution)/shard_map/ppermute | solution.py:164
  3.0 6.6 %collective-permute-start.3 = (bf16[128,512]{1,0:T(8,128)(2,1)}, bf16[128,512]{1,0:T(8,128)(2,1)S(1)}, u32[]{:S(2)}, u32[]{:S(2)}) collective-permute-start(bf16[128,512]{1,0:T(8,128)(2,1)} %bitcast.5), channel_id=1, source_target_pairs={{0,1},{1,0},{2,3},{3,2},{4,5},{5,4},{6,7},{7,6},{8,9},{9,8},{10,11... | collective-permute-start | bytes 393224 | tf_op jit(solution)/shard_map/ppermute | solution.py:164
  7.5 6.8 %collective-permute-start.1 = (bf16[128,512]{1,0:T(8,128)(2,1)S(1)}, bf16[128,512]{1,0:T(8,128)(2,1)S(1)}, u32[]{:S(2)}, u32[]{:S(2)}) collective-permute-start(bf16[128,512]{1,0:T(8,128)(2,1)S(1)} %collective-permute-done.refs_2_), channel_id=1, source_target_pairs={{0,4},{1,5},{4,8},{5,9},{8,12},{9,13},{12,14},{13,15},{14,10},{15,... | collective-permute-start | bytes 393224 | tf_op jit(solution)/shard_map/ppermute | solution.py:164
  9.6 6.4 %collective-permute-start.7 = (bf16[128,512]{1,0:T(8,128)(2,1)S(1)}, bf16[128,512]{1,0:T(8,128)(2,1)S(1)}, u32[]{:S(2)}, u32[]{:S(2)}) collective-permute-start(bf16[128,512]{1,0:T(8,128)(2,1)S(1)} %collective-permute-done.2.refs_3_), channel_id=1, source_target_pairs={{0,1},{1,0},{2,3},{3,2},{4,5},{5,4},{6,7},{7,6},{8,9},{9,8},{10,11... | collective-permute-start | bytes 393224 | tf_op jit(solution)/shard_map/ppermute | solution.py:164
  9.8 6.2 %collective-permute-start.5 = (bf16[128,512]{1,0:T(8,128)(2,1)S(1)}, bf16[128,512]{1,0:T(8,128)(2,1)S(1)}, u32[]{:S(2)}, u32[]{:S(2)}) collective-permute-start(bf16[128,512]{1,0:T(8,128)(2,1)S(1)} %collective-permute-done.2.refs_3_), channel_id=1, source_target_pairs={{4,0},{5,1},{8,4},{9,5},{12,8},{13,9},{14,12},{15,13},{10,14},{11,... | collective-permute-start | bytes 393224 | tf_op jit(solution)/shard_map/ppermute | solution.py:164
  10.2 5.9 %collective-permute-start.6 = (bf16[128,512]{1,0:T(8,128)(2,1)S(1)}, bf16[128,512]{1,0:T(8,128)(2,1)S(1)}, u32[]{:S(2)}, u32[]{:S(2)}) collective-permute-start(bf16[128,512]{1,0:T(8,128)(2,1)S(1)} %collective-permute-done.refs_2_), channel_id=1, source_target_pairs={{0,1},{1,0},{2,3},{3,2},{4,5},{5,4},{6,7},{7,6},{8,9},{9,8},{10,11... | collective-permute-start | bytes 393224 | tf_op jit(solution)/shard_map/ppermute | solution.py:164
  14.3 6.7 %collective-permute-start.4 = (bf16[128,512]{1,0:T(8,128)(2,1)S(1)}, bf16[128,512]{1,0:T(8,128)(2,1)S(1)}, u32[]{:S(2)}, u32[]{:S(2)}) collective-permute-start(bf16[128,512]{1,0:T(8,128)(2,1)S(1)} %collective-permute-done.1.refs_3_), channel_id=1, source_target_pairs={{0,4},{1,5},{4,8},{5,9},{8,12},{9,13},{12,14},{13,15},{14,10},{15,... | collective-permute-start | bytes 393224 | tf_op jit(solution)/shard_map/ppermute | solution.py:164
  16.1 7.2 %collective-permute-start.11 = (bf16[128,512]{1,0:T(8,128)(2,1)S(1)}, bf16[128,512]{1,0:T(8,128)(2,1)S(1)}, u32[]{:S(2)}, u32[]{:S(2)}) collective-permute-start(bf16[128,512]{1,0:T(8,128)(2,1)S(1)} %collective-permute-done.5.refs_4_), channel_id=1, source_target_pairs={{0,1},{1,0},{2,3},{3,2},{4,5},{5,4},{6,7},{7,6},{8,9},{9,8},{10,11... | collective-permute-start | bytes 393224 | tf_op jit(solution)/shard_map/ppermute | solution.py:164
  16.4 10.5 %collective-permute-start.9 = (bf16[128,512]{1,0:T(8,128)(2,1)S(1)}, bf16[128,512]{1,0:T(8,128)(2,1)S(1)}, u32[]{:S(2)}, u32[]{:S(2)}) collective-permute-start(bf16[128,512]{1,0:T(8,128)(2,1)S(1)} %collective-permute-done.5.refs_4_), channel_id=1, source_target_pairs={{4,0},{5,1},{8,4},{9,5},{12,8},{13,9},{14,12},{15,13},{10,14},{11,... | collective-permute-start | bytes 393224 | tf_op jit(solution)/shard_map/ppermute | solution.py:164
  16.7 6.6 %collective-permute-start.10 = (bf16[128,512]{1,0:T(8,128)(2,1)S(1)}, bf16[128,512]{1,0:T(8,128)(2,1)S(1)}, u32[]{:S(2)}, u32[]{:S(2)}) collective-permute-start(bf16[128,512]{1,0:T(8,128)(2,1)S(1)} %collective-permute-done.1.refs_3_), channel_id=1, source_target_pairs={{0,1},{1,0},{2,3},{3,2},{4,5},{5,4},{6,7},{7,6},{8,9},{9,8},{10,11... | collective-permute-start | bytes 393224 | tf_op jit(solution)/shard_map/ppermute | solution.py:164
  21.5 6.2 %collective-permute-start.8 = (bf16[128,512]{1,0:T(8,128)(2,1)S(1)}, bf16[128,512]{1,0:T(8,128)(2,1)S(1)}, u32[]{:S(2)}, u32[]{:S(2)}) collective-permute-start(bf16[128,512]{1,0:T(8,128)(2,1)S(1)} %collective-permute-done.4.refs_3_), channel_id=1, source_target_pairs={{0,4},{1,5},{4,8},{5,9},{8,12},{9,13},{12,14},{13,15},{14,10},{15,... | collective-permute-start | bytes 393224 | tf_op jit(solution)/shard_map/ppermute | solution.py:164
  39.6 6.0 %collective-permute-start.23 = (bf16[128,512]{1,0:T(8,128)(2,1)S(1)}, bf16[128,512]{1,0:T(8,128)(2,1)S(1)}, u32[]{:S(2)}, u32[]{:S(2)}) collective-permute-start(bf16[128,512]{1,0:T(8,128)(2,1)S(1)} %add_convert_fusion.13), channel_id=1, source_target_pairs={{0,4},{1,5},{4,8},{5,9},{8,12},{9,13},{12,14},{13,15},{14,10},{15,... | collective-permute-start | bytes 393224 | tf_op jit(solution)/shard_map/ppermute | solution.py:164
  44.6 6.2 %collective-permute-start.21 = (bf16[128,512]{1,0:T(8,128)(2,1)S(1)}, bf16[128,512]{1,0:T(8,128)(2,1)S(1)}, u32[]{:S(2)}, u32[]{:S(2)}) collective-permute-start(bf16[128,512]{1,0:T(8,128)(2,1)S(1)} %add_convert_fusion.12), channel_id=1, source_target_pairs={{4,0},{5,1},{8,4},{9,5},{12,8},{13,9},{14,12},{15,13},{10,14},{11,... | collective-permute-start | bytes 393224 | tf_op jit(solution)/shard_map/ppermute | solution.py:164
  45.6 6.0 %collective-permute-start.24 = (bf16[128,512]{1,0:T(8,128)(2,1)S(1)}, bf16[128,512]{1,0:T(8,128)(2,1)S(1)}, u32[]{:S(2)}, u32[]{:S(2)}) collective-permute-start(bf16[128,512]{1,0:T(8,128)(2,1)S(1)} %add_convert_fusion.11), channel_id=1, source_target_pairs={{0,4},{1,5},{4,8},{5,9},{8,12},{9,13},{12,14},{13,15},{14,10},{15,... | collective-permute-start | bytes 393224 | tf_op jit(solution)/shard_map/ppermute | solution.py:164
  50.9 6.7 %collective-permute-start.26 = (bf16[128,512]{1,0:T(8,128)(2,1)S(1)}, bf16[128,512]{1,0:T(8,128)(2,1)S(1)}, u32[]{:S(2)}, u32[]{:S(2)}) collective-permute-start(bf16[128,512]{1,0:T(8,128)(2,1)S(1)} %add_convert_fusion.10), channel_id=1, source_target_pairs={{4,0},{5,1},{8,4},{9,5},{12,8},{13,9},{14,12},{15,13},{10,14},{11,... | collective-permute-start | bytes 393224 | tf_op jit(solution)/shard_map/ppermute | solution.py:164
  51.6 6.0 %collective-permute-start.25 = (bf16[128,512]{1,0:T(8,128)(2,1)S(1)}, bf16[128,512]{1,0:T(8,128)(2,1)S(1)}, u32[]{:S(2)}, u32[]{:S(2)}) collective-permute-start(bf16[128,512]{1,0:T(8,128)(2,1)S(1)} %add_convert_fusion.9), channel_id=1, source_target_pairs={{0,4},{1,5},{4,8},{5,9},{8,12},{9,13},{12,14},{13,15},{14,10},{15,... | collective-permute-start | bytes 393224 | tf_op jit(solution)/shard_map/ppermute | solution.py:164
  57.7 6.0 %collective-permute-start.28 = (bf16[128,512]{1,0:T(8,128)(2,1)S(1)}, bf16[128,512]{1,0:T(8,128)(2,1)S(1)}, u32[]{:S(2)}, u32[]{:S(2)}) collective-permute-start(bf16[128,512]{1,0:T(8,128)(2,1)S(1)} %add_convert_fusion.8.refs_1_), channel_id=1, source_target_pairs={{0,4},{1,5},{4,8},{5,9},{8,12},{9,13},{12,14},{13,15},{14,10},{15,... | collective-permute-start | bytes 393224 | tf_op jit(solution)/shard_map/ppermute | solution.py:164
  65.3 5.9 %collective-permute-start.33 = (bf16[128,512]{1,0:T(8,128)(2,1)S(1)}, bf16[128,512]{1,0:T(8,128)(2,1)S(1)}, u32[]{:S(2)}, u32[]{:S(2)}) collective-permute-start(bf16[128,512]{1,0:T(8,128)(2,1)S(1)} %collective-permute-done.30.refs_3_), channel_id=1, source_target_pairs={{4,0},{5,1},{8,4},{9,5},{12,8},{13,9},{14,12},{15,13},{10,14},{11,... | collective-permute-start | bytes 393224 | tf_op jit(solution)/shard_map/ppermute | solution.py:164
  71.2 7.9 %collective-permute-start.37 = (bf16[128,512]{1,0:T(8,128)(2,1)S(1)}, bf16[128,512]{1,0:T(8,128)(2,1)S(1)}, u32[]{:S(2)}, u32[]{:S(2)}) collective-permute-start(bf16[128,512]{1,0:T(8,128)(2,1)S(1)} %collective-permute-done.33.refs_4_), channel_id=1, source_target_pairs={{4,0},{5,1},{8,4},{9,5},{12,8},{13,9},{14,12},{15,13},{10,14},{11,... | collective-permute-start | bytes 393224 | tf_op jit(solution)/shard_map/ppermute | solution.py:164
  74.5 5.9 %collective-permute-start.36 = (bf16[128,512]{1,0:T(8,128)(2,1)S(1)}, bf16[128,512]{1,0:T(8,128)(2,1)S(1)}, u32[]{:S(2)}, u32[]{:S(2)}) collective-permute-start(bf16[128,512]{1,0:T(8,128)(2,1)S(1)} %collective-permute-done.32.refs_3_), channel_id=1, source_target_pairs={{0,4},{1,5},{4,8},{5,9},{8,12},{9,13},{12,14},{13,15},{14,10},{15,... | collective-permute-start | bytes 393224 | tf_op jit(solution)/shard_map/ppermute | solution.py:164
  89.8 6.0 %collective-permute-start.51 = (bf16[128,512]{1,0:T(8,128)(2,1)S(1)}, bf16[128,512]{1,0:T(8,128)(2,1)S(1)}, u32[]{:S(2)}, u32[]{:S(2)}) collective-permute-start(bf16[128,512]{1,0:T(8,128)(2,1)S(1)} %add_convert_fusion.5), channel_id=1, source_target_pairs={{0,4},{1,5},{4,8},{5,9},{8,12},{9,13},{12,14},{13,15},{14,10},{15,... | collective-permute-start | bytes 393224 | tf_op jit(solution)/shard_map/ppermute | solution.py:164
  95.8 6.0 %collective-permute-start.52 = (bf16[128,512]{1,0:T(8,128)(2,1)S(1)}, bf16[128,512]{1,0:T(8,128)(2,1)S(1)}, u32[]{:S(2)}, u32[]{:S(2)}) collective-permute-start(bf16[128,512]{1,0:T(8,128)(2,1)S(1)} %add_convert_fusion.3), channel_id=1, source_target_pairs={{0,4},{1,5},{4,8},{5,9},{8,12},{9,13},{12,14},{13,15},{14,10},{15,... | collective-permute-start | bytes 393224 | tf_op jit(solution)/shard_map/ppermute | solution.py:164
  99.6 7.4 %collective-permute-start.54 = (bf16[128,512]{1,0:T(8,128)(2,1)S(1)}, bf16[128,512]{1,0:T(8,128)(2,1)S(1)}, u32[]{:S(2)}, u32[]{:S(2)}) collective-permute-start(bf16[128,512]{1,0:T(8,128)(2,1)S(1)} %add_convert_fusion.2), channel_id=1, source_target_pairs={{4,0},{5,1},{8,4},{9,5},{12,8},{13,9},{14,12},{15,13},{10,14},{11,... | collective-permute-start | bytes 393224 | tf_op jit(solution)/shard_map/ppermute | solution.py:164
  (33 other events, 145.2 us)
